TPU v7x, 32 devices: a whole 2x2x4 slice. The times are simulated.
32 devices in a mesh: groups: 2 (over x), frame: 16 (over z, y, core).
Axes of the slice: x: 2, y: 2, z: 4, core: 2. Of those that a mesh axis runs over, the one named last changes fastest.
Arguments:
- latents: bfloat16 [128, 2, 64, 320], P(('groups', 'frame')), parts along dimension 0, may hold values from -6 to 6
- norm_gain: float32 [320], replicated, may hold values from 0.1 to 1.9
- w_qkv: bfloat16 [320, 960], replicated, may hold values from -0.3125 to 0.3125
- w_out: bfloat16 [320, 320], replicated, may hold values from -0.3125 to 0.3125
- gn_gain: float32 [2, 320], replicated, may hold values from 0.1 to 1.9
- conv_one: bfloat16 [3, 3, 320, 320], replicated, may hold values from -0.109375 to 0.109375
- conv_two: bfloat16 [3, 3, 320, 320], replicated, may hold values from -0.109375 to 0.109375
- step_embed: float32 [320], replicated, may hold values from -4 to 4
- offsets: int32 [32], P('groups'), parts along dimension 0, may hold values from 0 to 3
- numerators: int32 [16], replicated, may hold values from 1 to 16
Outputs:
- result: bfloat16 [128, 2, 64, 320], P(('groups', 'frame')), parts along dimension 0
There are 2 independent parts, one for each index of `groups`. A program takes and returns all parts, laid end to end along the dimension named above; an argument that names none is the same for every part. Nothing has to cross between parts.
All inputs are finite; a program needn't handle non-finite values.
Results may differ from a plain program's by a relative error of at most 0.009.
Values may be sent and summed in bfloat16 or wider, within the bound.
No kernel may reach another device: no remote copies, remote signals or barrier semaphores. Data moves between devices by JAX's collectives and lax.ppermute only.
A program may use at most 64 MiB of HBM per device.

v0:
```python
import jax
import jax.numpy as jnp
from jax import lax
from jax.sharding import PartitionSpec as P

HEADS = 5
HEAD_DIM = 64
NORM_GROUPS = 32
BLOCK = 4
WINDOW = 16


def shifted(shard, axis, by):
    count = lax.axis_size(axis)
    return lax.ppermute(shard, axis, [(i, (i + by) % count) for i in range(count)])


def layer_project(frames, norm_gain, w_qkv):
    channels = frames.shape[-1]
    values32 = frames.astype(jnp.float32)
    average = jnp.mean(values32, axis=-1, keepdims=True)
    centered = values32 - average
    variance = jnp.mean(centered * centered, axis=-1, keepdims=True)
    normed = (centered * lax.rsqrt(variance + 1e-05) * norm_gain).astype(jnp.bfloat16)
    qkv = jnp.dot(normed.reshape(-1, channels), w_qkv, preferred_element_type=jnp.float32).astype(
        jnp.bfloat16
    )
    return qkv.reshape(frames.shape[0], -1, 3 * channels)


def window_attend(window, numer_f):
    frame_count, pos_count, triple = window.shape
    channels = triple // 3
    queries = window[..., :channels].reshape(frame_count, pos_count, HEADS, HEAD_DIM)
    keys = window[..., channels : 2 * channels].reshape(frame_count, pos_count, HEADS, HEAD_DIM)
    values = window[..., 2 * channels :].reshape(frame_count, pos_count, HEADS, HEAD_DIM)
    scores = jnp.einsum(
        "jphd,kphd->phjk", queries, keys, preferred_element_type=jnp.float32
    ) / jnp.sqrt(jnp.float32(HEAD_DIM))
    highest = jnp.max(scores, axis=-1, keepdims=True)
    expos = jnp.exp(scores - highest)
    probs = (expos / jnp.sum(expos, axis=-1, keepdims=True)).astype(jnp.bfloat16)
    attended = jnp.einsum(
        "phjk,kphd->jphd", probs, values, preferred_element_type=jnp.float32
    ).reshape(frame_count, pos_count, channels)
    return (attended * numer_f[:, None, None]).astype(jnp.bfloat16)


def group_act(tensor, gain):
    shape = tensor.shape
    grouped = tensor.reshape(shape[0], shape[1], shape[2], NORM_GROUPS, shape[3] // NORM_GROUPS)
    average = jnp.mean(grouped, axis=(1, 2, 4), keepdims=True)
    centered = grouped - average
    variance = jnp.mean(centered * centered, axis=(1, 2, 4), keepdims=True)
    normed = (centered * lax.rsqrt(variance + 1e-05)).reshape(shape) * gain
    return jax.nn.silu(normed).astype(jnp.bfloat16)


def conv_three(tensor, kernel):
    return lax.conv_general_dilated(
        tensor,
        kernel,
        (1, 1),
        "SAME",
        dimension_numbers=("NHWC", "HWIO", "NHWC"),
        preferred_element_type=jnp.float32,
    )


def body(
    latents, norm_gain, w_qkv, w_out, gn_gain, conv_one, conv_two, step_embed, offsets, numerators
):
    block_len, tile_rows, tile_cols, channels = latents.shape
    reach = WINDOW // BLOCK
    nblocks = offsets.shape[0]
    position = lax.axis_index("frame")
    numer_f = numerators.astype(jnp.float32)
    pieces = [latents]
    for distance in range(1, reach + 1):
        pieces.append(shifted(latents, "frame", -distance))
    span = jnp.concatenate(pieces, 0)
    span = layer_project(span, norm_gain, w_qkv)
    block_ids = jnp.arange(nblocks, dtype=jnp.int32)
    start_shift = jnp.sum(jnp.where(block_ids == position, offsets, 0))
    window = lax.dynamic_slice_in_dim(span, start_shift, WINDOW, 0)
    weighted = window_attend(window, numer_f)
    pos_count = weighted.shape[1]
    slots = jnp.zeros(((reach + 1) * block_len, pos_count, channels), jnp.bfloat16)
    slots = lax.dynamic_update_slice_in_dim(slots, weighted, start_shift, 0)
    totals = slots[:block_len].astype(jnp.float32)
    for distance in range(1, reach + 1):
        piece = slots[distance * block_len : (distance + 1) * block_len]
        totals = totals + shifted(piece, "frame", distance).astype(jnp.float32)
    back_steps = jnp.arange(reach + 1, dtype=jnp.int32)
    owners = (position - back_steps) % nblocks
    shifts_back = jnp.sum(
        jnp.where(block_ids[None, :] == owners[:, None], offsets[None, :], 0), axis=1
    )
    slot_pos = (
        block_len * back_steps[:, None]
        + jnp.arange(block_len, dtype=jnp.int32)[None, :]
        - shifts_back[:, None]
    )
    matches = slot_pos[:, :, None] == jnp.arange(WINDOW, dtype=jnp.int32)[None, None, :]
    denominator = jnp.sum(jnp.where(matches, numer_f[None, None, :], 0.0), axis=(0, 2))
    combined = (totals / denominator[:, None, None]).astype(jnp.bfloat16)
    projected = jnp.dot(
        combined.reshape(-1, channels), w_out, preferred_element_type=jnp.float32
    ).reshape(latents.shape)
    hidden = (latents.astype(jnp.float32) + projected).astype(jnp.bfloat16)
    first_act = group_act(hidden.astype(jnp.float32), gn_gain[0])
    middle = conv_three(first_act, conv_one) + step_embed
    second_act = group_act(middle, gn_gain[1])
    return (hidden.astype(jnp.float32) + conv_three(second_act, conv_two)).astype(jnp.bfloat16)


def solution(mesh):
    return jax.shard_map(
        body,
        mesh=mesh,
        in_specs=(
            P(("groups", "frame"), None, None, None),
            P(),
            P(),
            P(),
            P(),
            P(),
            P(),
            P(),
            P("groups"),
            P(),
        ),
        out_specs=P(("groups", "frame"), None, None, None),
        check_vma=False,
    )
```

profile of v0, /device:TPU:5, one launch (start us, length us, event | category | flops | bytes accessed | tf_op | source)
XLA Modules:
  0.0 157.0 jit_solution(2478372511884069237)
XLA Ops:
  0.7 4.7 %collective-permute-start.2 = (bf16[4,2,64,320]{3,2,1,0:T(8,128)(2,1)}, bf16[4,2,64,320]{3,2,1,0:T(8,128)(2,1)S(1)}, u32[]{:S(2)}, u32[]{:S(2)}) collective-permute-start(bf16[4,2,64,320]{3,2,1,0:T(8,128)(2,1)} %param.10), channel_id=1, source_target_pairs={{0,13},{1,14},{2,15},{3,0},{4,1},{5,2},{6,3},{7,4},{8,5},{9,6},{10... | collective-permute-start | bytes 983048 | tf_op jit(solution)/shard_map/ppermute | solution.py:15
  15.1 3.1 %collective-permute-done.2 = bf16[4,2,64,320]{3,2,1,0:T(8,128)(2,1)S(1)} collective-permute-done((bf16[4,2,64,320]{3,2,1,0:T(8,128)(2,1)}, bf16[4,2,64,320]{3,2,1,0:T(8,128)(2,1)S(1)}, u32[]{:S(2)}, u32[]{:S(2)}) %collective-permute-start.2) | collective-permute-done | bytes 327712 | tf_op jit(solution)/shard_map/ppermute | solution.py:15
  19.8 2.1 %convert_reduce_fusion = f32[20,2,64]{2,1,0:T(2,128)S(1)} fusion(bf16[20,2,64,320]{3,2,1,0:T(8,128)(2,1)} %constant_dynamic-update-slice_fusion), kind=kLoop, calls=%fused_computation.17 | loop fusion | flops 1635840 | bytes 1648640 | tf_op jit(solution)/shard_map/reduce_sum | solution.py:21
  23.3 2.8 %fusion.4 = bf16[2560,320]{1,0:T(8,128)(2,1)S(1)} fusion(bf16[20,2,64,320]{3,2,1,0:T(8,128)(2,1)} %constant_dynamic-update-slice_fusion, f32[320]{0:T(512)S(1)} %copy-done.10, f32[2560]{0:T(1024)S(1)} %rsqrt.28, f32[2560]{0:T(1024)S(1)} %div.50), kind=kLoop, calls=%fused_computation.9 | loop fusion | flops 4096000 | bytes 3298560 | tf_op jit(solution)/shard_map/convert_element_type | solution.py:24
  26.1 4.5 %convolution_convert_fusion = bf16[2560,960]{0,1:T(8,128)(2,1)} fusion(bf16[2560,320]{1,0:T(8,128)(2,1)S(1)} %fusion.4, bf16[320,960]{1,0:T(8,128)(2,1)S(1)} %copy-done.12), kind=kOutput, calls=%fused_computation.1 | convolution fusion | flops 1575321600 | bytes 7168000 | tf_op jit(solution)/shard_map/dot_general | solution.py:25
  30.6 7.9 %copy.36 = bf16[2560,960]{1,0:T(8,128)(2,1)} copy(bf16[2560,960]{0,1:T(8,128)(2,1)} %convolution_convert_fusion) | data formatting | bytes 9830400 | tf_op jit(solution)/shard_map/convert_element_type | solution.py:25
  38.5 5.7 %constant_dynamic-slice_fusion.2 = (bf16[16,128,320]{2,1,0:T(8,128)(2,1)}, bf16[16,128,320]{2,1,0:T(8,128)(2,1)}, bf16[16,128,320]{2,1,0:T(8,128)(2,1)}) fusion(bf16[20,128,960]{2,1,0:T(8,128)(2,1)} %bitcast.58, s32[]{:T(128)S(6)} %select_n.28, s32[]{:T(128)S(6)} %add.114, s32[]{:T(128)S(6)} %add.113), kind=kLoop, calls=%fused_computation.84 | loop fusion | bytes 7864332 | tf_op jit(solution)/shard_map/slice | solution.py:35
  44.2 1.9 %copy.38 = bf16[16,128,320]{1,2,0:T(8,128)(2,1)S(1)} copy(bf16[16,128,320]{2,1,0:T(8,128)(2,1)} %get-tuple-element.8) | data formatting | bytes 2621440 | tf_op jit(solution)/shard_map/slice | solution.py:34
  46.0 5.1 %copy.40 = bf16[16,128,5,64]{3,0,2,1:T(8,128)(2,1)} copy(bf16[16,128,5,64]{1,3,2,0:T(8,128)(2,1)S(1)} %bitcast.61) | data formatting | bytes 2621440 | tf_op jit(solution)/shard_map/reshape | solution.py:34
  53.0 5.1 %copy.41 = bf16[16,128,5,64]{3,0,2,1:T(8,128)(2,1)} copy(bf16[16,128,5,64]{1,3,2,0:T(8,128)(2,1)S(1)} %bitcast.62) | data formatting | bytes 2621440 | tf_op jit(solution)/shard_map/reshape | solution.py:35
  60.0 5.1 %copy.42 = bf16[16,128,5,64]{3,0,2,1:T(8,128)(2,1)} copy(bf16[16,128,5,64]{1,3,2,0:T(8,128)(2,1)S(1)} %bitcast.63) | data formatting | bytes 2621440 | tf_op jit(solution)/shard_map/reshape | solution.py:36
  65.2 7.4 %fusion.48 = (f32[128,5,16]{2,1,0:T(8,128)S(1)}, f32[128,5,16,16]{2,3,1,0:T(8,128)}) fusion(bf16[16,128,5,64]{3,0,2,1:T(8,128)(2,1)} %copy.40, bf16[16,128,5,64]{3,0,2,1:T(8,128)(2,1)} %copy.41), kind=kOutput, calls=%fused_computation.95 | convolution fusion | flops 21463056 | bytes 3317760 | tf_op jit(solution)/shard_map/sub | solution.py:41
  72.6 6.7 %fusion.11 = f32[16,128,5,64]{3,0,2,1:T(8,128)} fusion(bf16[16,128,5,64]{3,0,2,1:T(8,128)(2,1)} %copy.42, f32[128,5,16,16]{2,3,1,0:T(8,128)} %get-tuple-element.18, f32[128,5,16]{2,1,0:T(8,128)S(1)} %get-tuple-element.17), kind=kOutput, calls=%fused_computation.16 | convolution fusion | flops 21299200 | bytes 4628480 | tf_op jit(solution)/shard_map/phjk,kphd->jphd/dot_general | solution.py:43
  79.2 6.2 %copy.44 = f32[16,128,5,64]{1,3,2,0:T(8,128)} copy(f32[16,128,5,64]{3,0,2,1:T(8,128)} %fusion.11) | data formatting | bytes 5242880 | tf_op jit(solution)/shard_map/phjk,kphd->jphd/transpose | solution.py:43
  85.4 2.1 %fusion.8 = bf16[16,128,320]{1,2,0:T(8,128)(2,1)S(1)} fusion(f32[16,128,5,64]{1,3,2,0:T(8,128)} %copy.44, f32[16]{0:T(128)S(1)} %convert_element_type.69), kind=kLoop, calls=%fused_computation.13 | loop fusion | flops 1310720 | bytes 3932224 | tf_op jit(solution)/shard_map/convert_element_type | solution.py:46
  91.9 1.9 %copy.62 = bf16[4,128,320]{1,2,0:T(8,128)(2,1)} copy(bf16[4,128,320]{2,1,0:T(8,128)(2,1)} %get-tuple-element.12) | data formatting | bytes 655360
  93.8 16.5 %collective-permute-start.4 = (bf16[4,128,320]{1,2,0:T(8,128)(2,1)}, bf16[4,128,320]{1,2,0:T(8,128)(2,1)}, u32[]{:S(2)}, u32[]{:S(2)}) collective-permute-start(bf16[4,128,320]{1,2,0:T(8,128)(2,1)} %copy.62), channel_id=1, source_target_pairs={{0,1},{1,2},{2,3},{3,4},{4,5},{5,6},{6,7},{7,8},{8,9},{9,10},{10,1... | collective-permute-start | bytes 983048 | tf_op jit(solution)/shard_map/ppermute | solution.py:15
  113.9 3.1 %collective-permute-start.7 = (bf16[4,128,320]{2,1,0:T(8,128)(2,1)}, bf16[4,128,320]{2,1,0:T(8,128)(2,1)}, u32[]{:S(2)}, u32[]{:S(2)}) collective-permute-start(bf16[4,128,320]{2,1,0:T(8,128)(2,1)} %get-tuple-element.10), channel_id=1, source_target_pairs={{0,4},{1,5},{2,6},{3,7},{4,8},{5,9},{6,10},{7,11},{8,12},{9,13},{1... | collective-permute-start | bytes 983048 | tf_op jit(solution)/shard_map/ppermute | solution.py:15
  117.3 6.3 %collective-permute-done.5 = bf16[4,128,320]{1,2,0:T(8,128)(2,1)} collective-permute-done((bf16[4,128,320]{1,2,0:T(8,128)(2,1)}, bf16[4,128,320]{1,2,0:T(8,128)(2,1)}, u32[]{:S(2)}, u32[]{:S(2)}) %collective-permute-start.5) | collective-permute-done | bytes 327712 | tf_op jit(solution)/shard_map/ppermute | solution.py:15
  123.6 7.0 %collective-permute-done.6 = bf16[4,128,320]{1,2,0:T(8,128)(2,1)} collective-permute-done((bf16[4,128,320]{1,2,0:T(8,128)(2,1)}, bf16[4,128,320]{1,2,0:T(8,128)(2,1)}, u32[]{:S(2)}, u32[]{:S(2)}) %collective-permute-start.6) | collective-permute-done | bytes 327712 | tf_op jit(solution)/shard_map/ppermute | solution.py:15
  130.6 2.2 %convert_add_fusion = f32[4,128,320]{1,2,0:T(8,128)} fusion(bf16[4,128,320]{1,2,0:T(8,128)(2,1)} %collective-permute-done.6, bf16[4,128,320]{1,2,0:T(8,128)(2,1)} %collective-permute-done.5, bf16[4,128,320]{1,2,0:T(8,128)(2,1)} %collective-permute-done.4, bf16[4,128,320]{1,2,0:T(8,128)(2,1)S(1)} %copy.61), kind=kLoop, calls=%fused_computation.41 | loop fusion | flops 1146880 | bytes 1966080 | tf_op jit(solution)/shard_map/add | solution.py:93
  134.2 6.6 %collective-permute-done.7 = bf16[4,128,320]{2,1,0:T(8,128)(2,1)} collective-permute-done((bf16[4,128,320]{2,1,0:T(8,128)(2,1)}, bf16[4,128,320]{2,1,0:T(8,128)(2,1)}, u32[]{:S(2)}, u32[]{:S(2)}) %collective-permute-start.7) | collective-permute-done | bytes 327712 | tf_op jit(solution)/shard_map/ppermute | solution.py:15
  145.3 1.9 %fusion.12 = f32[2,32,9,320]{3,1,2,0:T(8,128)S(1)} fusion(bf16[3,3,320,320]{3,2,1,0:T(8,128)(2,1)S(1)} %copy-done, bf16[2,4,8,11,320]{4,1,3,2,0:T(4,128)(2,1)S(1)} %fusion.27, f32[320]{0:T(512)S(1)} %copy-done.7, pred[32,9]{0,1:T(8,128)(4,1)S(1)} %copy-done.8), kind=kOutput, calls=%fused_computation.19 | convolution fusion | flops 708157440 | bytes 3032608 | tf_op jit(solution)/shard_map/conv_general_dilated | solution.py:60
  153.1 1.9 %fusion.23 = f32[2,32,9,320]{3,1,2,0:T(8,128)S(1)} fusion(bf16[3,3,320,320]{3,2,1,0:T(8,128)(2,1)S(1)} %copy-done.11, bf16[2,4,7,1,320]{4,2,1,3,0:T(8,128)(2,1)S(1)} %get-tuple-element.16, bf16[2,4,7,1,320]{4,2,1,3,0:T(8,128)(2,1)S(1)} %get-tuple-element.15, bf16[2,4,8,9,320]{4,2,1,3,0:T(8,128)(2,1)S(1)} %select_bitcast_fusion), kind=kOutput, calls=%fused_computation.44 | convolution fusion | flops 710041600 | bytes 3020800 | tf_op jit(solution)/shard_map/conv_general_dilated | solution.py:60
  (103 shorter events, 36.8 us)
Async XLA Ops:
  0.0 145.3 %copy-start = (bf16[3,3,320,320]{3,2,1,0:T(8,128)(2,1)S(1)}, bf16[3,3,320,320]{3,2,1,0:T(8,128)(2,1)}, u32[]{:S(2)}) copy-start(bf16[3,3,320,320]{3,2,1,0:T(8,128)(2,1)} %param.15) | copy-start | bytes 5529604
  0.0 12.5 %collective-permute-start = (bf16[4,2,64,320]{3,2,1,0:T(8,128)(2,1)}, bf16[4,2,64,320]{3,2,1,0:T(8,128)(2,1)}, u32[]{:S(2)}, u32[]{:S(2)}) collective-permute-start(bf16[4,2,64,320]{3,2,1,0:T(8,128)(2,1)} %param.10), channel_id=1, source_target_pairs={{0,15},{1,0},{2,1},{3,2},{4,3},{5,4},{6,5},{7,6},{8,7},{9,8},{10,9... | collective-permute-start | bytes 983048 | tf_op jit(solution)/shard_map/ppermute | solution.py:15
  0.7 13.6 %collective-permute-start.1 = (bf16[4,2,64,320]{3,2,1,0:T(8,128)(2,1)}, bf16[4,2,64,320]{3,2,1,0:T(8,128)(2,1)S(1)}, u32[]{:S(2)}, u32[]{:S(2)}) collective-permute-start(bf16[4,2,64,320]{3,2,1,0:T(8,128)(2,1)} %param.10), channel_id=1, source_target_pairs={{0,14},{1,15},{2,0},{3,1},{4,2},{5,3},{6,4},{7,5},{8,6},{9,7},{10,... | collective-permute-start | bytes 983048 | tf_op jit(solution)/shard_map/ppermute | solution.py:15
  0.7 17.5 %collective-permute-start.2 = (bf16[4,2,64,320]{3,2,1,0:T(8,128)(2,1)}, bf16[4,2,64,320]{3,2,1,0:T(8,128)(2,1)S(1)}, u32[]{:S(2)}, u32[]{:S(2)}) collective-permute-start(bf16[4,2,64,320]{3,2,1,0:T(8,128)(2,1)} %param.10), channel_id=1, source_target_pairs={{0,13},{1,14},{2,15},{3,0},{4,1},{5,2},{6,3},{7,4},{8,5},{9,6},{10... | collective-permute-start | bytes 983048 | tf_op jit(solution)/shard_map/ppermute | solution.py:15
  5.4 13.6 %collective-permute-start.3 = (bf16[4,2,64,320]{3,2,1,0:T(8,128)(2,1)}, bf16[4,2,64,320]{3,2,1,0:T(8,128)(2,1)S(1)}, u32[]{:S(2)}, u32[]{:S(2)}) collective-permute-start(bf16[4,2,64,320]{3,2,1,0:T(8,128)(2,1)} %param.10), channel_id=1, source_target_pairs={{0,12},{1,13},{2,14},{3,15},{4,0},{5,1},{6,2},{7,3},{8,4},{9,5},{1... | collective-permute-start | bytes 983048 | tf_op jit(solution)/shard_map/ppermute | solution.py:15
  19.8 2.1 %copy-start.1 = (bf16[20,2,64,320]{3,2,1,0:T(8,128)(2,1)S(1)}, bf16[20,2,64,320]{3,2,1,0:T(8,128)(2,1)}, u32[]{:S(2)}) copy-start(bf16[20,2,64,320]{3,2,1,0:T(8,128)(2,1)} %constant_dynamic-update-slice_fusion) | copy-start | bytes 4915204
  19.8 3.5 %copy-start.10 = (f32[320]{0:T(512)S(1)}, f32[320]{0:T(512)}, u32[]{:S(2)}) copy-start(f32[320]{0:T(512)} %param.11) | copy-start | bytes 3844
  23.1 3.0 %copy-start.12 = (bf16[320,960]{1,0:T(8,128)(2,1)S(1)}, bf16[320,960]{1,0:T(8,128)(2,1)}, u32[]{:S(2)}) copy-start(bf16[320,960]{1,0:T(8,128)(2,1)} %param.12) | copy-start | bytes 1843204
  89.1 1.4 copy-start.5
  90.8 26.3 %copy-start.9 = (f32[2,320]{1,0:T(2,128)S(1)}, f32[2,320]{1,0:T(2,128)}, u32[]{:S(2)}) copy-start(f32[2,320]{1,0:T(2,128)} %param.14) | copy-start | bytes 7684
  93.8 23.5 %collective-permute-start.4 = (bf16[4,128,320]{1,2,0:T(8,128)(2,1)}, bf16[4,128,320]{1,2,0:T(8,128)(2,1)}, u32[]{:S(2)}, u32[]{:S(2)}) collective-permute-start(bf16[4,128,320]{1,2,0:T(8,128)(2,1)} %copy.62), channel_id=1, source_target_pairs={{0,1},{1,2},{2,3},{3,4},{4,5},{5,6},{6,7},{7,8},{8,9},{9,10},{10,1... | collective-permute-start | bytes 983048 | tf_op jit(solution)/shard_map/ppermute | solution.py:15
  111.2 12.4 %collective-permute-start.5 = (bf16[4,128,320]{1,2,0:T(8,128)(2,1)}, bf16[4,128,320]{1,2,0:T(8,128)(2,1)}, u32[]{:S(2)}, u32[]{:S(2)}) collective-permute-start(bf16[4,128,320]{1,2,0:T(8,128)(2,1)} %copy.63), channel_id=1, source_target_pairs={{0,2},{1,3},{2,4},{3,5},{4,6},{5,7},{6,8},{7,9},{8,10},{9,11},{10,... | collective-permute-start | bytes 983048 | tf_op jit(solution)/shard_map/ppermute | solution.py:15
  112.1 18.6 %collective-permute-start.6 = (bf16[4,128,320]{1,2,0:T(8,128)(2,1)}, bf16[4,128,320]{1,2,0:T(8,128)(2,1)}, u32[]{:S(2)}, u32[]{:S(2)}) collective-permute-start(bf16[4,128,320]{1,2,0:T(8,128)(2,1)} %copy.64), channel_id=1, source_target_pairs={{0,3},{1,4},{2,5},{3,6},{4,7},{5,8},{6,9},{7,10},{8,11},{9,12},{10... | collective-permute-start | bytes 983048 | tf_op jit(solution)/shard_map/ppermute | solution.py:15
  113.9 26.8 %collective-permute-start.7 = (bf16[4,128,320]{2,1,0:T(8,128)(2,1)}, bf16[4,128,320]{2,1,0:T(8,128)(2,1)}, u32[]{:S(2)}, u32[]{:S(2)}) collective-permute-start(bf16[4,128,320]{2,1,0:T(8,128)(2,1)} %get-tuple-element.10), channel_id=1, source_target_pairs={{0,4},{1,5},{2,6},{3,7},{4,8},{5,9},{6,10},{7,11},{8,12},{9,13},{1... | collective-permute-start | bytes 983048 | tf_op jit(solution)/shard_map/ppermute | solution.py:15
  117.3 24.5 %copy-start.6 = (bf16[4,2,64,320]{3,2,1,0:T(8,128)(2,1)S(1)}, bf16[4,2,64,320]{3,2,1,0:T(8,128)(2,1)}, u32[]{:S(2)}) copy-start(bf16[4,2,64,320]{3,2,1,0:T(8,128)(2,1)} %param.10) | copy-start | bytes 983044
  143.2 1.8 %copy-start.2 = (f32[4,2,64,320]{3,2,1,0:T(8,128)}, f32[4,2,64,320]{3,2,1,0:T(8,128)S(1)}, u32[]{:S(2)}) copy-start(f32[4,2,64,320]{3,2,1,0:T(8,128)S(1)} %get-tuple-element.20) | copy-start | bytes 1966084
  143.8 1.5 copy-start.7
  143.8 1.5 copy-start.8
  148.8 0.9 copy-start.4
  151.2 1.9 %copy-start.11 = (bf16[3,3,320,320]{3,2,1,0:T(8,128)(2,1)S(1)}, bf16[3,3,320,320]{3,2,1,0:T(8,128)(2,1)}, u32[]{:S(2)}) copy-start(bf16[3,3,320,320]{3,2,1,0:T(8,128)(2,1)} %param.16) | copy-start | bytes 5529604
  155.0 1.1 copy-start.3
where the time goes:
time: 158 us; the launch traced here: 157 us
  local copies, waits for them, and re-layouts  62.2 us (39%)
  starting transfers between devices  26.8 us (17%)
  matrix products  23.8 us (15%)
  waiting for transfers between devices  23.4 us (15%)
  other arithmetic  18.4 us (12%)
  between operations  2.43 us (2%)
    ppermute x8, starting transfers between devices, shifted(): lax.ppermute(shard, axis, [(i, (i + by) % count) for i in range(count)])  26.8 us
    ppermute x8, waiting for transfers between devices, shifted(): lax.ppermute(shard, axis, [(i, (i + by) % count) for i in range(count)])  23.4 us
    unnamed x35, local copies, waits for them, and re-layouts  11.7 us
    convert_element_type x1, local copies, waits for them, and re-layouts, layer_project(): jnp.dot(normed.reshape(-1, channels), w_qkv, preferred_element_type=jnp.f...  7.87 us
    slice x2, local copies, waits for them, and re-layouts, window_attend(): window[..., channels:2 * channels]  7.52 us
    sub x1, matrix products, window_attend(): expos = jnp.exp(scores - highest)  7.4 us
    dot_general x1, matrix products, window_attend(): jnp.einsum('phjk,kphd->jphd', probs, values, preferred_element_type=jnp.f...  6.67 us
    transpose x1, local copies, waits for them, and re-layouts, window_attend(): jnp.einsum('phjk,kphd->jphd', probs, values, preferred_element_type=jnp.f...  6.18 us
  transfers between devices with their start and end apart: 8, of which 5 were waited for; matrix products, arithmetic and copies ran while one was open for 9% of the time, Pallas kernels for 0%

commit v1 on v0

v1 whole, which is shorter than its diff:
```python
import functools

import jax
import jax.numpy as jnp
from jax import lax
from jax.experimental import pallas as pl
from jax.experimental.pallas import tpu as pltpu
from jax.sharding import PartitionSpec as P

HEADS = 5
NORM_GROUPS = 32
BLOCK = 4
WINDOW = 16
REACH = WINDOW // BLOCK
EPS = 1e-05
LANES = 128
LOG2E = 1.4426950408889634
NT = (((1,), (1,)), ((), ()))
TN = (((0,), (0,)), ((), ()))


def attend_kernel(
    frames, cells, off_ref, num_ref, x_ref, gain_ref, w_ref, out_ref, qkv_ref, bias_ref, coef_ref, acc_ref
):
    channels = x_ref.shape[-1]
    head_dim = channels // HEADS
    blocks = frames // BLOCK
    wide = HEADS * frames

    x = x_ref[...].astype(jnp.float32)
    cen = x - jnp.mean(x, axis=-1, keepdims=True)
    var = jnp.mean(cen * cen, axis=-1, keepdims=True)
    normed = (cen * lax.rsqrt(var + EPS) * gain_ref[...]).astype(jnp.bfloat16)
    lanes = qkv_ref.shape[-1]
    chunks = acc_ref.shape[0]
    pad = jnp.zeros((x.shape[0], chunks * lanes - channels), jnp.float32)
    for i in range(3):
        part = jnp.dot(
            normed, w_ref[:, i * channels : (i + 1) * channels], preferred_element_type=jnp.float32
        )
        part = jnp.concatenate([part, pad], 1)
        for j in range(chunks):
            qkv_ref[i * chunks + j] = part[:, j * lanes : (j + 1) * lanes]

    frame = lax.broadcasted_iota(jnp.int32, (1, wide), 1) % frames
    block, rest = frame // BLOCK, frame % BLOCK
    key = lax.broadcasted_iota(jnp.int32, (frames, wide), 0)
    weights = []
    for back in range(REACH + 1):
        owner = (block - back + blocks) % blocks
        shift = jnp.zeros((1, wide), jnp.int32)
        for w in range(blocks):
            shift = jnp.where(owner == w, off_ref[w], shift)
        place = BLOCK * back + rest - shift
        weight = jnp.zeros((1, wide), jnp.int32)
        for j in range(WINDOW):
            weight = jnp.where(place == j, num_ref[j], weight)
        weights.append(weight.astype(jnp.float32))
        rel = key - (BLOCK * owner + shift)
        rel = jnp.where(rel < 0, rel + frames, rel)
        bias_ref[back] = jnp.where(rel < WINDOW, 0.0, -1e30)
    total = sum(weights)
    for back in range(REACH + 1):
        coef_ref[back] = weights[back] / total

    lane_head = lax.broadcasted_iota(jnp.int32, (1, chunks * lanes), 1) // head_dim

    def cell_step(p, carry):
        rows = pl.ds(p, frames, stride=cells)
        q, k, v = (
            jnp.concatenate([qkv_ref[i * chunks + j, rows, :] for j in range(chunks)], 1)
            for i in range(3)
        )
        q = q * (head_dim**-0.5)
        k = k.astype(jnp.bfloat16)
        v = v.astype(jnp.bfloat16)
        q_all = jnp.concatenate(
            [jnp.where(lane_head == h, q, 0.0) for h in range(HEADS)], 0
        ).astype(jnp.bfloat16)
        scores = lax.dot_general(k, q_all, NT, preferred_element_type=jnp.float32) * LOG2E
        mixed = jnp.zeros((frames, wide), jnp.float32)
        for back in range(REACH + 1):
            s = scores + bias_ref[back]
            e = jnp.exp2(s - jnp.max(s, axis=0, keepdims=True))
            z = jnp.sum(e, axis=0, keepdims=True)
            mixed = mixed + e * (coef_ref[back] / z)
        full = lax.dot_general(
            mixed.astype(jnp.bfloat16), v, TN, preferred_element_type=jnp.float32
        )
        out = full[:frames]
        for h in range(1, HEADS):
            out = jnp.where(lane_head == h, full[h * frames : (h + 1) * frames], out)
        for j in range(chunks):
            acc_ref[j, rows, :] = out[:, j * lanes : (j + 1) * lanes]
        return carry

    for p in range(cells):
        cell_step(p, 0)
    gathered = jnp.concatenate([acc_ref[j] for j in range(chunks)], 1)
    out_ref[...] = gathered[:, :channels].astype(out_ref.dtype)


def attend(x, norm_gain, w_qkv, offsets, numerators, frames, cells):
    channels = x.shape[-1]
    vmem = pl.BlockSpec(memory_space=pltpu.VMEM)
    smem = pl.BlockSpec(memory_space=pltpu.SMEM)
    rows = frames * cells
    wide = HEADS * frames
    chunks = -(-channels // LANES)
    return pl.pallas_call(
        functools.partial(attend_kernel, frames, cells),
        out_shape=jax.ShapeDtypeStruct((rows, channels), jnp.bfloat16),
        in_specs=[smem, smem, vmem, vmem, vmem],
        out_specs=vmem,
        scratch_shapes=[
            pltpu.VMEM((3 * chunks, rows, LANES), jnp.float32),
            pltpu.VMEM((REACH + 1, frames, wide), jnp.float32),
            pltpu.VMEM((REACH + 1, 1, wide), jnp.float32),
            pltpu.VMEM((chunks, rows, LANES), jnp.float32),
        ],
        compiler_params=pltpu.CompilerParams(vmem_limit_bytes=40 * 1024 * 1024),
        name="window_attention",
    )(offsets, numerators, x, norm_gain.reshape(1, channels), w_qkv)


def group_mean(sums, spread, count):
    high = sums.astype(jnp.bfloat16)
    left = sums - high.astype(jnp.float32)
    mid = left.astype(jnp.bfloat16)
    low = (left - mid.astype(jnp.float32)).astype(jnp.bfloat16)
    dot = functools.partial(jnp.dot, preferred_element_type=jnp.float32)
    return (dot(high, spread) + dot(mid, spread) + dot(low, spread)) * (1.0 / count)


def group_act(rows, gain, spread, count):
    sums = sum(jnp.sum(row, axis=1) for row in rows)
    average = group_mean(sums, spread, count)
    cens = [row - average[:, None, :] for row in rows]
    variance = group_mean(sum(jnp.sum(cen * cen, axis=1) for cen in cens), spread, count)
    scale = lax.rsqrt(variance + EPS) * gain
    acts = []
    for cen in cens:
        v = cen * scale[:, None, :]
        acts.append(v / (1.0 + jnp.exp(-v)))
    return acts


def conv_rows(acts, w_ref, taps_ref):
    frames, cols, channels = acts[0].shape
    deep = w_ref.shape[1]
    count = len(acts)
    col = lax.broadcasted_iota(jnp.int32, (frames * cols, 1), 0) % cols
    for r, act in enumerate(acts):
        flat = act.reshape(frames * cols, channels)
        before = jnp.where(col == 0, 0.0, pltpu.roll(flat, 1, 0))
        after = jnp.where(col == cols - 1, 0.0, pltpu.roll(flat, frames * cols - 1, 0))
        for kw, part in enumerate((before, flat, after)):
            start = (3 * r + kw) * deep
            taps_ref[:, start : start + channels] = part.astype(jnp.bfloat16)
    outs = []
    for r in range(count):
        lo, hi = max(r - 1, 0), min(r + 1, count - 1)
        left = taps_ref[:, 3 * lo * deep : 3 * (hi + 1) * deep]
        right = w_ref[3 * (lo - r + 1) : 3 * (hi - r + 2)]
        right = right.reshape(-1, channels)
        out = jnp.dot(left, right, preferred_element_type=jnp.float32)
        outs.append(out.reshape(frames, cols, channels))
    return outs


def res_kernel(
    comb_ref, lat_ref, w_out_ref, gn_ref, step_ref, one_hbm, two_hbm, out_ref, one_ref, two_ref, taps_ref, sem
):
    frames, count, cols, channels = lat_ref.shape
    deep = one_ref.shape[1]
    copies = []
    for i, (src, dst) in enumerate(((one_hbm, one_ref), (two_hbm, two_ref))):
        copy = pltpu.make_async_copy(src, dst.at[:, :channels, :], sem.at[i])
        copy.start()
        copies.append(copy)
    for ref in (one_ref, two_ref):
        ref[:, channels:, :] = jnp.zeros((ref.shape[0], deep - channels, channels), jnp.bfloat16)
    for i in range(3 * count):
        taps_ref[:, i * deep + channels : (i + 1) * deep] = jnp.zeros(
            (frames * cols, deep - channels), jnp.bfloat16
        )
    size = channels // NORM_GROUPS
    group_r = lax.broadcasted_iota(jnp.int32, (channels, channels), 0) // size
    group_c = lax.broadcasted_iota(jnp.int32, (channels, channels), 1) // size
    spread = jnp.where(group_r == group_c, 1.0, 0.0).astype(jnp.bfloat16)
    members = count * cols * size

    hidden = []
    for r in range(count):
        comb = comb_ref[:, r * cols : (r + 1) * cols, :].reshape(frames * cols, channels)
        proj = jnp.dot(comb, w_out_ref[...], preferred_element_type=jnp.float32)
        hid = lat_ref[:, r].astype(jnp.float32) + proj.reshape(frames, cols, channels)
        hidden.append(hid.astype(jnp.bfloat16).astype(jnp.float32))
    acts = group_act(hidden, gn_ref[0:1], spread, members)
    copies[0].wait()
    middle = [row + step_ref[...][None] for row in conv_rows(acts, one_ref, taps_ref)]
    acts = group_act(middle, gn_ref[1:2], spread, members)
    copies[1].wait()
    for r, row in enumerate(conv_rows(acts, two_ref, taps_ref)):
        out_ref[:, r] = (hidden[r] + row).astype(out_ref.dtype)


def res_block(combined, latents, w_out, gn_gain, conv_one, conv_two, step_embed):
    frames, count, cols, channels = latents.shape
    deep = -(-channels // 128) * 128
    vmem = pl.BlockSpec(memory_space=pltpu.VMEM)
    hbm = pl.BlockSpec(memory_space=pl.ANY)
    return pl.pallas_call(
        res_kernel,
        out_shape=jax.ShapeDtypeStruct(latents.shape, jnp.bfloat16),
        in_specs=[vmem] * 5 + [hbm] * 2,
        out_specs=vmem,
        scratch_shapes=[
            pltpu.VMEM((9, deep, channels), jnp.bfloat16),
            pltpu.VMEM((9, deep, channels), jnp.bfloat16),
            pltpu.VMEM((frames * cols, 3 * count * deep), jnp.bfloat16),
            pltpu.SemaphoreType.DMA((2,)),
        ],
        compiler_params=pltpu.CompilerParams(vmem_limit_bytes=32 * 1024 * 1024),
        name="res_block",
    )(
        combined,
        latents,
        w_out,
        gn_gain,
        step_embed.reshape(1, channels),
        conv_one.reshape(9, channels, channels),
        conv_two.reshape(9, channels, channels),
    )


def body(
    latents, norm_gain, w_qkv, w_out, gn_gain, conv_one, conv_two, step_embed, offsets, numerators
):
    block_len, tile_rows, tile_cols, channels = latents.shape
    count = lax.axis_size("frame")
    cells = tile_rows * tile_cols // count
    frames = block_len * count
    local = latents.reshape(block_len, tile_rows * tile_cols, channels)
    spread = lax.all_to_all(local, "frame", 1, 0, tiled=True)
    combined = attend(
        spread.reshape(frames * cells, channels), norm_gain, w_qkv, offsets, numerators, frames, cells
    )
    combined = lax.all_to_all(
        combined.reshape(frames, cells, channels), "frame", 0, 1, tiled=True
    )
    return res_block(combined, latents, w_out, gn_gain, conv_one, conv_two, step_embed)


def solution(mesh):
    return jax.shard_map(
        body,
        mesh=mesh,
        in_specs=(
            P(("groups", "frame"), None, None, None),
            P(),
            P(),
            P(),
            P(),
            P(),
            P(),
            P(),
            P("groups"),
            P(),
        ),
        out_specs=P(("groups", "frame"), None, None, None),
        check_vma=False,
    )
```

time: 158 us -> 53.3 us (0.34)
  the two profiles are of different devices: /device:TPU:5 before, /device:TPU:0 now
where the time goes in v1:
time: 53.3 us; the launch traced here: 52.9 us
  waiting for transfers between devices  23.7 us (44%)
  Pallas kernels  12.3 us (23%)
  starting transfers between devices  11.1 us (21%)
  local copies, waits for them, and re-layouts  5.57 us (10%)
    all_to_all x1, waiting for transfers between devices, body(): lax.all_to_all(combined.reshape(frames, cells, channels), 'frame', 0, 1,...  12.1 us
    all_to_all x1, waiting for transfers between devices, body(): spread = lax.all_to_all(local, 'frame', 1, 0, tiled=True)  11.6 us
    all_to_all x1, starting transfers between devices, body(): spread = lax.all_to_all(local, 'frame', 1, 0, tiled=True)  7.57 us
    pallas_call x1, Pallas kernels, res_block(): pl.pallas_call(res_kernel, out_shape=jax.ShapeDtypeStruct(latents.shape,...  6.18 us
    pallas_call x1, Pallas kernels, attend(): pl.pallas_call(functools.partial(attend_kernel, frames, cells), out_shape...  6.16 us
    unnamed x19, local copies, waits for them, and re-layouts  3.76 us
    all_to_all x1, starting transfers between devices, body(): lax.all_to_all(combined.reshape(frames, cells, channels), 'frame', 0, 1,...  3.55 us
    all_to_all x2, local copies, waits for them, and re-layouts, body(): spread = lax.all_to_all(local, 'frame', 1, 0, tiled=True)  1.08 us
  transfers between devices with their start and end apart: 2, of which 2 were waited for; matrix products, arithmetic and copies ran while one was open for 1% of the time, Pallas kernels for 0%

profile of v1, /device:TPU:0, one launch (start us, length us, event | category | flops | bytes accessed | tf_op | source)
XLA Modules:
  0.0 52.9 jit_solution(8869893986303635425)
XLA Ops:
  0.0 0.0 copy-start.3
  0.0 0.0 copy-start.6
  0.0 0.0 copy-start.7
  0.0 2.1 %copy.13 = bf16[4,2,64,320]{3,0,2,1:T(4,128)(2,1)} copy(bf16[4,2,64,320]{3,2,1,0:T(8,128)(2,1)} %lat_ref.1) | data formatting | bytes 655360 | tf_op args[0]
  2.1 0.0 copy-start.8
  2.1 7.6 %all-to-all-start = ((bf16[4,128,320]{2,0,1:T(4,128)(2,1)}), bf16[4,128,320]{2,0,1:T(4,128)(2,1)}, u32[]{:S(2)}, u32[]{:S(2)}) async-start(bf16[4,128,320]{2,0,1:T(4,128)(2,1)} %bitcast), calls=%async_computation | async-start | bytes 786432 | tf_op jit(solution)/shard_map/all_to_all | solution.py:245
  9.7 0.7 %reshape.24.gain_ref = f32[1,320]{1,0:T(1,128)S(1)} reshape(f32[320]{0:T(512)} %param.11) | data formatting | bytes 2560 | tf_op jit(solution)/shard_map/reshape | solution.py:123
  10.4 0.0 copy-start
  10.4 11.6 %all-to-all-done = bf16[4,128,320]{2,0,1:T(4,128)(2,1)} async-done(((bf16[4,128,320]{2,0,1:T(4,128)(2,1)}), bf16[4,128,320]{2,0,1:T(4,128)(2,1)}, u32[]{:S(2)}, u32[]{:S(2)}) %all-to-all-start) | async-done | bytes 327712 | tf_op jit(solution)/shard_map/all_to_all | solution.py:245
  22.0 1.0 %copy.20 = bf16[4,128,320]{2,1,0:T(8,128)(2,1)S(1)} copy(bf16[4,128,320]{2,0,1:T(4,128)(2,1)} %all-to-all-done) | data formatting | bytes 655360 | tf_op jit(solution)/shard_map/all_to_all | solution.py:245
  23.0 0.0 copy-done.3
  23.1 0.0 copy-done.6
  23.1 0.0 copy-done.7
  23.1 6.2 %window_attention.1 = bf16[512,320]{1,0:T(8,128)(2,1)} custom-call(s32[16]{0:T(128)S(1)} %copy-done.6, s32[16]{0:T(128)S(1)} %copy-done.7, bf16[512,320]{1,0:T(8,128)(2,1)S(1)} %bitcast.18, f32[1,320]{1,0:T(1,128)S(1)} %reshape.24.gain_ref, bf16[320,960]{1,0:T(8,128)(2,1)S(1)} %copy-done.3), custom_call_target="tpu_custom_call" | custom-call | tf_op jit(solution)/shard_map/window_attention/pallas_call | solution.py:110
  29.2 3.6 %all-to-all-start.1 = ((bf16[64,8,320]{2,1,0:T(8,128)(2,1)}), bf16[64,8,320]{2,1,0:T(8,128)(2,1)S(1)}, u32[]{:S(2)}, u32[]{:S(2)}) async-start(bf16[64,8,320]{2,1,0:T(8,128)(2,1)} %bitcast.4), calls=%async_computation.1 | async-start | bytes 786432 | tf_op jit(solution)/shard_map/all_to_all | solution.py:249
  32.8 0.0 copy-done.8
  32.8 12.1 %all-to-all-done.1 = bf16[64,8,320]{2,1,0:T(8,128)(2,1)S(1)} async-done(((bf16[64,8,320]{2,1,0:T(8,128)(2,1)}), bf16[64,8,320]{2,1,0:T(8,128)(2,1)S(1)}, u32[]{:S(2)}, u32[]{:S(2)}) %all-to-all-start.1) | async-done | bytes 327712 | tf_op jit(solution)/shard_map/all_to_all | solution.py:249
  45.0 0.0 copy-done
  45.0 0.0 copy-done.2
  45.0 0.0 copy-done.4
  45.0 0.0 copy-done.5
  45.1 0.0 copy-start.1
  45.1 1.6 %copy-done.1 = bf16[3,3,320,320]{3,2,1,0:T(8,128)(2,1)S(1)} copy-done((bf16[3,3,320,320]{3,2,1,0:T(8,128)(2,1)S(1)}, bf16[3,3,320,320]{3,2,1,0:T(8,128)(2,1)}, u32[]{:S(2)}) %copy-start.1) | copy-done | bytes 1843224
  46.7 6.2 %res_block.1 = bf16[4,2,64,320]{3,2,1,0:T(8,128)(2,1)} custom-call(bf16[4,128,320]{2,1,0:T(8,128)(2,1)S(1)} %bitcast.19, bf16[4,2,64,320]{3,2,1,0:T(8,128)(2,1)S(1)} %copy-done.2, bf16[320,320]{1,0:T(8,128)(2,1)S(1)} %copy-done.4, f32[2,320]{1,0:T(2,128)S(1)} %copy-done.5, f32[1,320]{1,0:T(1,128)S(1)} %reshape.26.step_ref, ...), custom_call_target="tpu_custom_call" | custom-call | tf_op jit(solution)/shard_map/res_block/pallas_call | solution.py:213
  (6 shorter events, 0.1 us)
Async XLA Ops:
  0.0 23.1 %copy-start.3 = (bf16[320,960]{1,0:T(8,128)(2,1)S(1)}, bf16[320,960]{1,0:T(8,128)(2,1)}, u32[]{:S(2)}) copy-start(bf16[320,960]{1,0:T(8,128)(2,1)} %w_ref.1) | copy-start | bytes 1843204
  0.0 23.1 %copy-start.6 = (s32[16]{0:T(128)S(1)}, s32[16]{0:T(128)}, u32[]{:S(2)}) copy-start(s32[16]{0:T(128)} %off_ref.1) | copy-start | bytes 196
  0.0 23.1 %copy-start.7 = (s32[16]{0:T(128)S(1)}, s32[16]{0:T(128)}, u32[]{:S(2)}) copy-start(s32[16]{0:T(128)} %num_ref.1) | copy-start | bytes 196
  2.1 30.7 %copy-start.8 = (f32[320]{0:T(512)S(1)}, f32[320]{0:T(512)}, u32[]{:S(2)}) copy-start(f32[320]{0:T(512)} %param.17) | copy-start | bytes 3844
  2.1 19.8 %all-to-all-start = ((bf16[4,128,320]{2,0,1:T(4,128)(2,1)}), bf16[4,128,320]{2,0,1:T(4,128)(2,1)}, u32[]{:S(2)}, u32[]{:S(2)}) async-start(bf16[4,128,320]{2,0,1:T(4,128)(2,1)} %bitcast), calls=%async_computation | async-start | bytes 786432 | tf_op jit(solution)/shard_map/all_to_all | solution.py:245
  10.4 34.6 %copy-start = (bf16[3,3,320,320]{3,2,1,0:T(8,128)(2,1)S(1)}, bf16[3,3,320,320]{3,2,1,0:T(8,128)(2,1)}, u32[]{:S(2)}) copy-start(bf16[3,3,320,320]{3,2,1,0:T(8,128)(2,1)} %param.15) | copy-start | bytes 5529604
  10.4 34.6 %copy-start.2 = (bf16[4,2,64,320]{3,2,1,0:T(8,128)(2,1)S(1)}, bf16[4,2,64,320]{3,2,1,0:T(8,128)(2,1)}, u32[]{:S(2)}) copy-start(bf16[4,2,64,320]{3,2,1,0:T(8,128)(2,1)} %lat_ref.1) | copy-start | bytes 983044
  10.4 34.6 %copy-start.4 = (bf16[320,320]{1,0:T(8,128)(2,1)S(1)}, bf16[320,320]{1,0:T(8,128)(2,1)}, u32[]{:S(2)}) copy-start(bf16[320,320]{1,0:T(8,128)(2,1)} %w_out_ref.1) | copy-start | bytes 614404
  10.4 34.7 %copy-start.5 = (f32[2,320]{1,0:T(2,128)S(1)}, f32[2,320]{1,0:T(2,128)}, u32[]{:S(2)}) copy-start(f32[2,320]{1,0:T(2,128)} %gn_ref.1) | copy-start | bytes 7684
  29.2 15.7 %all-to-all-start.1 = ((bf16[64,8,320]{2,1,0:T(8,128)(2,1)}), bf16[64,8,320]{2,1,0:T(8,128)(2,1)S(1)}, u32[]{:S(2)}, u32[]{:S(2)}) async-start(bf16[64,8,320]{2,1,0:T(8,128)(2,1)} %bitcast.4), calls=%async_computation.1 | async-start | bytes 786432 | tf_op jit(solution)/shard_map/all_to_all | solution.py:249
  45.1 1.6 %copy-start.1 = (bf16[3,3,320,320]{3,2,1,0:T(8,128)(2,1)S(1)}, bf16[3,3,320,320]{3,2,1,0:T(8,128)(2,1)}, u32[]{:S(2)}) copy-start(bf16[3,3,320,320]{3,2,1,0:T(8,128)(2,1)} %param.16) | copy-start | bytes 5529604

commit v2 on v1

v2 whole, which is shorter than its diff:
```python
import functools

import jax
import jax.numpy as jnp
from jax import lax
from jax.experimental import pallas as pl
from jax.experimental.pallas import tpu as pltpu
from jax.sharding import PartitionSpec as P

HEADS = 5
NORM_GROUPS = 32
BLOCK = 4
WINDOW = 16
REACH = WINDOW // BLOCK
EPS = 1e-05
LANES = 128
GROUP = 4
LOG2E = 1.4426950408889634
NT = (((1,), (1,)), ((), ()))
QUARTERS = 4
PACK = 2


def place():
    me = lax.axis_index("frame")
    return me % 2, me // 2 % 2, me // QUARTERS


def moved(array, target):
    count = lax.axis_size("frame")
    return lax.ppermute(array, "frame", [(i, target(i) % count) for i in range(count)])


def pack_kernel(lat_ref, mine_ref, theirs_ref):
    core, chip, _ = place()
    frames, _, cells, channels = lat_ref.shape
    half = cells // PACK
    for out_ref, side in ((mine_ref, core), (theirs_ref, 1 - core)):
        for i, tall in enumerate((chip, 1 - chip)):
            x = lat_ref[:, side * 2 + tall]
            x = jnp.concatenate([x[:, :half], x[:, half:]], -1)
            out_ref[i] = x.reshape(frames * half, PACK * channels)


def join_kernel(mine_ref, other_ref, near_ref, far_ref):
    rows = mine_ref.shape[1]
    for i, out_ref in enumerate((near_ref, far_ref)):
        out_ref[:rows] = mine_ref[i]
        out_ref[rows:] = other_ref[i]


def attend_kernel(
    cells, planes, off_ref, num_ref, *refs
):
    parts = refs[:6]
    gain_ref, w_ref, own_ref, sib_ref, far_own_ref, far_sib_ref = refs[6:12]
    norm_ref, q_ref, k_ref, v_ref, bias_ref, coef_ref, acc_ref = refs[12:]
    core, chip, plane = place()
    channels = w_ref.shape[0]
    head_dim = channels // HEADS
    half = cells // PACK
    part_rows = parts[0].shape[0]
    part_frames = part_rows // half
    key_frames, query_frames = part_frames * 6, part_frames * 2
    key_rows, query_rows = key_frames * half, query_frames * half
    blocks = planes * QUARTERS
    frames = blocks * BLOCK
    group = GROUP
    wide = group * HEADS * query_frames
    chunks, lanes = k_ref.shape[0], k_ref.shape[2]

    for b, part in enumerate(parts):
        for a in range(PACK):
            x = part[:, a * channels : (a + 1) * channels].astype(jnp.float32)
            cen = x - jnp.mean(x, axis=-1, keepdims=True)
            var = jnp.mean(cen * cen, axis=-1, keepdims=True)
            start = a * key_rows + b * part_rows
            norm_ref[start : start + part_rows] = (
                cen * lax.rsqrt(var + EPS) * gain_ref[...]
            ).astype(jnp.bfloat16)
    pad = jnp.zeros((channels, chunks * lanes - channels), jnp.bfloat16)
    for i, (out_ref, rows) in enumerate(((q_ref, query_rows), (k_ref, key_rows), (v_ref, key_rows))):
        w = jnp.concatenate([w_ref[:, i * channels : (i + 1) * channels], pad], 1)
        for a in range(PACK):
            here = norm_ref[a * key_rows : a * key_rows + rows]
            res = jnp.dot(here, w, preferred_element_type=jnp.float32)
            for j in range(chunks):
                out_ref[j, a * rows : (a + 1) * rows] = res[:, j * lanes : (j + 1) * lanes]

    ids = []
    for step in (0, planes - 1, 1):
        for tall in (chip, 1 - chip):
            base = lax.rem(plane + step, planes) * QUARTERS + 2 * tall
            ids += [base + core, base + 1 - core]
    lane = lax.broadcasted_iota(jnp.int32, (1, wide), 1)
    query = lane % query_frames
    block = jnp.zeros((1, wide), jnp.int32)
    for i in range(query_frames // BLOCK):
        block = jnp.where(query // BLOCK == i, ids[i], block)
    rest = query % BLOCK
    spot = lax.broadcasted_iota(jnp.int32, (key_frames, wide), 0)
    key = jnp.zeros((key_frames, wide), jnp.int32)
    for i, at in enumerate(ids):
        key = jnp.where(spot // BLOCK == i, at * BLOCK, key)
    key = key + spot % BLOCK
    weights = []
    for back in range(REACH + 1):
        owner = block - back
        owner = jnp.where(owner < 0, owner + blocks, owner)
        shift = jnp.zeros((1, wide), jnp.int32)
        for w in range(blocks):
            shift = jnp.where(owner == w, off_ref[w], shift)
        at = BLOCK * back + rest - shift
        weight = jnp.zeros((1, wide), jnp.int32)
        for j in range(WINDOW):
            weight = jnp.where(at == j, num_ref[j], weight)
        weights.append(weight.astype(jnp.float32))
        rel = key - (BLOCK * owner + shift)
        rel = jnp.where(rel < 0, rel + frames, rel)
        bias_ref[back] = jnp.where(rel < WINDOW, 0.0, -1e30)
    total = sum(weights)
    for back in range(REACH + 1):
        coef_ref[back] = weights[back] / total

    lane_head = lax.broadcasted_iota(jnp.int32, (1, chunks * lanes), 1) // head_dim
    lane_cell = lane // (HEADS * query_frames)
    span = HEADS * query_frames

    def rows_of(ref, start, size):
        rows = pl.ds(start, size, stride=half)
        return jnp.concatenate([ref[j, rows, :] for j in range(chunks)], 1)

    def group_step(a, first):
        keys, values, queries = [], [], []
        for g in range(group):
            at = first + g
            keys.append(rows_of(k_ref, a * key_rows + at, key_frames).astype(jnp.bfloat16))
            values.append(rows_of(v_ref, a * key_rows + at, key_frames).astype(jnp.bfloat16))
            q = rows_of(q_ref, a * query_rows + at, query_frames) * (head_dim**-0.5)
            queries += [jnp.where(lane_head == h, q, 0.0) for h in range(HEADS)]
        keys = jnp.concatenate(keys, 0)
        queries = jnp.concatenate(queries, 0).astype(jnp.bfloat16)
        cross = lax.dot_general(keys, queries, NT, preferred_element_type=jnp.float32)
        scores = cross[:key_frames]
        for g in range(1, group):
            scores = jnp.where(lane_cell == g, cross[g * key_frames : (g + 1) * key_frames], scores)
        scores = scores * LOG2E
        mixed = jnp.zeros((key_frames, wide), jnp.float32)
        for back in range(REACH + 1):
            s = scores + bias_ref[back]
            e = jnp.exp2(s - jnp.max(s, axis=0, keepdims=True))
            z = jnp.sum(e, axis=0, keepdims=True)
            mixed = mixed + e * (coef_ref[back] / z)
        mixed = mixed.T.astype(jnp.bfloat16)
        for g in range(group):
            full = jnp.dot(
                mixed[g * span : (g + 1) * span], values[g], preferred_element_type=jnp.float32
            )
            out = full[:query_frames]
            for h in range(1, HEADS):
                out = jnp.where(lane_head == h, full[h * query_frames : (h + 1) * query_frames], out)
            rows = pl.ds(a * query_rows + first + g, query_frames, stride=half)
            for j in range(chunks):
                acc_ref[j, rows, :] = out[:, j * lanes : (j + 1) * lanes]

    for a in range(PACK):
        for first in range(0, half, group):
            group_step(a, first)
    quarter = query_rows // 4
    for i, out_ref in enumerate((own_ref, sib_ref, far_own_ref, far_sib_ref)):
        pieces = []
        for a in range(PACK):
            start = a * query_rows + i * quarter
            piece = jnp.concatenate([acc_ref[j, start : start + quarter] for j in range(chunks)], 1)
            pieces.append(piece[:, :channels])
        out_ref[...] = jnp.concatenate(pieces, 1).astype(out_ref.dtype)


def attend(parts, norm_gain, w_qkv, offsets, numerators, cells, planes):
    channels = w_qkv.shape[0]
    vmem = pl.BlockSpec(memory_space=pltpu.VMEM)
    smem = pl.BlockSpec(memory_space=pltpu.SMEM)
    rows, packed = parts[0].shape
    chunks = -(-channels // LANES)
    query_frames = 2 * rows * PACK // cells
    wide = GROUP * HEADS * query_frames
    keys, queries = 6 * rows * PACK, 2 * rows * PACK
    return pl.pallas_call(
        functools.partial(attend_kernel, cells, planes),
        out_shape=[jax.ShapeDtypeStruct((rows // 2, packed), jnp.bfloat16)] * 4,
        in_specs=[smem, smem] + [vmem] * 8,
        out_specs=[vmem] * 4,
        scratch_shapes=[
            pltpu.VMEM((keys, channels), jnp.bfloat16),
            pltpu.VMEM((chunks, queries, LANES), jnp.float32),
            pltpu.VMEM((chunks, keys, LANES), jnp.float32),
            pltpu.VMEM((chunks, keys, LANES), jnp.float32),
            pltpu.VMEM((REACH + 1, 3 * query_frames, wide), jnp.float32),
            pltpu.VMEM((REACH + 1, 1, wide), jnp.float32),
            pltpu.VMEM((chunks, queries, LANES), jnp.float32),
        ],
        compiler_params=pltpu.CompilerParams(vmem_limit_bytes=24 * 1024 * 1024),
        name="window_attention",
    )(offsets, numerators, *parts, norm_gain.reshape(1, channels), w_qkv)


def group_mean(sums, spread, count):
    high = sums.astype(jnp.bfloat16)
    left = sums - high.astype(jnp.float32)
    mid = left.astype(jnp.bfloat16)
    low = (left - mid.astype(jnp.float32)).astype(jnp.bfloat16)
    dot = functools.partial(jnp.dot, preferred_element_type=jnp.float32)
    return (dot(high, spread) + dot(mid, spread) + dot(low, spread)) * (1.0 / count)


def group_act(rows, gain, spread, count):
    sums = sum(jnp.sum(row, axis=1) for row in rows)
    average = group_mean(sums, spread, count)
    cens = [row - average[:, None, :] for row in rows]
    variance = group_mean(sum(jnp.sum(cen * cen, axis=1) for cen in cens), spread, count)
    scale = lax.rsqrt(variance + EPS) * gain
    acts = []
    for cen in cens:
        v = cen * scale[:, None, :]
        acts.append(v / (1.0 + jnp.exp(-v)))
    return acts


def conv_rows(acts, w_ref, taps_ref):
    frames, cols, channels = acts[0].shape
    deep = w_ref.shape[1]
    count = len(acts)
    col = lax.broadcasted_iota(jnp.int32, (frames * cols, 1), 0) % cols
    for r, act in enumerate(acts):
        flat = act.reshape(frames * cols, channels)
        before = jnp.where(col == 0, 0.0, pltpu.roll(flat, 1, 0))
        after = jnp.where(col == cols - 1, 0.0, pltpu.roll(flat, frames * cols - 1, 0))
        for kw, part in enumerate((before, flat, after)):
            start = (3 * r + kw) * deep
            taps_ref[:, start : start + channels] = part.astype(jnp.bfloat16)
    outs = []
    for r in range(count):
        lo, hi = max(r - 1, 0), min(r + 1, count - 1)
        left = taps_ref[:, 3 * lo * deep : 3 * (hi + 1) * deep]
        right = w_ref[3 * (lo - r + 1) : 3 * (hi - r + 2)]
        right = right.reshape(-1, channels)
        out = jnp.dot(left, right, preferred_element_type=jnp.float32)
        outs.append(out.reshape(frames, cols, channels))
    return outs


def res_kernel(
    p0_ref, p1_ref, p2_ref, p3_ref, lat_ref, w_out_ref, gn_ref, step_ref, one_hbm, two_hbm, out_ref,
    comb_ref, one_ref, two_ref, taps_ref, sem
):
    frames, count, cols, channels = lat_ref.shape
    deep = one_ref.shape[1]
    copies = []
    for i, (src, dst) in enumerate(((one_hbm, one_ref), (two_hbm, two_ref))):
        copy = pltpu.make_async_copy(src, dst.at[:, :channels, :], sem.at[i])
        copy.start()
        copies.append(copy)
    for ref in (one_ref, two_ref):
        ref[:, channels:, :] = jnp.zeros((ref.shape[0], deep - channels, channels), jnp.bfloat16)
    for i in range(3 * count):
        taps_ref[:, i * deep + channels : (i + 1) * deep] = jnp.zeros(
            (frames * cols, deep - channels), jnp.bfloat16
        )
    size = channels // NORM_GROUPS
    group_r = lax.broadcasted_iota(jnp.int32, (channels, channels), 0) // size
    group_c = lax.broadcasted_iota(jnp.int32, (channels, channels), 1) // size
    spread = jnp.where(group_r == group_c, 1.0, 0.0).astype(jnp.bfloat16)
    members = count * cols * size

    core, chip, _ = place()
    half = comb_ref.shape[2] // PACK
    for part, side, tall in (
        (p0_ref, core, chip), (p1_ref, 1 - core, chip), (p2_ref, core, 1 - chip), (p3_ref, 1 - core, 1 - chip)
    ):
        for a in range(PACK):
            piece = part[:, a * channels : (a + 1) * channels].reshape(frames, half, channels)
            comb_ref[:, side * 2 + tall, a * half : (a + 1) * half, :] = piece
    combined = comb_ref[...].reshape(frames, count * cols, channels)
    hidden = []
    for r in range(count):
        comb = combined[:, r * cols : (r + 1) * cols, :].reshape(frames * cols, channels)
        proj = jnp.dot(comb, w_out_ref[...], preferred_element_type=jnp.float32)
        hid = lat_ref[:, r].astype(jnp.float32) + proj.reshape(frames, cols, channels)
        hidden.append(hid.astype(jnp.bfloat16).astype(jnp.float32))
    acts = group_act(hidden, gn_ref[0:1], spread, members)
    copies[0].wait()
    middle = [row + step_ref[...][None] for row in conv_rows(acts, one_ref, taps_ref)]
    acts = group_act(middle, gn_ref[1:2], spread, members)
    copies[1].wait()
    for r, row in enumerate(conv_rows(acts, two_ref, taps_ref)):
        out_ref[:, r] = (hidden[r] + row).astype(out_ref.dtype)


def res_block(parts, latents, w_out, gn_gain, conv_one, conv_two, step_embed):
    frames, count, cols, channels = latents.shape
    deep = -(-channels // 128) * 128
    vmem = pl.BlockSpec(memory_space=pltpu.VMEM)
    hbm = pl.BlockSpec(memory_space=pltpu.HBM)
    return pl.pallas_call(
        res_kernel,
        out_shape=jax.ShapeDtypeStruct(latents.shape, jnp.bfloat16),
        in_specs=[vmem] * 8 + [hbm] * 2,
        out_specs=vmem,
        scratch_shapes=[
            pltpu.VMEM((frames, QUARTERS, count * cols // QUARTERS, channels), jnp.bfloat16),
            pltpu.VMEM((9, deep, channels), jnp.bfloat16),
            pltpu.VMEM((9, deep, channels), jnp.bfloat16),
            pltpu.VMEM((frames * cols, 3 * count * deep), jnp.bfloat16),
            pltpu.SemaphoreType.DMA((2,)),
        ],
        compiler_params=pltpu.CompilerParams(vmem_limit_bytes=24 * 1024 * 1024),
        name="res_block",
    )(
        *parts,
        latents,
        w_out,
        gn_gain,
        step_embed.reshape(1, channels),
        conv_one.reshape(9, channels, channels),
        conv_two.reshape(9, channels, channels),
    )


def body(
    latents, norm_gain, w_qkv, w_out, gn_gain, conv_one, conv_two, step_embed, offsets, numerators
):
    block_len, tile_rows, tile_cols, channels = latents.shape
    planes = lax.axis_size("frame") // QUARTERS
    cells = tile_rows * tile_cols // QUARTERS
    vmem = pl.BlockSpec(memory_space=pltpu.VMEM)
    rows, packed = block_len * cells // PACK, PACK * channels
    mine, theirs = pl.pallas_call(
        pack_kernel,
        out_shape=[jax.ShapeDtypeStruct((2, rows, packed), jnp.bfloat16)] * 2,
        in_specs=[vmem],
        out_specs=[vmem] * 2,
        name="pack",
    )(latents.reshape(block_len, QUARTERS, cells, channels))
    other = moved(theirs, lambda i: i ^ 1)
    near, far = pl.pallas_call(
        join_kernel,
        out_shape=[jax.ShapeDtypeStruct((2 * rows, packed), jnp.bfloat16)] * 2,
        in_specs=[vmem] * 2,
        out_specs=[vmem] * 2,
        name="join",
    )(mine, other)
    parts = [
        near,
        moved(far, lambda i: i ^ 2),
        moved(near, lambda i: i + QUARTERS),
        moved(far, lambda i: (i ^ 2) + QUARTERS),
        moved(near, lambda i: i - QUARTERS),
        moved(far, lambda i: (i ^ 2) - QUARTERS),
    ]
    own, sib, far_own, far_sib = attend(
        parts, norm_gain, w_qkv, offsets, numerators, cells, planes
    )
    pieces = [
        own,
        moved(sib, lambda i: i ^ 1),
        moved(far_own, lambda i: i ^ 2),
        moved(moved(far_sib, lambda i: i ^ 1), lambda i: i ^ 2),
    ]
    return res_block(pieces, latents, w_out, gn_gain, conv_one, conv_two, step_embed)


def solution(mesh):
    return jax.shard_map(
        body,
        mesh=mesh,
        in_specs=(
            P(("groups", "frame"), None, None, None),
            P(),
            P(),
            P(),
            P(),
            P(),
            P(),
            P(),
            P("groups"),
            P(),
        ),
        out_specs=P(("groups", "frame"), None, None, None),
        check_vma=False,
    )
```

time: 53.3 us -> 59 us (1.11)
  waiting for transfers between devices: 23.7 us -> 15.5 us
  Pallas kernels: 12.3 us -> 20.4 us
  local copies, waits for them, and re-layouts: 5.57 us -> 9.59 us
  starting transfers between devices: 11.1 us -> 12.9 us
    all_to_all x2 -> x0, waiting for transfers between devices: 23.7 us -> none  [the longest x1 12.1 us: body(): lax.all_to_all(combined.reshape(frames, cells, channels), 'frame', 0, 1,...]
    ppermute x0 -> x10, waiting for transfers between devices: none -> 15.5 us  [moved(): lax.ppermute(array, 'frame', [(i, target(i) % count) for i in range(count)])]
    ppermute x0 -> x10, starting transfers between devices: none -> 12.9 us  [moved(): lax.ppermute(array, 'frame', [(i, target(i) % count) for i in range(count)])]
    all_to_all x2 -> x0, starting transfers between devices: 11.1 us -> none  [the longest x1 7.57 us: body(): spread = lax.all_to_all(local, 'frame', 1, 0, tiled=True)]
    pallas_call x1 -> x3, Pallas kernels: 6.16 us -> 14.1 us  [the longest x1 10.4 us: attend(): pl.pallas_call(functools.partial(attend_kernel, cells, planes), out_shape...]
    unnamed x19 -> x20, local copies, waits for them, and re-layouts: 3.76 us -> 8.22 us
    all_to_all x3 -> x0, local copies, waits for them, and re-layouts: 1.12 us -> none  [the longest x2 1.08 us: body(): spread = lax.all_to_all(local, 'frame', 1, 0, tiled=True)]
    reshape x1, local copies, waits for them, and re-layouts: 0.01 us -> 0.68 us  [res_block(): step_embed.reshape(1, channels)]
  transfers between devices with their start and end apart: 2 -> 10, of which waited for: 2 -> 7; matrix products, arithmetic and copies ran while one was open for 1% -> 2% of each run, Pallas kernels for 0% -> 0%
where the time goes in v2:
time: 59 us; the launch traced here: 58.6 us
  Pallas kernels  20.4 us (35%)
  waiting for transfers between devices  15.5 us (26%)
  starting transfers between devices  12.9 us (22%)
  local copies, waits for them, and re-layouts  9.59 us (16%)
    ppermute x10, waiting for transfers between devices, moved(): lax.ppermute(array, 'frame', [(i, target(i) % count) for i in range(count)])  15.5 us
    ppermute x10, starting transfers between devices, moved(): lax.ppermute(array, 'frame', [(i, target(i) % count) for i in range(count)])  12.9 us
    pallas_call x1, Pallas kernels, attend(): pl.pallas_call(functools.partial(attend_kernel, cells, planes), out_shape...  10.4 us
    unnamed x20, local copies, waits for them, and re-layouts  8.22 us
    pallas_call x1, Pallas kernels, res_block(): pl.pallas_call(res_kernel, out_shape=jax.ShapeDtypeStruct(latents.shape,...  6.3 us
    pallas_call x1, Pallas kernels, body(): pl.pallas_call(pack_kernel, out_shape=[jax.ShapeDtypeStruct((2, rows, pac...  1.96 us
    pallas_call x1, Pallas kernels, body(): pl.pallas_call(join_kernel, out_shape=[jax.ShapeDtypeStruct((2 * rows, pa...  1.73 us
  transfers between devices with their start and end apart: 10, of which 7 were waited for; matrix products, arithmetic and copies ran while one was open for 2% of the time, Pallas kernels for 0%

profile of v2, /device:TPU:0, one launch (start us, length us, event | category | flops | bytes accessed | tf_op | source)
XLA Modules:
  0.0 58.6 jit_solution(11145847692854143823)
XLA Ops:
  0.0 2.0 %pack.1 = (bf16[2,64,640]{2,1,0:T(8,128)(2,1)}, bf16[2,64,640]{2,1,0:T(8,128)(2,1)}) custom-call(bf16[4,4,32,320]{3,2,1,0:T(8,128)(2,1)} %bitcast.5), custom_call_target="tpu_custom_call" | custom-call | tf_op jit(solution)/shard_map/pack/pallas_call | solution.py:337
  2.4 1.2 %collective-permute-done.other_ref = bf16[2,64,640]{2,1,0:T(8,128)(2,1)S(1)} collective-permute-done((bf16[2,64,640]{2,1,0:T(8,128)(2,1)}, bf16[2,64,640]{2,1,0:T(8,128)(2,1)S(1)}, u32[]{:S(2)}, u32[]{:S(2)}) %collective-permute-start) | collective-permute-done | bytes 163872 | tf_op jit(solution)/shard_map/ppermute | solution.py:31
  4.3 1.7 %join.1 = (bf16[128,640]{1,0:T(8,128)(2,1)}, bf16[128,640]{1,0:T(8,128)(2,1)}) custom-call(bf16[2,64,640]{2,1,0:T(8,128)(2,1)} %get-tuple-element.13.mine_ref, bf16[2,64,640]{2,1,0:T(8,128)(2,1)} %copy-done.9), custom_call_target="tpu_custom_call" | custom-call | tf_op jit(solution)/shard_map/join/pallas_call | solution.py:345
  6.0 2.9 %collective-permute-start.1 = (bf16[128,640]{1,0:T(8,128)(2,1)}, bf16[128,640]{1,0:T(8,128)(2,1)S(1)}, u32[]{:S(2)}, u32[]{:S(2)}) collective-permute-start(bf16[128,640]{1,0:T(8,128)(2,1)} %get-tuple-element.16), channel_id=1, source_target_pairs={{0,2},{1,3},{2,0},{3,1},{4,6},{5,7},{6,4},{7,5},{8,10},{9,11},{10,... | collective-permute-start | bytes 491528 | tf_op jit(solution)/shard_map/ppermute | solution.py:31
  8.9 1.6 %collective-permute-start.2 = (bf16[128,640]{1,0:T(8,128)(2,1)}, bf16[128,640]{1,0:T(8,128)(2,1)S(1)}, u32[]{:S(2)}, u32[]{:S(2)}) collective-permute-start(bf16[128,640]{1,0:T(8,128)(2,1)} %get-tuple-element.15.refs_0_), channel_id=1, source_target_pairs={{0,4},{1,5},{2,6},{3,7},{4,8},{5,9},{6,10},{7,11},{8,12},{9,13},{1... | collective-permute-start | bytes 491528 | tf_op jit(solution)/shard_map/ppermute | solution.py:31
  10.5 1.5 %collective-permute-start.3 = (bf16[128,640]{1,0:T(8,128)(2,1)}, bf16[128,640]{1,0:T(8,128)(2,1)S(1)}, u32[]{:S(2)}, u32[]{:S(2)}) collective-permute-start(bf16[128,640]{1,0:T(8,128)(2,1)} %get-tuple-element.16), channel_id=1, source_target_pairs={{0,6},{1,7},{2,4},{3,5},{4,10},{5,11},{6,8},{7,9},{8,14},{9,15},{1... | collective-permute-start | bytes 491528 | tf_op jit(solution)/shard_map/ppermute | solution.py:31
  12.0 2.2 %collective-permute-start.4 = (bf16[128,640]{1,0:T(8,128)(2,1)}, bf16[128,640]{1,0:T(8,128)(2,1)S(1)}, u32[]{:S(2)}, u32[]{:S(2)}) collective-permute-start(bf16[128,640]{1,0:T(8,128)(2,1)} %get-tuple-element.15.refs_0_), channel_id=1, source_target_pairs={{0,12},{1,13},{2,14},{3,15},{4,0},{5,1},{6,2},{7,3},{8,4},{9,5},{1... | collective-permute-start | bytes 491528 | tf_op jit(solution)/shard_map/ppermute | solution.py:31
  14.3 1.4 %collective-permute-start.5 = (bf16[128,640]{1,0:T(8,128)(2,1)}, bf16[128,640]{1,0:T(8,128)(2,1)S(1)}, u32[]{:S(2)}, u32[]{:S(2)}) collective-permute-start(bf16[128,640]{1,0:T(8,128)(2,1)} %get-tuple-element.16), channel_id=1, source_target_pairs={{0,14},{1,15},{2,12},{3,13},{4,2},{5,3},{6,0},{7,1},{8,6},{9,7},{1... | collective-permute-start | bytes 491528 | tf_op jit(solution)/shard_map/ppermute | solution.py:31
  16.4 1.8 %collective-permute-done.2.refs_2_ = bf16[128,640]{1,0:T(8,128)(2,1)S(1)} collective-permute-done((bf16[128,640]{1,0:T(8,128)(2,1)}, bf16[128,640]{1,0:T(8,128)(2,1)S(1)}, u32[]{:S(2)}, u32[]{:S(2)}) %collective-permute-start.2) | collective-permute-done | bytes 163872 | tf_op jit(solution)/shard_map/ppermute | solution.py:31
  18.2 3.1 %collective-permute-done.3.refs_3_ = bf16[128,640]{1,0:T(8,128)(2,1)S(1)} collective-permute-done((bf16[128,640]{1,0:T(8,128)(2,1)}, bf16[128,640]{1,0:T(8,128)(2,1)S(1)}, u32[]{:S(2)}, u32[]{:S(2)}) %collective-permute-start.3) | collective-permute-done | bytes 163872 | tf_op jit(solution)/shard_map/ppermute | solution.py:31
  21.3 2.8 %collective-permute-done.4.refs_4_ = bf16[128,640]{1,0:T(8,128)(2,1)S(1)} collective-permute-done((bf16[128,640]{1,0:T(8,128)(2,1)}, bf16[128,640]{1,0:T(8,128)(2,1)S(1)}, u32[]{:S(2)}, u32[]{:S(2)}) %collective-permute-start.4) | collective-permute-done | bytes 163872 | tf_op jit(solution)/shard_map/ppermute | solution.py:31
  24.1 3.3 %collective-permute-done.5.refs_5_ = bf16[128,640]{1,0:T(8,128)(2,1)S(1)} collective-permute-done((bf16[128,640]{1,0:T(8,128)(2,1)}, bf16[128,640]{1,0:T(8,128)(2,1)S(1)}, u32[]{:S(2)}, u32[]{:S(2)}) %collective-permute-start.5) | collective-permute-done | bytes 163872 | tf_op jit(solution)/shard_map/ppermute | solution.py:31
  27.4 1.1 %copy-done.3 = bf16[320,960]{1,0:T(8,128)(2,1)S(1)} copy-done((bf16[320,960]{1,0:T(8,128)(2,1)S(1)}, bf16[320,960]{1,0:T(8,128)(2,1)}, u32[]{:S(2)}) %copy-start.3) | copy-done | bytes 614424
  28.5 0.9 %copy-done.5 = bf16[128,640]{1,0:T(8,128)(2,1)S(1)} copy-done((bf16[128,640]{1,0:T(8,128)(2,1)S(1)}, bf16[128,640]{1,0:T(8,128)(2,1)}, u32[]{:S(2)}) %copy-start.5) | copy-done | bytes 163864
  30.8 10.4 %window_attention.1 = (bf16[64,640]{1,0:T(8,128)(2,1)S(1)}, bf16[64,640]{1,0:T(8,128)(2,1)S(1)}, bf16[64,640]{1,0:T(8,128)(2,1)S(1)}, bf16[64,640]{1,0:T(8,128)(2,1)S(1)}) custom-call(s32[16]{0:T(128)S(1)} %copy-done.7, s32[16]{0:T(128)S(1)} %copy-done.8, bf16[128,640]{1,0:T(8,128)(2,1)S(1)} %copy-done.5, ...), custom_call_target="tpu_custom_call" | custom-call | tf_op jit(solution)/shard_map/window_attention/pallas_call | solution.py:188
  41.7 1.5 %collective-permute-start.7 = (bf16[64,640]{1,0:T(8,128)(2,1)S(1)}, bf16[64,640]{1,0:T(8,128)(2,1)S(1)}, u32[]{:S(2)}, u32[]{:S(2)}) collective-permute-start(bf16[64,640]{1,0:T(8,128)(2,1)S(1)} %get-tuple-element.19), channel_id=1, source_target_pairs={{0,2},{1,3},{2,0},{3,1},{4,6},{5,7},{6,4},{7,5},{8,10},{9,11},{10,... | collective-permute-start | bytes 245768 | tf_op jit(solution)/shard_map/ppermute | solution.py:31
  43.2 0.8 %collective-permute-start.9 = (bf16[64,640]{1,0:T(8,128)(2,1)S(1)}, bf16[64,640]{1,0:T(8,128)(2,1)S(1)}, u32[]{:S(2)}, u32[]{:S(2)}) collective-permute-start(bf16[64,640]{1,0:T(8,128)(2,1)S(1)} %collective-permute-done.8), channel_id=1, source_target_pairs={{0,2},{1,3},{2,0},{3,1},{4,6},{5,7},{6,4},{7,5},{8,10},{9,11},{10,... | collective-permute-start | bytes 245768 | tf_op jit(solution)/shard_map/ppermute | solution.py:31
  44.0 0.7 %reshape.17.step_ref = f32[1,320]{1,0:T(1,128)S(1)} reshape(f32[320]{0:T(512)} %param.17) | data formatting | bytes 2560 | tf_op jit(solution)/shard_map/reshape | solution.py:323
  44.7 2.1 %collective-permute-done.7.p2_ref = bf16[64,640]{1,0:T(8,128)(2,1)S(1)} collective-permute-done((bf16[64,640]{1,0:T(8,128)(2,1)S(1)}, bf16[64,640]{1,0:T(8,128)(2,1)S(1)}, u32[]{:S(2)}, u32[]{:S(2)}) %collective-permute-start.7) | collective-permute-done | bytes 81952 | tf_op jit(solution)/shard_map/ppermute | solution.py:31
  46.8 1.1 %collective-permute-done.9.p3_ref = bf16[64,640]{1,0:T(8,128)(2,1)S(1)} collective-permute-done((bf16[64,640]{1,0:T(8,128)(2,1)S(1)}, bf16[64,640]{1,0:T(8,128)(2,1)S(1)}, u32[]{:S(2)}, u32[]{:S(2)}) %collective-permute-start.9) | collective-permute-done | bytes 81952 | tf_op jit(solution)/shard_map/ppermute | solution.py:31
  47.9 1.6 %copy-done.1 = bf16[3,3,320,320]{3,2,1,0:T(8,128)(2,1)S(1)} copy-done((bf16[3,3,320,320]{3,2,1,0:T(8,128)(2,1)S(1)}, bf16[3,3,320,320]{3,2,1,0:T(8,128)(2,1)}, u32[]{:S(2)}) %copy-start.1) | copy-done | bytes 1843224
  49.5 1.0 %copy-done.2 = bf16[4,2,64,320]{3,2,1,0:T(8,128)(2,1)S(1)} copy-done((bf16[4,2,64,320]{3,2,1,0:T(8,128)(2,1)S(1)}, bf16[4,2,64,320]{3,2,1,0:T(8,128)(2,1)}, u32[]{:S(2)}) %copy-start.2) | copy-done | bytes 327704
  50.5 0.9 %copy-done.4 = bf16[320,320]{1,0:T(8,128)(2,1)S(1)} copy-done((bf16[320,320]{1,0:T(8,128)(2,1)S(1)}, bf16[320,320]{1,0:T(8,128)(2,1)}, u32[]{:S(2)}) %copy-start.4) | copy-done | bytes 204824
  52.2 6.3 %res_block.1 = bf16[4,2,64,320]{3,2,1,0:T(8,128)(2,1)} custom-call(bf16[64,640]{1,0:T(8,128)(2,1)S(1)} %get-tuple-element.17.p0_ref, bf16[64,640]{1,0:T(8,128)(2,1)S(1)} %collective-permute-done.6.p1_ref, bf16[64,640]{1,0:T(8,128)(2,1)S(1)} %collective-permute-done.7.p2_ref, bf16[64,640]{1,0:T(8,128)(2,1)S(1)} %collective-permute-done.9.p3_ref, ...), custom_call_target="tpu_custom_call" | custom-call | tf_op jit(solution)/shard_map/res_block/pallas_call | solution.py:304
  (22 shorter events, 4.4 us)
Async XLA Ops:
  0.0 47.9 %copy-start = (bf16[3,3,320,320]{3,2,1,0:T(8,128)(2,1)S(1)}, bf16[3,3,320,320]{3,2,1,0:T(8,128)(2,1)}, u32[]{:S(2)}) copy-start(bf16[3,3,320,320]{3,2,1,0:T(8,128)(2,1)} %param.15) | copy-start | bytes 5529604
  2.0 1.7 %collective-permute-start = (bf16[2,64,640]{2,1,0:T(8,128)(2,1)}, bf16[2,64,640]{2,1,0:T(8,128)(2,1)S(1)}, u32[]{:S(2)}, u32[]{:S(2)}) collective-permute-start(bf16[2,64,640]{2,1,0:T(8,128)(2,1)} %get-tuple-element.14), channel_id=1, source_target_pairs={{0,1},{1,0},{2,3},{3,2},{4,5},{5,4},{6,7},{7,6},{8,9},{9,8},{10,11... | collective-permute-start | bytes 491528 | tf_op jit(solution)/shard_map/ppermute | solution.py:31
  3.7 0.7 %copy-start.9 = (bf16[2,64,640]{2,1,0:T(8,128)(2,1)}, bf16[2,64,640]{2,1,0:T(8,128)(2,1)S(1)}, u32[]{:S(2)}) copy-start(bf16[2,64,640]{2,1,0:T(8,128)(2,1)S(1)} %collective-permute-done.other_ref) | copy-start | bytes 491524
  6.0 10.3 %collective-permute-start.1 = (bf16[128,640]{1,0:T(8,128)(2,1)}, bf16[128,640]{1,0:T(8,128)(2,1)S(1)}, u32[]{:S(2)}, u32[]{:S(2)}) collective-permute-start(bf16[128,640]{1,0:T(8,128)(2,1)} %get-tuple-element.16), channel_id=1, source_target_pairs={{0,2},{1,3},{2,0},{3,1},{4,6},{5,7},{6,4},{7,5},{8,10},{9,11},{10,... | collective-permute-start | bytes 491528 | tf_op jit(solution)/shard_map/ppermute | solution.py:31
  8.9 9.2 %collective-permute-start.2 = (bf16[128,640]{1,0:T(8,128)(2,1)}, bf16[128,640]{1,0:T(8,128)(2,1)S(1)}, u32[]{:S(2)}, u32[]{:S(2)}) collective-permute-start(bf16[128,640]{1,0:T(8,128)(2,1)} %get-tuple-element.15.refs_0_), channel_id=1, source_target_pairs={{0,4},{1,5},{2,6},{3,7},{4,8},{5,9},{6,10},{7,11},{8,12},{9,13},{1... | collective-permute-start | bytes 491528 | tf_op jit(solution)/shard_map/ppermute | solution.py:31
  10.5 10.8 %collective-permute-start.3 = (bf16[128,640]{1,0:T(8,128)(2,1)}, bf16[128,640]{1,0:T(8,128)(2,1)S(1)}, u32[]{:S(2)}, u32[]{:S(2)}) collective-permute-start(bf16[128,640]{1,0:T(8,128)(2,1)} %get-tuple-element.16), channel_id=1, source_target_pairs={{0,6},{1,7},{2,4},{3,5},{4,10},{5,11},{6,8},{7,9},{8,14},{9,15},{1... | collective-permute-start | bytes 491528 | tf_op jit(solution)/shard_map/ppermute | solution.py:31
  12.0 12.1 %collective-permute-start.4 = (bf16[128,640]{1,0:T(8,128)(2,1)}, bf16[128,640]{1,0:T(8,128)(2,1)S(1)}, u32[]{:S(2)}, u32[]{:S(2)}) collective-permute-start(bf16[128,640]{1,0:T(8,128)(2,1)} %get-tuple-element.15.refs_0_), channel_id=1, source_target_pairs={{0,12},{1,13},{2,14},{3,15},{4,0},{5,1},{6,2},{7,3},{8,4},{9,5},{1... | collective-permute-start | bytes 491528 | tf_op jit(solution)/shard_map/ppermute | solution.py:31
  14.3 13.2 %collective-permute-start.5 = (bf16[128,640]{1,0:T(8,128)(2,1)}, bf16[128,640]{1,0:T(8,128)(2,1)S(1)}, u32[]{:S(2)}, u32[]{:S(2)}) collective-permute-start(bf16[128,640]{1,0:T(8,128)(2,1)} %get-tuple-element.16), channel_id=1, source_target_pairs={{0,14},{1,15},{2,12},{3,13},{4,2},{5,3},{6,0},{7,1},{8,6},{9,7},{1... | collective-permute-start | bytes 491528 | tf_op jit(solution)/shard_map/ppermute | solution.py:31
  27.4 1.1 %copy-start.3 = (bf16[320,960]{1,0:T(8,128)(2,1)S(1)}, bf16[320,960]{1,0:T(8,128)(2,1)}, u32[]{:S(2)}) copy-start(bf16[320,960]{1,0:T(8,128)(2,1)} %refs_7_.1) | copy-start | bytes 1843204
  28.5 0.9 %copy-start.5 = (bf16[128,640]{1,0:T(8,128)(2,1)S(1)}, bf16[128,640]{1,0:T(8,128)(2,1)}, u32[]{:S(2)}) copy-start(bf16[128,640]{1,0:T(8,128)(2,1)} %get-tuple-element.15.refs_0_) | copy-start | bytes 491524
  29.4 0.7 %copy-start.7 = (s32[16]{0:T(128)S(1)}, s32[16]{0:T(128)}, u32[]{:S(2)}) copy-start(s32[16]{0:T(128)} %off_ref.1) | copy-start | bytes 196
  30.1 0.7 %copy-start.8 = (s32[16]{0:T(128)S(1)}, s32[16]{0:T(128)}, u32[]{:S(2)}) copy-start(s32[16]{0:T(128)} %num_ref.1) | copy-start | bytes 196
  41.1 2.1 %collective-permute-start.8 = (bf16[64,640]{1,0:T(8,128)(2,1)S(1)}, bf16[64,640]{1,0:T(8,128)(2,1)S(1)}, u32[]{:S(2)}, u32[]{:S(2)}) collective-permute-start(bf16[64,640]{1,0:T(8,128)(2,1)S(1)} %get-tuple-element.20), channel_id=1, source_target_pairs={{0,1},{1,0},{2,3},{3,2},{4,5},{5,4},{6,7},{7,6},{8,9},{9,8},{10,11... | collective-permute-start | bytes 245768 | tf_op jit(solution)/shard_map/ppermute | solution.py:31
  41.2 3.5 %collective-permute-start.6 = (bf16[64,640]{1,0:T(8,128)(2,1)S(1)}, bf16[64,640]{1,0:T(8,128)(2,1)S(1)}, u32[]{:S(2)}, u32[]{:S(2)}) collective-permute-start(bf16[64,640]{1,0:T(8,128)(2,1)S(1)} %get-tuple-element.18), channel_id=1, source_target_pairs={{0,1},{1,0},{2,3},{3,2},{4,5},{5,4},{6,7},{7,6},{8,9},{9,8},{10,11... | collective-permute-start | bytes 245768 | tf_op jit(solution)/shard_map/ppermute | solution.py:31
  41.7 5.1 %collective-permute-start.7 = (bf16[64,640]{1,0:T(8,128)(2,1)S(1)}, bf16[64,640]{1,0:T(8,128)(2,1)S(1)}, u32[]{:S(2)}, u32[]{:S(2)}) collective-permute-start(bf16[64,640]{1,0:T(8,128)(2,1)S(1)} %get-tuple-element.19), channel_id=1, source_target_pairs={{0,2},{1,3},{2,0},{3,1},{4,6},{5,7},{6,4},{7,5},{8,10},{9,11},{10,... | collective-permute-start | bytes 245768 | tf_op jit(solution)/shard_map/ppermute | solution.py:31
  43.2 4.7 %collective-permute-start.9 = (bf16[64,640]{1,0:T(8,128)(2,1)S(1)}, bf16[64,640]{1,0:T(8,128)(2,1)S(1)}, u32[]{:S(2)}, u32[]{:S(2)}) collective-permute-start(bf16[64,640]{1,0:T(8,128)(2,1)S(1)} %collective-permute-done.8), channel_id=1, source_target_pairs={{0,2},{1,3},{2,0},{3,1},{4,6},{5,7},{6,4},{7,5},{8,10},{9,11},{10,... | collective-permute-start | bytes 245768 | tf_op jit(solution)/shard_map/ppermute | solution.py:31
  47.9 1.6 %copy-start.1 = (bf16[3,3,320,320]{3,2,1,0:T(8,128)(2,1)S(1)}, bf16[3,3,320,320]{3,2,1,0:T(8,128)(2,1)}, u32[]{:S(2)}) copy-start(bf16[3,3,320,320]{3,2,1,0:T(8,128)(2,1)} %param.16) | copy-start | bytes 5529604
  49.5 1.0 %copy-start.2 = (bf16[4,2,64,320]{3,2,1,0:T(8,128)(2,1)S(1)}, bf16[4,2,64,320]{3,2,1,0:T(8,128)(2,1)}, u32[]{:S(2)}) copy-start(bf16[4,2,64,320]{3,2,1,0:T(8,128)(2,1)} %lat_ref.1) | copy-start | bytes 983044
  50.5 0.9 %copy-start.4 = (bf16[320,320]{1,0:T(8,128)(2,1)S(1)}, bf16[320,320]{1,0:T(8,128)(2,1)}, u32[]{:S(2)}) copy-start(bf16[320,320]{1,0:T(8,128)(2,1)} %w_out_ref.1) | copy-start | bytes 614404
  51.5 0.7 %copy-start.6 = (f32[2,320]{1,0:T(2,128)S(1)}, f32[2,320]{1,0:T(2,128)}, u32[]{:S(2)}) copy-start(f32[2,320]{1,0:T(2,128)} %gn_ref.1) | copy-start | bytes 7684

commit v3 on v2

--- a/solution.py
+++ b/solution.py
@@ -14,7 +14,7 @@
 REACH = WINDOW // BLOCK
 EPS = 1e-05
 LANES = 128
-GROUP = 4
+GROUP = 2
 LOG2E = 1.4426950408889634
 NT = (((1,), (1,)), ((), ()))
 QUARTERS = 4
@@ -31,56 +31,95 @@
     return lax.ppermute(array, "frame", [(i, target(i) % count) for i in range(count)])
 
 
-def pack_kernel(lat_ref, mine_ref, theirs_ref):
+def pack_lanes(first, second):
+    low = lax.broadcasted_iota(jnp.int32, first[-1].shape, first[-1].ndim - 1) < LANES // 2
+    tail = jnp.where(low, first[-1], pltpu.roll(second[-1], LANES // 2, second[-1].ndim - 1))
+    return jnp.concatenate(first[:-1] + second[:-1] + [tail], -1)
+
+
+def unpack_lanes(rows):
+    chunks = [rows[:, i : i + LANES] for i in range(0, rows.shape[1], LANES)]
+    full = len(chunks) // 2
+    low = lax.broadcasted_iota(jnp.int32, chunks[-1].shape, 1) < LANES // 2
+    first = chunks[:full] + [jnp.where(low, chunks[-1], 0.0)]
+    second = chunks[full:-1] + [jnp.where(low, pltpu.roll(chunks[-1], LANES // 2, 1), 0.0)]
+    return first, second
+
+
+def fetch(pairs, sem):
+    copies = [pltpu.make_async_copy(src, dst, sem.at[i]) for i, (src, dst) in enumerate(pairs)]
+    for copy in copies:
+        copy.start()
+    return copies
+
+
+def pack_kernel(lat_ref, near_ref, far_ref):
     core, chip, _ = place()
     frames, _, cells, channels = lat_ref.shape
     half = cells // PACK
-    for out_ref, side in ((mine_ref, core), (theirs_ref, 1 - core)):
-        for i, tall in enumerate((chip, 1 - chip)):
-            x = lat_ref[:, side * 2 + tall]
-            x = jnp.concatenate([x[:, :half], x[:, half:]], -1)
-            out_ref[i] = x.reshape(frames * half, PACK * channels)
-
-
-def join_kernel(mine_ref, other_ref, near_ref, far_ref):
-    rows = mine_ref.shape[1]
-    for i, out_ref in enumerate((near_ref, far_ref)):
-        out_ref[:rows] = mine_ref[i]
-        out_ref[rows:] = other_ref[i]
-
-
-def attend_kernel(
-    cells, planes, off_ref, num_ref, *refs
-):
-    parts = refs[:6]
-    gain_ref, w_ref, own_ref, sib_ref, far_own_ref, far_sib_ref = refs[6:12]
-    norm_ref, q_ref, k_ref, v_ref, bias_ref, coef_ref, acc_ref = refs[12:]
+    width = -(-channels // LANES) * LANES
+    for out_ref, tall in ((near_ref, chip), (far_ref, 1 - chip)):
+        for i, side in enumerate((core, 1 - core)):
+            x = lat_ref[:, side * 2 + tall].astype(jnp.float32)
+            x = jnp.concatenate([x, jnp.zeros((frames, cells, width - channels), x.dtype)], -1)
+            halves = []
+            for a in range(PACK):
+                rows = x[:, a * half : (a + 1) * half].reshape(frames * half, width)
+                halves.append([rows[:, j : j + LANES] for j in range(0, width, LANES)])
+            out_ref[i] = pack_lanes(*halves).astype(out_ref.dtype)
+
+
+def attend_kernel(cells, planes, *refs):
+    sources, refs = refs[:12], refs[12:]
+    off_hbm, num_hbm, gain_hbm, w_hbm, own_ref, sib_ref, far_own_ref, far_sib_ref = refs[:8]
+    (
+        off_ref, num_ref, gain_ref, w_ref, part_ref, norm_ref, q_ref, k_ref, v_ref, bias_ref, coef_ref, acc_ref, sem,
+    ) = refs[8:]
     core, chip, plane = place()
     channels = w_ref.shape[0]
     head_dim = channels // HEADS
     half = cells // PACK
-    part_rows = parts[0].shape[0]
+    part_rows = part_ref.shape[1]
     part_frames = part_rows // half
-    key_frames, query_frames = part_frames * 6, part_frames * 2
+    key_frames, query_frames = part_frames * 12, part_frames * 4
     key_rows, query_rows = key_frames * half, query_frames * half
     blocks = planes * QUARTERS
     frames = blocks * BLOCK
     group = GROUP
     wide = group * HEADS * query_frames
     chunks, lanes = k_ref.shape[0], k_ref.shape[2]
-
-    for b, part in enumerate(parts):
-        for a in range(PACK):
-            x = part[:, a * channels : (a + 1) * channels].astype(jnp.float32)
-            cen = x - jnp.mean(x, axis=-1, keepdims=True)
-            var = jnp.mean(cen * cen, axis=-1, keepdims=True)
-            start = a * key_rows + b * part_rows
-            norm_ref[start : start + part_rows] = (
-                cen * lax.rsqrt(var + EPS) * gain_ref[...]
-            ).astype(jnp.bfloat16)
+    copies = fetch(
+        [(gain_hbm, gain_ref)]
+        + [(src.at[i % 2], part_ref.at[i]) for i, src in enumerate(sources)]
+        + [(w_hbm, w_ref), (off_hbm, off_ref), (num_hbm, num_ref)],
+        sem,
+    )
+
+    copies[0].wait()
+    gain = gain_ref[...]
+    pad = jnp.zeros((1, chunks * lanes - channels), jnp.float32)
+    gain = jnp.concatenate([gain, pad], 1)
+    last = lax.broadcasted_iota(jnp.int32, (part_rows, lanes), 1) < channels - (chunks - 1) * lanes
+    for i in range(len(sources)):
+        copies[1 + i].wait()
+        for a, x in enumerate(unpack_lanes(part_ref[i].astype(jnp.float32))):
+            average = jnp.sum(sum(x), axis=-1, keepdims=True) * (1.0 / channels)
+            cen = [chunk - average for chunk in x]
+            cen[-1] = jnp.where(last, cen[-1], 0.0)
+            var = jnp.sum(sum(chunk * chunk for chunk in cen), axis=-1, keepdims=True)
+            scale = lax.rsqrt(var * (1.0 / channels) + EPS)
+            start = a * key_rows + i * part_rows
+            normed = [
+                chunk * scale * gain[:, j * lanes : (j + 1) * lanes] for j, chunk in enumerate(cen)
+            ]
+            norm_ref[start : start + part_rows] = jnp.concatenate(normed, 1).astype(jnp.bfloat16)
+    for copy in copies[1 + len(sources) :]:
+        copy.wait()
     pad = jnp.zeros((channels, chunks * lanes - channels), jnp.bfloat16)
+    below = jnp.zeros((chunks * lanes - channels, chunks * lanes), jnp.bfloat16)
     for i, (out_ref, rows) in enumerate(((q_ref, query_rows), (k_ref, key_rows), (v_ref, key_rows))):
         w = jnp.concatenate([w_ref[:, i * channels : (i + 1) * channels], pad], 1)
+        w = jnp.concatenate([w, below], 0)
         for a in range(PACK):
             here = norm_ref[a * key_rows : a * key_rows + rows]
             res = jnp.dot(here, w, preferred_element_type=jnp.float32)
@@ -171,37 +210,41 @@
         pieces = []
         for a in range(PACK):
             start = a * query_rows + i * quarter
-            piece = jnp.concatenate([acc_ref[j, start : start + quarter] for j in range(chunks)], 1)
-            pieces.append(piece[:, :channels])
-        out_ref[...] = jnp.concatenate(pieces, 1).astype(out_ref.dtype)
+            pieces.append([acc_ref[j, start : start + quarter] for j in range(chunks)])
+        out_ref[...] = pack_lanes(*pieces).astype(out_ref.dtype)
 
 
 def attend(parts, norm_gain, w_qkv, offsets, numerators, cells, planes):
     channels = w_qkv.shape[0]
     vmem = pl.BlockSpec(memory_space=pltpu.VMEM)
-    smem = pl.BlockSpec(memory_space=pltpu.SMEM)
-    rows, packed = parts[0].shape
+    _, rows, packed = parts[0].shape
     chunks = -(-channels // LANES)
-    query_frames = 2 * rows * PACK // cells
+    query_frames = 4 * rows * PACK // cells
     wide = GROUP * HEADS * query_frames
-    keys, queries = 6 * rows * PACK, 2 * rows * PACK
+    keys, queries = 12 * rows * PACK, 4 * rows * PACK
     return pl.pallas_call(
         functools.partial(attend_kernel, cells, planes),
-        out_shape=[jax.ShapeDtypeStruct((rows // 2, packed), jnp.bfloat16)] * 4,
-        in_specs=[smem, smem] + [vmem] * 8,
+        out_shape=[jax.ShapeDtypeStruct((rows, packed), jnp.bfloat16)] * 4,
+        in_specs=[pl.BlockSpec(memory_space=pl.ANY)] * 16,
         out_specs=[vmem] * 4,
         scratch_shapes=[
-            pltpu.VMEM((keys, channels), jnp.bfloat16),
+            pltpu.SMEM(offsets.shape, jnp.int32),
+            pltpu.SMEM(numerators.shape, jnp.int32),
+            pltpu.VMEM((1, channels), jnp.float32),
+            pltpu.VMEM(w_qkv.shape, jnp.bfloat16),
+            pltpu.VMEM((12, rows, packed), jnp.bfloat16),
+            pltpu.VMEM((keys, chunks * LANES), jnp.bfloat16),
             pltpu.VMEM((chunks, queries, LANES), jnp.float32),
             pltpu.VMEM((chunks, keys, LANES), jnp.float32),
             pltpu.VMEM((chunks, keys, LANES), jnp.float32),
             pltpu.VMEM((REACH + 1, 3 * query_frames, wide), jnp.float32),
             pltpu.VMEM((REACH + 1, 1, wide), jnp.float32),
             pltpu.VMEM((chunks, queries, LANES), jnp.float32),
+            pltpu.SemaphoreType.DMA((16,)),
         ],
-        compiler_params=pltpu.CompilerParams(vmem_limit_bytes=24 * 1024 * 1024),
+        compiler_params=pltpu.CompilerParams(vmem_limit_bytes=60 * 1024 * 1024),
         name="window_attention",
-    )(offsets, numerators, *parts, norm_gain.reshape(1, channels), w_qkv)
+    )(*parts, offsets, numerators, norm_gain.reshape(1, channels), w_qkv)
 
 
 def group_mean(sums, spread, count):
@@ -249,17 +292,16 @@
     return outs
 
 
-def res_kernel(
-    p0_ref, p1_ref, p2_ref, p3_ref, lat_ref, w_out_ref, gn_ref, step_ref, one_hbm, two_hbm, out_ref,
-    comb_ref, one_ref, two_ref, taps_ref, sem
-):
+def res_kernel(*refs):
+    sources, out_ref = refs[:10], refs[10]
+    (
+        part_ref, lat_ref, w_out_ref, gn_ref, step_ref, one_ref, two_ref, comb_ref, taps_ref, sem,
+    ) = refs[11:]
     frames, count, cols, channels = lat_ref.shape
     deep = one_ref.shape[1]
-    copies = []
-    for i, (src, dst) in enumerate(((one_hbm, one_ref), (two_hbm, two_ref))):
-        copy = pltpu.make_async_copy(src, dst.at[:, :channels, :], sem.at[i])
-        copy.start()
-        copies.append(copy)
+    targets = [part_ref.at[i] for i in range(4)] + [w_out_ref, lat_ref, gn_ref, step_ref]
+    targets += [ref.at[:, :channels, :] for ref in (one_ref, two_ref)]
+    copies = fetch(list(zip(sources, targets)), sem)
     for ref in (one_ref, two_ref):
         ref[:, channels:, :] = jnp.zeros((ref.shape[0], deep - channels, channels), jnp.bfloat16)
     for i in range(3 * count):
@@ -274,12 +316,17 @@
 
     core, chip, _ = place()
     half = comb_ref.shape[2] // PACK
-    for part, side, tall in (
-        (p0_ref, core, chip), (p1_ref, 1 - core, chip), (p2_ref, core, 1 - chip), (p3_ref, 1 - core, 1 - chip)
+    for i, (side, tall) in enumerate(
+        ((core, chip), (1 - core, chip), (core, 1 - chip), (1 - core, 1 - chip))
     ):
-        for a in range(PACK):
-            piece = part[:, a * channels : (a + 1) * channels].reshape(frames, half, channels)
-            comb_ref[:, side * 2 + tall, a * half : (a + 1) * half, :] = piece
+        copies[i].wait()
+        for a, piece in enumerate(unpack_lanes(part_ref[i].astype(jnp.float32))):
+            piece = jnp.concatenate(piece, 1)[:, :channels].astype(jnp.bfloat16)
+            comb_ref[:, side * 2 + tall, a * half : (a + 1) * half, :] = piece.reshape(
+                frames, half, channels
+            )
+    for copy in copies[4:8]:
+        copy.wait()
     combined = comb_ref[...].reshape(frames, count * cols, channels)
     hidden = []
     for r in range(count):
@@ -288,10 +335,10 @@
         hid = lat_ref[:, r].astype(jnp.float32) + proj.reshape(frames, cols, channels)
         hidden.append(hid.astype(jnp.bfloat16).astype(jnp.float32))
     acts = group_act(hidden, gn_ref[0:1], spread, members)
-    copies[0].wait()
+    copies[8].wait()
     middle = [row + step_ref[...][None] for row in conv_rows(acts, one_ref, taps_ref)]
     acts = group_act(middle, gn_ref[1:2], spread, members)
-    copies[1].wait()
+    copies[9].wait()
     for r, row in enumerate(conv_rows(acts, two_ref, taps_ref)):
         out_ref[:, r] = (hidden[r] + row).astype(out_ref.dtype)
 
@@ -300,25 +347,29 @@
     frames, count, cols, channels = latents.shape
     deep = -(-channels // 128) * 128
     vmem = pl.BlockSpec(memory_space=pltpu.VMEM)
-    hbm = pl.BlockSpec(memory_space=pltpu.HBM)
     return pl.pallas_call(
         res_kernel,
         out_shape=jax.ShapeDtypeStruct(latents.shape, jnp.bfloat16),
-        in_specs=[vmem] * 8 + [hbm] * 2,
+        in_specs=[pl.BlockSpec(memory_space=pl.ANY)] * 10,
         out_specs=vmem,
         scratch_shapes=[
-            pltpu.VMEM((frames, QUARTERS, count * cols // QUARTERS, channels), jnp.bfloat16),
+            pltpu.VMEM((4,) + parts[0].shape, jnp.bfloat16),
+            pltpu.VMEM(latents.shape, jnp.bfloat16),
+            pltpu.VMEM(w_out.shape, jnp.bfloat16),
+            pltpu.VMEM(gn_gain.shape, jnp.float32),
+            pltpu.VMEM((1, channels), jnp.float32),
             pltpu.VMEM((9, deep, channels), jnp.bfloat16),
             pltpu.VMEM((9, deep, channels), jnp.bfloat16),
+            pltpu.VMEM((frames, QUARTERS, count * cols // QUARTERS, channels), jnp.bfloat16),
             pltpu.VMEM((frames * cols, 3 * count * deep), jnp.bfloat16),
-            pltpu.SemaphoreType.DMA((2,)),
+            pltpu.SemaphoreType.DMA((10,)),
         ],
-        compiler_params=pltpu.CompilerParams(vmem_limit_bytes=24 * 1024 * 1024),
+        compiler_params=pltpu.CompilerParams(vmem_limit_bytes=60 * 1024 * 1024),
         name="res_block",
     )(
         *parts,
+        w_out,
         latents,
-        w_out,
         gn_gain,
         step_embed.reshape(1, channels),
         conv_one.reshape(9, channels, channels),
@@ -334,22 +385,14 @@
     cells = tile_rows * tile_cols // QUARTERS
     vmem = pl.BlockSpec(memory_space=pltpu.VMEM)
     rows, packed = block_len * cells // PACK, PACK * channels
-    mine, theirs = pl.pallas_call(
+    near, far = pl.pallas_call(
         pack_kernel,
         out_shape=[jax.ShapeDtypeStruct((2, rows, packed), jnp.bfloat16)] * 2,
         in_specs=[vmem],
         out_specs=[vmem] * 2,
         name="pack",
     )(latents.reshape(block_len, QUARTERS, cells, channels))
-    other = moved(theirs, lambda i: i ^ 1)
-    near, far = pl.pallas_call(
-        join_kernel,
-        out_shape=[jax.ShapeDtypeStruct((2 * rows, packed), jnp.bfloat16)] * 2,
-        in_specs=[vmem] * 2,
-        out_specs=[vmem] * 2,
-        name="join",
-    )(mine, other)
-    parts = [
+    landed = [
         near,
         moved(far, lambda i: i ^ 2),
         moved(near, lambda i: i + QUARTERS),
@@ -357,6 +400,9 @@
         moved(near, lambda i: i - QUARTERS),
         moved(far, lambda i: (i ^ 2) - QUARTERS),
     ]
+    parts = []
+    for piece in landed:
+        parts += [piece, moved(piece, lambda i: i ^ 1)]
     own, sib, far_own, far_sib = attend(
         parts, norm_gain, w_qkv, offsets, numerators, cells, planes
     )

time: 59 us -> 51.4 us (0.87)
  local copies, waits for them, and re-layouts: 9.59 us -> 3.93 us
  Pallas kernels: 20.4 us -> 19.3 us
    unnamed x20 -> x30, local copies, waits for them, and re-layouts: 8.22 us -> 2.07 us
    pallas_call x1 -> x0, Pallas kernels: 1.73 us -> none  [body(): pl.pallas_call(join_kernel, out_shape=[jax.ShapeDtypeStruct((2 * rows, pa...]
    pallas_call x1, Pallas kernels: 6.3 us -> 7.11 us  [res_block(): pl.pallas_call(res_kernel, out_shape=jax.ShapeDtypeStruct(latents.shape,...]
    ppermute x10 -> x15, starting transfers between devices: 12.9 us -> 12.6 us  [moved(): lax.ppermute(array, 'frame', [(i, target(i) % count) for i in range(count)])]
    ppermute x10 -> x15, waiting for transfers between devices: 15.5 us -> 15.2 us  [moved(): lax.ppermute(array, 'frame', [(i, target(i) % count) for i in range(count)])]
  transfers between devices with their start and end apart: 10 -> 15, of which waited for: 7 -> 8; matrix products, arithmetic and copies ran while one was open for 2% -> 4% of each run, Pallas kernels for 0% -> 0%
where the time goes in v3:
time: 51.4 us; the launch traced here: 51.2 us
  Pallas kernels  19.3 us (38%)
  waiting for transfers between devices  15.2 us (30%)
  starting transfers between devices  12.6 us (25%)
  local copies, waits for them, and re-layouts  3.93 us (8%)
    ppermute x15, waiting for transfers between devices, moved(): lax.ppermute(array, 'frame', [(i, target(i) % count) for i in range(count)])  15.2 us
    ppermute x15, starting transfers between devices, moved(): lax.ppermute(array, 'frame', [(i, target(i) % count) for i in range(count)])  12.6 us
    pallas_call x1, Pallas kernels, attend(): pl.pallas_call(functools.partial(attend_kernel, cells, planes), out_shape...  10.4 us
    pallas_call x1, Pallas kernels, res_block(): pl.pallas_call(res_kernel, out_shape=jax.ShapeDtypeStruct(latents.shape,...  7.11 us
    unnamed x30, local copies, waits for them, and re-layouts  2.07 us
    pallas_call x1, Pallas kernels, body(): pl.pallas_call(pack_kernel, out_shape=[jax.ShapeDtypeStruct((2, rows, pac...  1.81 us
    reshape x1, local copies, waits for them, and re-layouts, attend(): norm_gain.reshape(1, channels)  1.27 us
  transfers between devices with their start and end apart: 15, of which 8 were waited for; matrix products, arithmetic and copies ran while one was open for 4% of the time, Pallas kernels for 0%

profile of v3, /device:TPU:0, one launch (start us, length us, event | category | flops | bytes accessed | tf_op | source)
XLA Modules:
  0.0 51.2 jit_solution(2766828961298812760)
XLA Ops:
  0.0 1.8 %pack.1 = (bf16[2,64,640]{2,1,0:T(8,128)(2,1)}, bf16[2,64,640]{2,1,0:T(8,128)(2,1)}) custom-call(bf16[4,4,32,320]{3,2,1,0:T(8,128)(2,1)} %bitcast.5), custom_call_target="tpu_custom_call" | custom-call | tf_op jit(solution)/shard_map/pack/pallas_call | solution.py:388
  1.8 3.0 %collective-permute-start.3 = (bf16[2,64,640]{2,1,0:T(8,128)(2,1)}, bf16[2,64,640]{2,1,0:T(8,128)(2,1)S(1)}, u32[]{:S(2)}, u32[]{:S(2)}) collective-permute-start(bf16[2,64,640]{2,1,0:T(8,128)(2,1)} %get-tuple-element.11.refs_0_), channel_id=1, source_target_pairs={{0,4},{1,5},{2,6},{3,7},{4,8},{5,9},{6,10},{7,11},{8,12},{9,13},{1... | collective-permute-start | bytes 491528 | tf_op jit(solution)/shard_map/ppermute | solution.py:31
  4.8 2.0 %collective-permute-start.7 = (bf16[2,64,640]{2,1,0:T(8,128)(2,1)}, bf16[2,64,640]{2,1,0:T(8,128)(2,1)S(1)}, u32[]{:S(2)}, u32[]{:S(2)}) collective-permute-start(bf16[2,64,640]{2,1,0:T(8,128)(2,1)} %get-tuple-element.11.refs_0_), channel_id=1, source_target_pairs={{0,12},{1,13},{2,14},{3,15},{4,0},{5,1},{6,2},{7,3},{8,4},{9,5},{1... | collective-permute-start | bytes 491528 | tf_op jit(solution)/shard_map/ppermute | solution.py:31
  6.9 3.0 %collective-permute-start.9 = (bf16[2,64,640]{2,1,0:T(8,128)(2,1)}, bf16[2,64,640]{2,1,0:T(8,128)(2,1)S(1)}, u32[]{:S(2)}, u32[]{:S(2)}) collective-permute-start(bf16[2,64,640]{2,1,0:T(8,128)(2,1)} %get-tuple-element.12), channel_id=1, source_target_pairs={{0,14},{1,15},{2,12},{3,13},{4,2},{5,3},{6,0},{7,1},{8,6},{9,7},{1... | collective-permute-start | bytes 491528 | tf_op jit(solution)/shard_map/ppermute | solution.py:31
  9.8 0.5 collective-permute-start.1
  10.4 1.2 %collective-permute-start.5 = (bf16[2,64,640]{2,1,0:T(8,128)(2,1)}, bf16[2,64,640]{2,1,0:T(8,128)(2,1)S(1)}, u32[]{:S(2)}, u32[]{:S(2)}) collective-permute-start(bf16[2,64,640]{2,1,0:T(8,128)(2,1)} %get-tuple-element.12), channel_id=1, source_target_pairs={{0,6},{1,7},{2,4},{3,5},{4,10},{5,11},{6,8},{7,9},{8,14},{9,15},{1... | collective-permute-start | bytes 491528 | tf_op jit(solution)/shard_map/ppermute | solution.py:31
  11.5 0.6 %collective-permute-done.3.refs_4_ = bf16[2,64,640]{2,1,0:T(8,128)(2,1)S(1)} collective-permute-done((bf16[2,64,640]{2,1,0:T(8,128)(2,1)}, bf16[2,64,640]{2,1,0:T(8,128)(2,1)S(1)}, u32[]{:S(2)}, u32[]{:S(2)}) %collective-permute-start.3) | collective-permute-done | bytes 163872 | tf_op jit(solution)/shard_map/ppermute | solution.py:31
  12.2 2.8 %collective-permute-done.7.refs_8_ = bf16[2,64,640]{2,1,0:T(8,128)(2,1)S(1)} collective-permute-done((bf16[2,64,640]{2,1,0:T(8,128)(2,1)}, bf16[2,64,640]{2,1,0:T(8,128)(2,1)S(1)}, u32[]{:S(2)}, u32[]{:S(2)}) %collective-permute-start.7) | collective-permute-done | bytes 163872 | tf_op jit(solution)/shard_map/ppermute | solution.py:31
  14.9 4.4 %collective-permute-done.9.refs_10_ = bf16[2,64,640]{2,1,0:T(8,128)(2,1)S(1)} collective-permute-done((bf16[2,64,640]{2,1,0:T(8,128)(2,1)}, bf16[2,64,640]{2,1,0:T(8,128)(2,1)S(1)}, u32[]{:S(2)}, u32[]{:S(2)}) %collective-permute-start.9) | collective-permute-done | bytes 163872 | tf_op jit(solution)/shard_map/ppermute | solution.py:31
  19.8 3.0 %collective-permute-done.5.refs_6_ = bf16[2,64,640]{2,1,0:T(8,128)(2,1)S(1)} collective-permute-done((bf16[2,64,640]{2,1,0:T(8,128)(2,1)}, bf16[2,64,640]{2,1,0:T(8,128)(2,1)S(1)}, u32[]{:S(2)}, u32[]{:S(2)}) %collective-permute-start.5) | collective-permute-done | bytes 163872 | tf_op jit(solution)/shard_map/ppermute | solution.py:31
  22.8 0.5 collective-permute-start.6
  23.3 1.3 %reshape.16.refs_14_ = f32[1,320]{1,0:T(1,128)} reshape(f32[320]{0:T(512)} %param.11) | data formatting | bytes 2560 | tf_op jit(solution)/shard_map/reshape | solution.py:247
  24.7 0.5 %copy-done.6 = bf16[2,64,640]{2,1,0:T(8,128)(2,1)} copy-done((bf16[2,64,640]{2,1,0:T(8,128)(2,1)}, bf16[2,64,640]{2,1,0:T(8,128)(2,1)S(1)}, u32[]{:S(2)}) %copy-start.6) | copy-done | bytes 163864
  25.5 0.7 %copy-done.10 = bf16[2,64,640]{2,1,0:T(8,128)(2,1)} copy-done((bf16[2,64,640]{2,1,0:T(8,128)(2,1)}, bf16[2,64,640]{2,1,0:T(8,128)(2,1)S(1)}, u32[]{:S(2)}) %copy-start.10) | copy-done | bytes 163864
  26.1 10.4 %window_attention.1 = (bf16[64,640]{1,0:T(8,128)(2,1)}, bf16[64,640]{1,0:T(8,128)(2,1)}, bf16[64,640]{1,0:T(8,128)(2,1)}, bf16[64,640]{1,0:T(8,128)(2,1)}) custom-call(bf16[2,64,640]{2,1,0:T(8,128)(2,1)} %get-tuple-element.11.refs_0_, bf16[2,64,640]{2,1,0:T(8,128)(2,1)} %copy-done.5, bf16[2,64,640]{2,1,0:T(8,128)(2,1)} %copy-done.3, ...), custom_call_target="tpu_custom_call" | custom-call | tf_op jit(solution)/shard_map/window_attention/pallas_call | solution.py:225
  36.7 0.4 collective-permute-start.11
  37.1 0.5 collective-permute-start.12
  37.6 0.5 collective-permute-done.13
  38.1 1.1 %collective-permute-start.14 = (bf16[64,640]{1,0:T(8,128)(2,1)S(1)}, bf16[64,640]{1,0:T(8,128)(2,1)S(1)}, u32[]{:S(2)}, u32[]{:S(2)}) collective-permute-start(bf16[64,640]{1,0:T(8,128)(2,1)S(1)} %collective-permute-done.13), channel_id=1, source_target_pairs={{0,2},{1,3},{2,0},{3,1},{4,6},{5,7},{6,4},{7,5},{8,10},{9,11},{10,... | collective-permute-start | bytes 245768 | tf_op jit(solution)/shard_map/ppermute | solution.py:31
  39.1 0.6 %reshape.17.refs_7_ = f32[1,320]{1,0:T(1,128)} reshape(f32[320]{0:T(512)S(1)} %copy-done.14) | data formatting | bytes 2560 | tf_op jit(solution)/shard_map/reshape | solution.py:374
  39.7 2.9 %collective-permute-done.12.refs_2_ = bf16[64,640]{1,0:T(8,128)(2,1)S(1)} collective-permute-done((bf16[64,640]{1,0:T(8,128)(2,1)}, bf16[64,640]{1,0:T(8,128)(2,1)S(1)}, u32[]{:S(2)}, u32[]{:S(2)}) %collective-permute-start.12) | collective-permute-done | bytes 81952 | tf_op jit(solution)/shard_map/ppermute | solution.py:31
  42.6 0.9 %collective-permute-done.14.refs_3_ = bf16[64,640]{1,0:T(8,128)(2,1)S(1)} collective-permute-done((bf16[64,640]{1,0:T(8,128)(2,1)S(1)}, bf16[64,640]{1,0:T(8,128)(2,1)S(1)}, u32[]{:S(2)}, u32[]{:S(2)}) %collective-permute-start.14) | collective-permute-done | bytes 81952 | tf_op jit(solution)/shard_map/ppermute | solution.py:31
  43.5 0.6 %copy-done.13 = bf16[64,640]{1,0:T(8,128)(2,1)} copy-done((bf16[64,640]{1,0:T(8,128)(2,1)}, bf16[64,640]{1,0:T(8,128)(2,1)S(1)}, u32[]{:S(2)}) %copy-start.13) | copy-done | bytes 81944
  44.1 7.1 %res_block.1 = bf16[4,2,64,320]{3,2,1,0:T(8,128)(2,1)} custom-call(bf16[64,640]{1,0:T(8,128)(2,1)} %get-tuple-element.13.refs_0_, bf16[64,640]{1,0:T(8,128)(2,1)} %copy-done.11, bf16[64,640]{1,0:T(8,128)(2,1)} %copy-done.12, bf16[64,640]{1,0:T(8,128)(2,1)} %copy-done.13, bf16[320,320]{1,0:T(8,128)(2,1)} %refs_4_.1, bf16[4,2,64,320]{3,2,1,0:T(8,128)(2,1)} %refs_5_.1, ...), custom_call_target="tpu_custom_call" | custom-call | tf_op jit(solution)/shard_map/res_block/pallas_call | solution.py:350
  (41 shorter events, 1.0 us)
Async XLA Ops:
  0.0 39.1 %copy-start.14 = (f32[320]{0:T(512)S(1)}, f32[320]{0:T(512)}, u32[]{:S(2)}) copy-start(f32[320]{0:T(512)} %param.17) | copy-start | bytes 3844
  1.8 10.3 %collective-permute-start.3 = (bf16[2,64,640]{2,1,0:T(8,128)(2,1)}, bf16[2,64,640]{2,1,0:T(8,128)(2,1)S(1)}, u32[]{:S(2)}, u32[]{:S(2)}) collective-permute-start(bf16[2,64,640]{2,1,0:T(8,128)(2,1)} %get-tuple-element.11.refs_0_), channel_id=1, source_target_pairs={{0,4},{1,5},{2,6},{3,7},{4,8},{5,9},{6,10},{7,11},{8,12},{9,13},{1... | collective-permute-start | bytes 491528 | tf_op jit(solution)/shard_map/ppermute | solution.py:31
  4.8 10.1 %collective-permute-start.7 = (bf16[2,64,640]{2,1,0:T(8,128)(2,1)}, bf16[2,64,640]{2,1,0:T(8,128)(2,1)S(1)}, u32[]{:S(2)}, u32[]{:S(2)}) collective-permute-start(bf16[2,64,640]{2,1,0:T(8,128)(2,1)} %get-tuple-element.11.refs_0_), channel_id=1, source_target_pairs={{0,12},{1,13},{2,14},{3,15},{4,0},{5,1},{6,2},{7,3},{8,4},{9,5},{1... | collective-permute-start | bytes 491528 | tf_op jit(solution)/shard_map/ppermute | solution.py:31
  6.9 12.4 %collective-permute-start.9 = (bf16[2,64,640]{2,1,0:T(8,128)(2,1)}, bf16[2,64,640]{2,1,0:T(8,128)(2,1)S(1)}, u32[]{:S(2)}, u32[]{:S(2)}) collective-permute-start(bf16[2,64,640]{2,1,0:T(8,128)(2,1)} %get-tuple-element.12), channel_id=1, source_target_pairs={{0,14},{1,15},{2,12},{3,13},{4,2},{5,3},{6,0},{7,1},{8,6},{9,7},{1... | collective-permute-start | bytes 491528 | tf_op jit(solution)/shard_map/ppermute | solution.py:31
  9.8 9.7 %collective-permute-start.1 = (bf16[2,64,640]{2,1,0:T(8,128)(2,1)}, bf16[2,64,640]{2,1,0:T(8,128)(2,1)S(1)}, u32[]{:S(2)}, u32[]{:S(2)}) collective-permute-start(bf16[2,64,640]{2,1,0:T(8,128)(2,1)} %get-tuple-element.12), channel_id=1, source_target_pairs={{0,2},{1,3},{2,0},{3,1},{4,6},{5,7},{6,4},{7,5},{8,10},{9,11},{10,... | collective-permute-start | bytes 491528 | tf_op jit(solution)/shard_map/ppermute | solution.py:31
  10.4 12.4 %collective-permute-start.5 = (bf16[2,64,640]{2,1,0:T(8,128)(2,1)}, bf16[2,64,640]{2,1,0:T(8,128)(2,1)S(1)}, u32[]{:S(2)}, u32[]{:S(2)}) collective-permute-start(bf16[2,64,640]{2,1,0:T(8,128)(2,1)} %get-tuple-element.12), channel_id=1, source_target_pairs={{0,6},{1,7},{2,4},{3,5},{4,10},{5,11},{6,8},{7,9},{8,14},{9,15},{1... | collective-permute-start | bytes 491528 | tf_op jit(solution)/shard_map/ppermute | solution.py:31
  12.1 12.5 %copy-start = (bf16[2,64,640]{2,1,0:T(8,128)(2,1)}, bf16[2,64,640]{2,1,0:T(8,128)(2,1)S(1)}, u32[]{:S(2)}) copy-start(bf16[2,64,640]{2,1,0:T(8,128)(2,1)S(1)} %collective-permute-done.3.refs_4_) | copy-start | bytes 491524
  12.2 10.7 %collective-permute-start = (bf16[2,64,640]{2,1,0:T(8,128)(2,1)}, bf16[2,64,640]{2,1,0:T(8,128)(2,1)S(1)}, u32[]{:S(2)}, u32[]{:S(2)}) collective-permute-start(bf16[2,64,640]{2,1,0:T(8,128)(2,1)} %get-tuple-element.11.refs_0_), channel_id=1, source_target_pairs={{0,1},{1,0},{2,3},{3,2},{4,5},{5,4},{6,7},{7,6},{8,9},{9,8},{10,11... | collective-permute-start | bytes 491528 | tf_op jit(solution)/shard_map/ppermute | solution.py:31
  14.9 9.7 %copy-start.1 = (bf16[2,64,640]{2,1,0:T(8,128)(2,1)}, bf16[2,64,640]{2,1,0:T(8,128)(2,1)S(1)}, u32[]{:S(2)}) copy-start(bf16[2,64,640]{2,1,0:T(8,128)(2,1)S(1)} %collective-permute-done.7.refs_8_) | copy-start | bytes 491524
  14.9 9.7 %collective-permute-start.4 = (bf16[2,64,640]{2,1,0:T(8,128)(2,1)S(1)}, bf16[2,64,640]{2,1,0:T(8,128)(2,1)S(1)}, u32[]{:S(2)}, u32[]{:S(2)}) collective-permute-start(bf16[2,64,640]{2,1,0:T(8,128)(2,1)S(1)} %collective-permute-done.3.refs_4_), channel_id=1, source_target_pairs={{0,1},{1,0},{2,3},{3,2},{4,5},{5,4},{6,7},{7,6},{8,9},{9,8},{10,11... | collective-permute-start | bytes 491528 | tf_op jit(solution)/shard_map/ppermute | solution.py:31
  19.3 5.4 %copy-start.2 = (bf16[2,64,640]{2,1,0:T(8,128)(2,1)}, bf16[2,64,640]{2,1,0:T(8,128)(2,1)S(1)}, u32[]{:S(2)}) copy-start(bf16[2,64,640]{2,1,0:T(8,128)(2,1)S(1)} %collective-permute-done.9.refs_10_) | copy-start | bytes 491524
  19.3 5.3 %collective-permute-start.8 = (bf16[2,64,640]{2,1,0:T(8,128)(2,1)S(1)}, bf16[2,64,640]{2,1,0:T(8,128)(2,1)S(1)}, u32[]{:S(2)}, u32[]{:S(2)}) collective-permute-start(bf16[2,64,640]{2,1,0:T(8,128)(2,1)S(1)} %collective-permute-done.7.refs_8_), channel_id=1, source_target_pairs={{0,1},{1,0},{2,3},{3,2},{4,5},{5,4},{6,7},{7,6},{8,9},{9,8},{10,11... | collective-permute-start | bytes 491528 | tf_op jit(solution)/shard_map/ppermute | solution.py:31
  19.6 5.1 %copy-start.3 = (bf16[2,64,640]{2,1,0:T(8,128)(2,1)}, bf16[2,64,640]{2,1,0:T(8,128)(2,1)S(1)}, u32[]{:S(2)}) copy-start(bf16[2,64,640]{2,1,0:T(8,128)(2,1)S(1)} %collective-permute-done.1.refs_2_) | copy-start | bytes 491524
  19.6 5.1 %collective-permute-start.10 = (bf16[2,64,640]{2,1,0:T(8,128)(2,1)S(1)}, bf16[2,64,640]{2,1,0:T(8,128)(2,1)S(1)}, u32[]{:S(2)}, u32[]{:S(2)}) collective-permute-start(bf16[2,64,640]{2,1,0:T(8,128)(2,1)S(1)} %collective-permute-done.9.refs_10_), channel_id=1, source_target_pairs={{0,1},{1,0},{2,3},{3,2},{4,5},{5,4},{6,7},{7,6},{8,9},{9,8},{10,11... | collective-permute-start | bytes 491528 | tf_op jit(solution)/shard_map/ppermute | solution.py:31
  22.8 1.9 %copy-start.4 = (bf16[2,64,640]{2,1,0:T(8,128)(2,1)}, bf16[2,64,640]{2,1,0:T(8,128)(2,1)S(1)}, u32[]{:S(2)}) copy-start(bf16[2,64,640]{2,1,0:T(8,128)(2,1)S(1)} %collective-permute-done.5.refs_6_) | copy-start | bytes 491524
  22.8 1.8 %collective-permute-start.2 = (bf16[2,64,640]{2,1,0:T(8,128)(2,1)S(1)}, bf16[2,64,640]{2,1,0:T(8,128)(2,1)S(1)}, u32[]{:S(2)}, u32[]{:S(2)}) collective-permute-start(bf16[2,64,640]{2,1,0:T(8,128)(2,1)S(1)} %collective-permute-done.1.refs_2_), channel_id=1, source_target_pairs={{0,1},{1,0},{2,3},{3,2},{4,5},{5,4},{6,7},{7,6},{8,9},{9,8},{10,11... | collective-permute-start | bytes 491528 | tf_op jit(solution)/shard_map/ppermute | solution.py:31
  22.8 1.9 %copy-start.5 = (bf16[2,64,640]{2,1,0:T(8,128)(2,1)}, bf16[2,64,640]{2,1,0:T(8,128)(2,1)S(1)}, u32[]{:S(2)}) copy-start(bf16[2,64,640]{2,1,0:T(8,128)(2,1)S(1)} %collective-permute-done.refs_1_) | copy-start | bytes 491524
  22.8 1.8 %collective-permute-start.6 = (bf16[2,64,640]{2,1,0:T(8,128)(2,1)S(1)}, bf16[2,64,640]{2,1,0:T(8,128)(2,1)S(1)}, u32[]{:S(2)}, u32[]{:S(2)}) collective-permute-start(bf16[2,64,640]{2,1,0:T(8,128)(2,1)S(1)} %collective-permute-done.5.refs_6_), channel_id=1, source_target_pairs={{0,1},{1,0},{2,3},{3,2},{4,5},{5,4},{6,7},{7,6},{8,9},{9,8},{10,11... | collective-permute-start | bytes 491528 | tf_op jit(solution)/shard_map/ppermute | solution.py:31
  36.5 1.6 %collective-permute-start.13 = (bf16[64,640]{1,0:T(8,128)(2,1)}, bf16[64,640]{1,0:T(8,128)(2,1)S(1)}, u32[]{:S(2)}, u32[]{:S(2)}) collective-permute-start(bf16[64,640]{1,0:T(8,128)(2,1)} %get-tuple-element.16), channel_id=1, source_target_pairs={{0,1},{1,0},{2,3},{3,2},{4,5},{5,4},{6,7},{7,6},{8,9},{9,8},{10,11... | collective-permute-start | bytes 245768 | tf_op jit(solution)/shard_map/ppermute | solution.py:31
  36.7 3.1 %collective-permute-start.11 = (bf16[64,640]{1,0:T(8,128)(2,1)}, bf16[64,640]{1,0:T(8,128)(2,1)S(1)}, u32[]{:S(2)}, u32[]{:S(2)}) collective-permute-start(bf16[64,640]{1,0:T(8,128)(2,1)} %get-tuple-element.14), channel_id=1, source_target_pairs={{0,1},{1,0},{2,3},{3,2},{4,5},{5,4},{6,7},{7,6},{8,9},{9,8},{10,11... | collective-permute-start | bytes 245768 | tf_op jit(solution)/shard_map/ppermute | solution.py:31
  37.1 5.5 %collective-permute-start.12 = (bf16[64,640]{1,0:T(8,128)(2,1)}, bf16[64,640]{1,0:T(8,128)(2,1)S(1)}, u32[]{:S(2)}, u32[]{:S(2)}) collective-permute-start(bf16[64,640]{1,0:T(8,128)(2,1)} %get-tuple-element.15), channel_id=1, source_target_pairs={{0,2},{1,3},{2,0},{3,1},{4,6},{5,7},{6,4},{7,5},{8,10},{9,11},{10,... | collective-permute-start | bytes 245768 | tf_op jit(solution)/shard_map/ppermute | solution.py:31
  38.1 5.4 %collective-permute-start.14 = (bf16[64,640]{1,0:T(8,128)(2,1)S(1)}, bf16[64,640]{1,0:T(8,128)(2,1)S(1)}, u32[]{:S(2)}, u32[]{:S(2)}) collective-permute-start(bf16[64,640]{1,0:T(8,128)(2,1)S(1)} %collective-permute-done.13), channel_id=1, source_target_pairs={{0,2},{1,3},{2,0},{3,1},{4,6},{5,7},{6,4},{7,5},{8,10},{9,11},{10,... | collective-permute-start | bytes 245768 | tf_op jit(solution)/shard_map/ppermute | solution.py:31
  39.7 3.8 %copy-start.11 = (bf16[64,640]{1,0:T(8,128)(2,1)}, bf16[64,640]{1,0:T(8,128)(2,1)S(1)}, u32[]{:S(2)}) copy-start(bf16[64,640]{1,0:T(8,128)(2,1)S(1)} %collective-permute-done.11.refs_1_) | copy-start | bytes 245764
  42.6 0.9 %copy-start.12 = (bf16[64,640]{1,0:T(8,128)(2,1)}, bf16[64,640]{1,0:T(8,128)(2,1)S(1)}, u32[]{:S(2)}) copy-start(bf16[64,640]{1,0:T(8,128)(2,1)S(1)} %collective-permute-done.12.refs_2_) | copy-start | bytes 245764
  (6 other events, 4.2 us)

commit v4 on v3

--- a/solution.py
+++ b/solution.py
@@ -53,7 +53,7 @@
     return copies
 
 
-def pack_kernel(lat_ref, near_ref, far_ref):
+def pack_kernel(lat_ref, gain_ref, near_ref, far_ref):
     core, chip, _ = place()
     frames, _, cells, channels = lat_ref.shape
     half = cells // PACK
@@ -61,6 +61,9 @@
     for out_ref, tall in ((near_ref, chip), (far_ref, 1 - chip)):
         for i, side in enumerate((core, 1 - core)):
             x = lat_ref[:, side * 2 + tall].astype(jnp.float32)
+            cen = x - jnp.mean(x, axis=-1, keepdims=True)
+            var = jnp.mean(cen * cen, axis=-1, keepdims=True)
+            x = cen * lax.rsqrt(var + EPS) * gain_ref[...].reshape(1, 1, channels)
             x = jnp.concatenate([x, jnp.zeros((frames, cells, width - channels), x.dtype)], -1)
             halves = []
             for a in range(PACK):
@@ -71,10 +74,10 @@
 
 def attend_kernel(cells, planes, *refs):
     sources, refs = refs[:12], refs[12:]
-    off_hbm, num_hbm, gain_hbm, w_hbm, own_ref, sib_ref, far_own_ref, far_sib_ref = refs[:8]
+    off_hbm, num_hbm, w_hbm, own_ref, sib_ref, far_own_ref, far_sib_ref = refs[:7]
     (
-        off_ref, num_ref, gain_ref, w_ref, part_ref, norm_ref, q_ref, k_ref, v_ref, bias_ref, coef_ref, acc_ref, sem,
-    ) = refs[8:]
+        off_ref, num_ref, w_ref, part_ref, norm_ref, q_ref, k_ref, v_ref, bias_ref, coef_ref, acc_ref, sem,
+    ) = refs[7:]
     core, chip, plane = place()
     channels = w_ref.shape[0]
     head_dim = channels // HEADS
@@ -89,31 +92,17 @@
     wide = group * HEADS * query_frames
     chunks, lanes = k_ref.shape[0], k_ref.shape[2]
     copies = fetch(
-        [(gain_hbm, gain_ref)]
-        + [(src.at[i % 2], part_ref.at[i]) for i, src in enumerate(sources)]
+        [(src.at[i % 2], part_ref.at[i]) for i, src in enumerate(sources)]
         + [(w_hbm, w_ref), (off_hbm, off_ref), (num_hbm, num_ref)],
         sem,
     )
 
-    copies[0].wait()
-    gain = gain_ref[...]
-    pad = jnp.zeros((1, chunks * lanes - channels), jnp.float32)
-    gain = jnp.concatenate([gain, pad], 1)
-    last = lax.broadcasted_iota(jnp.int32, (part_rows, lanes), 1) < channels - (chunks - 1) * lanes
     for i in range(len(sources)):
-        copies[1 + i].wait()
+        copies[i].wait()
         for a, x in enumerate(unpack_lanes(part_ref[i].astype(jnp.float32))):
-            average = jnp.sum(sum(x), axis=-1, keepdims=True) * (1.0 / channels)
-            cen = [chunk - average for chunk in x]
-            cen[-1] = jnp.where(last, cen[-1], 0.0)
-            var = jnp.sum(sum(chunk * chunk for chunk in cen), axis=-1, keepdims=True)
-            scale = lax.rsqrt(var * (1.0 / channels) + EPS)
             start = a * key_rows + i * part_rows
-            normed = [
-                chunk * scale * gain[:, j * lanes : (j + 1) * lanes] for j, chunk in enumerate(cen)
-            ]
-            norm_ref[start : start + part_rows] = jnp.concatenate(normed, 1).astype(jnp.bfloat16)
-    for copy in copies[1 + len(sources) :]:
+            norm_ref[start : start + part_rows] = jnp.concatenate(x, 1).astype(jnp.bfloat16)
+    for copy in copies[len(sources) :]:
         copy.wait()
     pad = jnp.zeros((channels, chunks * lanes - channels), jnp.bfloat16)
     below = jnp.zeros((chunks * lanes - channels, chunks * lanes), jnp.bfloat16)
@@ -214,7 +203,7 @@
         out_ref[...] = pack_lanes(*pieces).astype(out_ref.dtype)
 
 
-def attend(parts, norm_gain, w_qkv, offsets, numerators, cells, planes):
+def attend(parts, w_qkv, offsets, numerators, cells, planes):
     channels = w_qkv.shape[0]
     vmem = pl.BlockSpec(memory_space=pltpu.VMEM)
     _, rows, packed = parts[0].shape
@@ -225,12 +214,11 @@
     return pl.pallas_call(
         functools.partial(attend_kernel, cells, planes),
         out_shape=[jax.ShapeDtypeStruct((rows, packed), jnp.bfloat16)] * 4,
-        in_specs=[pl.BlockSpec(memory_space=pl.ANY)] * 16,
+        in_specs=[pl.BlockSpec(memory_space=pl.ANY)] * 15,
         out_specs=[vmem] * 4,
         scratch_shapes=[
             pltpu.SMEM(offsets.shape, jnp.int32),
             pltpu.SMEM(numerators.shape, jnp.int32),
-            pltpu.VMEM((1, channels), jnp.float32),
             pltpu.VMEM(w_qkv.shape, jnp.bfloat16),
             pltpu.VMEM((12, rows, packed), jnp.bfloat16),
             pltpu.VMEM((keys, chunks * LANES), jnp.bfloat16),
@@ -240,11 +228,11 @@
             pltpu.VMEM((REACH + 1, 3 * query_frames, wide), jnp.float32),
             pltpu.VMEM((REACH + 1, 1, wide), jnp.float32),
             pltpu.VMEM((chunks, queries, LANES), jnp.float32),
-            pltpu.SemaphoreType.DMA((16,)),
+            pltpu.SemaphoreType.DMA((15,)),
         ],
         compiler_params=pltpu.CompilerParams(vmem_limit_bytes=60 * 1024 * 1024),
         name="window_attention",
-    )(*parts, offsets, numerators, norm_gain.reshape(1, channels), w_qkv)
+    )(*parts, offsets, numerators, w_qkv)
 
 
 def group_mean(sums, spread, count):
@@ -336,7 +324,7 @@
         hidden.append(hid.astype(jnp.bfloat16).astype(jnp.float32))
     acts = group_act(hidden, gn_ref[0:1], spread, members)
     copies[8].wait()
-    middle = [row + step_ref[...][None] for row in conv_rows(acts, one_ref, taps_ref)]
+    middle = [row + step_ref[...].reshape(1, 1, channels) for row in conv_rows(acts, one_ref, taps_ref)]
     acts = group_act(middle, gn_ref[1:2], spread, members)
     copies[9].wait()
     for r, row in enumerate(conv_rows(acts, two_ref, taps_ref)):
@@ -357,7 +345,7 @@
             pltpu.VMEM(latents.shape, jnp.bfloat16),
             pltpu.VMEM(w_out.shape, jnp.bfloat16),
             pltpu.VMEM(gn_gain.shape, jnp.float32),
-            pltpu.VMEM((1, channels), jnp.float32),
+            pltpu.VMEM(step_embed.shape, jnp.float32),
             pltpu.VMEM((9, deep, channels), jnp.bfloat16),
             pltpu.VMEM((9, deep, channels), jnp.bfloat16),
             pltpu.VMEM((frames, QUARTERS, count * cols // QUARTERS, channels), jnp.bfloat16),
@@ -371,7 +359,7 @@
         w_out,
         latents,
         gn_gain,
-        step_embed.reshape(1, channels),
+        step_embed,
         conv_one.reshape(9, channels, channels),
         conv_two.reshape(9, channels, channels),
     )
@@ -388,10 +376,10 @@
     near, far = pl.pallas_call(
         pack_kernel,
         out_shape=[jax.ShapeDtypeStruct((2, rows, packed), jnp.bfloat16)] * 2,
-        in_specs=[vmem],
+        in_specs=[vmem] * 2,
         out_specs=[vmem] * 2,
-        name="pack",
-    )(latents.reshape(block_len, QUARTERS, cells, channels))
+        name="norm_pack",
+    )(latents.reshape(block_len, QUARTERS, cells, channels), norm_gain)
     landed = [
         near,
         moved(far, lambda i: i ^ 2),
@@ -400,17 +388,18 @@
         moved(near, lambda i: i - QUARTERS),
         moved(far, lambda i: (i ^ 2) - QUARTERS),
     ]
+    landed[:4] = lax.optimization_barrier(landed[:4])
     parts = []
     for piece in landed:
         parts += [piece, moved(piece, lambda i: i ^ 1)]
     own, sib, far_own, far_sib = attend(
-        parts, norm_gain, w_qkv, offsets, numerators, cells, planes
+        parts, w_qkv, offsets, numerators, cells, planes
     )
     pieces = [
         own,
         moved(sib, lambda i: i ^ 1),
         moved(far_own, lambda i: i ^ 2),
-        moved(moved(far_sib, lambda i: i ^ 1), lambda i: i ^ 2),
+        moved(far_sib, lambda i: i ^ 3),
     ]
     return res_block(pieces, latents, w_out, gn_gain, conv_one, conv_two, step_embed)
 

time: 51.4 us -> 47.7 us (0.928)
  local copies, waits for them, and re-layouts: 3.93 us -> 1.66 us
  Pallas kernels: 19.3 us -> 17.5 us
  starting transfers between devices: 12.6 us -> 14.4 us
  waiting for transfers between devices: 15.2 us -> 13.8 us
    pallas_call x1, Pallas kernels: 10.4 us -> 8.31 us  [attend(): pl.pallas_call(functools.partial(attend_kernel, cells, planes), out_shape...]
    reshape x2 -> x0, local copies, waits for them, and re-layouts: 1.85 us -> none  [the longest x1 1.27 us: attend(): norm_gain.reshape(1, channels)]
    ppermute x15 -> x14, starting transfers between devices: 12.6 us -> 14.4 us  [moved(): lax.ppermute(array, 'frame', [(i, target(i) % count) for i in range(count)])]
    ppermute x15 -> x14, waiting for transfers between devices: 15.2 us -> 13.8 us  [moved(): lax.ppermute(array, 'frame', [(i, target(i) % count) for i in range(count)])]
    unnamed x30 -> x28, local copies, waits for them, and re-layouts: 2.07 us -> 1.66 us
  transfers between devices with their start and end apart: 15 -> 14, of which waited for: 8 -> 8; matrix products, arithmetic and copies ran while one was open for 4% -> 0% of each run, Pallas kernels for 0% -> 0%
where the time goes in v4:
time: 47.7 us; the launch traced here: 47.3 us
  Pallas kernels  17.5 us (37%)
  starting transfers between devices  14.4 us (30%)
  waiting for transfers between devices  13.8 us (29%)
  local copies, waits for them, and re-layouts  1.66 us (3%)
    ppermute x14, starting transfers between devices, moved(): lax.ppermute(array, 'frame', [(i, target(i) % count) for i in range(count)])  14.4 us
    ppermute x14, waiting for transfers between devices, moved(): lax.ppermute(array, 'frame', [(i, target(i) % count) for i in range(count)])  13.8 us
    pallas_call x1, Pallas kernels, attend(): pl.pallas_call(functools.partial(attend_kernel, cells, planes), out_shape...  8.31 us
    pallas_call x1, Pallas kernels, res_block(): pl.pallas_call(res_kernel, out_shape=jax.ShapeDtypeStruct(latents.shape,...  7.11 us
    pallas_call x1, Pallas kernels, body(): pl.pallas_call(pack_kernel, out_shape=[jax.ShapeDtypeStruct((2, rows, pac...  2.04 us
    unnamed x28, local copies, waits for them, and re-layouts  1.66 us
  transfers between devices with their start and end apart: 14, of which 8 were waited for; matrix products, arithmetic and copies ran while one was open for 0% of the time, Pallas kernels for 0%

profile of v4, /device:TPU:0, one launch (start us, length us, event | category | flops | bytes accessed | tf_op | source)
XLA Modules:
  0.0 47.3 jit_solution(5575949663365012442)
XLA Ops:
  0.0 2.0 %norm_pack.1 = (bf16[2,64,640]{2,1,0:T(8,128)(2,1)}, bf16[2,64,640]{2,1,0:T(8,128)(2,1)}) custom-call(bf16[4,4,32,320]{3,2,1,0:T(8,128)(2,1)} %bitcast.5, f32[320]{0:T(512)} %gain_ref.1), custom_call_target="tpu_custom_call" | custom-call | tf_op jit(solution)/shard_map/norm_pack/pallas_call | solution.py:376
  2.0 5.0 %collective-permute-start.7 = (bf16[2,64,640]{2,1,0:T(8,128)(2,1)}, bf16[2,64,640]{2,1,0:T(8,128)(2,1)S(1)}, u32[]{:S(2)}, u32[]{:S(2)}) collective-permute-start(bf16[2,64,640]{2,1,0:T(8,128)(2,1)} %get-tuple-element.17.refs_0_), channel_id=1, source_target_pairs={{0,12},{1,13},{2,14},{3,15},{4,0},{5,1},{6,2},{7,3},{8,4},{9,5},{1... | collective-permute-start | bytes 491528 | tf_op jit(solution)/shard_map/ppermute | solution.py:31
  7.1 1.0 %collective-permute-start.2 = (bf16[2,64,640]{2,1,0:T(8,128)(2,1)}, bf16[2,64,640]{2,1,0:T(8,128)(2,1)S(1)}, u32[]{:S(2)}, u32[]{:S(2)}) collective-permute-start(bf16[2,64,640]{2,1,0:T(8,128)(2,1)} %get-tuple-element.16), channel_id=1, source_target_pairs={{0,6},{1,7},{2,4},{3,5},{4,10},{5,11},{6,8},{7,9},{8,14},{9,15},{1... | collective-permute-start | bytes 491528 | tf_op jit(solution)/shard_map/ppermute | solution.py:31
  8.0 0.6 %collective-permute-start = (bf16[2,64,640]{2,1,0:T(8,128)(2,1)}, bf16[2,64,640]{2,1,0:T(8,128)(2,1)S(1)}, u32[]{:S(2)}, u32[]{:S(2)}) collective-permute-start(bf16[2,64,640]{2,1,0:T(8,128)(2,1)} %get-tuple-element.16), channel_id=1, source_target_pairs={{0,2},{1,3},{2,0},{3,1},{4,6},{5,7},{6,4},{7,5},{8,10},{9,11},{10,... | collective-permute-start | bytes 491528 | tf_op jit(solution)/shard_map/ppermute | solution.py:31
  8.6 4.7 %collective-permute-start.9 = (bf16[2,64,640]{2,1,0:T(8,128)(2,1)}, bf16[2,64,640]{2,1,0:T(8,128)(2,1)S(1)}, u32[]{:S(2)}, u32[]{:S(2)}) collective-permute-start(bf16[2,64,640]{2,1,0:T(8,128)(2,1)} %get-tuple-element.16), channel_id=1, source_target_pairs={{0,14},{1,15},{2,12},{3,13},{4,2},{5,3},{6,0},{7,1},{8,6},{9,7},{1... | collective-permute-start | bytes 491528 | tf_op jit(solution)/shard_map/ppermute | solution.py:31
  13.3 3.0 %collective-permute-done.1.refs_4_ = bf16[2,64,640]{2,1,0:T(8,128)(2,1)S(1)} collective-permute-done((bf16[2,64,640]{2,1,0:T(8,128)(2,1)}, bf16[2,64,640]{2,1,0:T(8,128)(2,1)S(1)}, u32[]{:S(2)}, u32[]{:S(2)}) %collective-permute-start.1) | collective-permute-done | bytes 163872 | tf_op jit(solution)/shard_map/ppermute | solution.py:31
  16.3 4.4 %collective-permute-done.2.refs_6_ = bf16[2,64,640]{2,1,0:T(8,128)(2,1)S(1)} collective-permute-done((bf16[2,64,640]{2,1,0:T(8,128)(2,1)}, bf16[2,64,640]{2,1,0:T(8,128)(2,1)S(1)}, u32[]{:S(2)}, u32[]{:S(2)}) %collective-permute-start.2) | collective-permute-done | bytes 163872 | tf_op jit(solution)/shard_map/ppermute | solution.py:31
  20.8 0.5 %collective-permute-start.4 = (bf16[2,64,640]{2,1,0:T(8,128)(2,1)S(1)}, bf16[2,64,640]{2,1,0:T(8,128)(2,1)S(1)}, u32[]{:S(2)}, u32[]{:S(2)}) collective-permute-start(bf16[2,64,640]{2,1,0:T(8,128)(2,1)S(1)} %collective-permute-done.refs_2_), channel_id=1, source_target_pairs={{0,1},{1,0},{2,3},{3,2},{4,5},{5,4},{6,7},{7,6},{8,9},{9,8},{10,11... | collective-permute-start | bytes 491528 | tf_op jit(solution)/shard_map/ppermute | solution.py:31
  21.3 0.8 %collective-permute-done.9.refs_10_ = bf16[2,64,640]{2,1,0:T(8,128)(2,1)S(1)} collective-permute-done((bf16[2,64,640]{2,1,0:T(8,128)(2,1)}, bf16[2,64,640]{2,1,0:T(8,128)(2,1)S(1)}, u32[]{:S(2)}, u32[]{:S(2)}) %collective-permute-start.9) | collective-permute-done | bytes 163872 | tf_op jit(solution)/shard_map/ppermute | solution.py:31
  22.1 0.5 %collective-permute-start.5 = (bf16[2,64,640]{2,1,0:T(8,128)(2,1)S(1)}, bf16[2,64,640]{2,1,0:T(8,128)(2,1)S(1)}, u32[]{:S(2)}, u32[]{:S(2)}) collective-permute-start(bf16[2,64,640]{2,1,0:T(8,128)(2,1)S(1)} %collective-permute-done.1.refs_4_), channel_id=1, source_target_pairs={{0,1},{1,0},{2,3},{3,2},{4,5},{5,4},{6,7},{7,6},{8,9},{9,8},{10,11... | collective-permute-start | bytes 491528 | tf_op jit(solution)/shard_map/ppermute | solution.py:31
  22.7 0.8 %collective-permute-done.10.refs_11_ = bf16[2,64,640]{2,1,0:T(8,128)(2,1)S(1)} collective-permute-done((bf16[2,64,640]{2,1,0:T(8,128)(2,1)S(1)}, bf16[2,64,640]{2,1,0:T(8,128)(2,1)S(1)}, u32[]{:S(2)}, u32[]{:S(2)}) %collective-permute-start.10) | collective-permute-done | bytes 163872 | tf_op jit(solution)/shard_map/ppermute | solution.py:31
  23.5 0.2 collective-permute-done.5.refs_5_
  23.8 0.3 collective-permute-done.6.refs_7_
  24.1 0.1 copy-done.8
  24.4 0.7 %copy-done.10 = bf16[2,64,640]{2,1,0:T(8,128)(2,1)} copy-done((bf16[2,64,640]{2,1,0:T(8,128)(2,1)}, bf16[2,64,640]{2,1,0:T(8,128)(2,1)S(1)}, u32[]{:S(2)}) %copy-start.10) | copy-done | bytes 163864
  25.1 8.3 %window_attention.1 = (bf16[64,640]{1,0:T(8,128)(2,1)}, bf16[64,640]{1,0:T(8,128)(2,1)}, bf16[64,640]{1,0:T(8,128)(2,1)}, bf16[64,640]{1,0:T(8,128)(2,1)}) custom-call(bf16[2,64,640]{2,1,0:T(8,128)(2,1)} %get-tuple-element.17.refs_0_, bf16[2,64,640]{2,1,0:T(8,128)(2,1)} %copy-done.6, bf16[2,64,640]{2,1,0:T(8,128)(2,1)} %copy-done.3, ...), custom_call_target="tpu_custom_call" | custom-call | tf_op jit(solution)/shard_map/window_attention/pallas_call | solution.py:214
  33.4 0.3 collective-permute-start.11
  33.8 0.9 %collective-permute-start.12 = (bf16[64,640]{1,0:T(8,128)(2,1)}, bf16[64,640]{1,0:T(8,128)(2,1)S(1)}, u32[]{:S(2)}, u32[]{:S(2)}) collective-permute-start(bf16[64,640]{1,0:T(8,128)(2,1)} %get-tuple-element.23), channel_id=1, source_target_pairs={{0,2},{1,3},{2,0},{3,1},{4,6},{5,7},{6,4},{7,5},{8,10},{9,11},{10,... | collective-permute-start | bytes 245768 | tf_op jit(solution)/shard_map/ppermute | solution.py:31
  34.7 0.7 %collective-permute-start.13 = (bf16[64,640]{1,0:T(8,128)(2,1)}, bf16[64,640]{1,0:T(8,128)(2,1)S(1)}, u32[]{:S(2)}, u32[]{:S(2)}) collective-permute-start(bf16[64,640]{1,0:T(8,128)(2,1)} %get-tuple-element.24), channel_id=1, source_target_pairs={{0,3},{1,2},{2,1},{3,0},{4,7},{5,6},{6,5},{7,4},{8,11},{9,10},{10,... | collective-permute-start | bytes 245768 | tf_op jit(solution)/shard_map/ppermute | solution.py:31
  35.3 3.9 %collective-permute-done.12.refs_2_ = bf16[64,640]{1,0:T(8,128)(2,1)S(1)} collective-permute-done((bf16[64,640]{1,0:T(8,128)(2,1)}, bf16[64,640]{1,0:T(8,128)(2,1)S(1)}, u32[]{:S(2)}, u32[]{:S(2)}) %collective-permute-start.12) | collective-permute-done | bytes 81952 | tf_op jit(solution)/shard_map/ppermute | solution.py:31
  39.2 0.4 collective-permute-done.13.refs_3_
  39.6 0.3 copy-done.12
  39.9 0.4 copy-done.13
  40.2 7.1 %res_block.1 = bf16[4,2,64,320]{3,2,1,0:T(8,128)(2,1)} custom-call(bf16[64,640]{1,0:T(8,128)(2,1)} %get-tuple-element.21.refs_0_, bf16[64,640]{1,0:T(8,128)(2,1)} %copy-done.11, bf16[64,640]{1,0:T(8,128)(2,1)} %copy-done.12, bf16[64,640]{1,0:T(8,128)(2,1)} %copy-done.13, bf16[320,320]{1,0:T(8,128)(2,1)} %refs_4_.1, bf16[4,2,64,320]{3,2,1,0:T(8,128)(2,1)} %refs_5_.1, ...), custom_call_target="tpu_custom_call" | custom-call | tf_op jit(solution)/shard_map/res_block/pallas_call | solution.py:338
  (35 shorter events, 0.4 us)
Async XLA Ops:
  2.0 11.3 %collective-permute-start.7 = (bf16[2,64,640]{2,1,0:T(8,128)(2,1)}, bf16[2,64,640]{2,1,0:T(8,128)(2,1)S(1)}, u32[]{:S(2)}, u32[]{:S(2)}) collective-permute-start(bf16[2,64,640]{2,1,0:T(8,128)(2,1)} %get-tuple-element.17.refs_0_), channel_id=1, source_target_pairs={{0,12},{1,13},{2,14},{3,15},{4,0},{5,1},{6,2},{7,3},{8,4},{9,5},{1... | collective-permute-start | bytes 491528 | tf_op jit(solution)/shard_map/ppermute | solution.py:31
  7.1 9.2 %collective-permute-start.1 = (bf16[2,64,640]{2,1,0:T(8,128)(2,1)}, bf16[2,64,640]{2,1,0:T(8,128)(2,1)S(1)}, u32[]{:S(2)}, u32[]{:S(2)}) collective-permute-start(bf16[2,64,640]{2,1,0:T(8,128)(2,1)} %get-tuple-element.17.refs_0_), channel_id=1, source_target_pairs={{0,4},{1,5},{2,6},{3,7},{4,8},{5,9},{6,10},{7,11},{8,12},{9,13},{1... | collective-permute-start | bytes 491528 | tf_op jit(solution)/shard_map/ppermute | solution.py:31
  7.1 13.6 %collective-permute-start.2 = (bf16[2,64,640]{2,1,0:T(8,128)(2,1)}, bf16[2,64,640]{2,1,0:T(8,128)(2,1)S(1)}, u32[]{:S(2)}, u32[]{:S(2)}) collective-permute-start(bf16[2,64,640]{2,1,0:T(8,128)(2,1)} %get-tuple-element.16), channel_id=1, source_target_pairs={{0,6},{1,7},{2,4},{3,5},{4,10},{5,11},{6,8},{7,9},{8,14},{9,15},{1... | collective-permute-start | bytes 491528 | tf_op jit(solution)/shard_map/ppermute | solution.py:31
  8.0 12.7 %collective-permute-start = (bf16[2,64,640]{2,1,0:T(8,128)(2,1)}, bf16[2,64,640]{2,1,0:T(8,128)(2,1)S(1)}, u32[]{:S(2)}, u32[]{:S(2)}) collective-permute-start(bf16[2,64,640]{2,1,0:T(8,128)(2,1)} %get-tuple-element.16), channel_id=1, source_target_pairs={{0,2},{1,3},{2,0},{3,1},{4,6},{5,7},{6,4},{7,5},{8,10},{9,11},{10,... | collective-permute-start | bytes 491528 | tf_op jit(solution)/shard_map/ppermute | solution.py:31
  8.6 13.5 %collective-permute-start.9 = (bf16[2,64,640]{2,1,0:T(8,128)(2,1)}, bf16[2,64,640]{2,1,0:T(8,128)(2,1)S(1)}, u32[]{:S(2)}, u32[]{:S(2)}) collective-permute-start(bf16[2,64,640]{2,1,0:T(8,128)(2,1)} %get-tuple-element.16), channel_id=1, source_target_pairs={{0,14},{1,15},{2,12},{3,13},{4,2},{5,3},{6,0},{7,1},{8,6},{9,7},{1... | collective-permute-start | bytes 491528 | tf_op jit(solution)/shard_map/ppermute | solution.py:31
  13.3 10.7 %copy-start = (bf16[2,64,640]{2,1,0:T(8,128)(2,1)}, bf16[2,64,640]{2,1,0:T(8,128)(2,1)S(1)}, u32[]{:S(2)}) copy-start(bf16[2,64,640]{2,1,0:T(8,128)(2,1)S(1)} %collective-permute-done.7.refs_8_) | copy-start | bytes 491524
  13.3 9.3 %collective-permute-start.8 = (bf16[2,64,640]{2,1,0:T(8,128)(2,1)S(1)}, bf16[2,64,640]{2,1,0:T(8,128)(2,1)S(1)}, u32[]{:S(2)}, u32[]{:S(2)}) collective-permute-start(bf16[2,64,640]{2,1,0:T(8,128)(2,1)S(1)} %collective-permute-done.7.refs_8_), channel_id=1, source_target_pairs={{0,1},{1,0},{2,3},{3,2},{4,5},{5,4},{6,7},{7,6},{8,9},{9,8},{10,11... | collective-permute-start | bytes 491528 | tf_op jit(solution)/shard_map/ppermute | solution.py:31
  16.3 7.7 %copy-start.1 = (bf16[2,64,640]{2,1,0:T(8,128)(2,1)}, bf16[2,64,640]{2,1,0:T(8,128)(2,1)S(1)}, u32[]{:S(2)}) copy-start(bf16[2,64,640]{2,1,0:T(8,128)(2,1)S(1)} %collective-permute-done.1.refs_4_) | copy-start | bytes 491524
  20.7 3.3 %copy-start.2 = (bf16[2,64,640]{2,1,0:T(8,128)(2,1)}, bf16[2,64,640]{2,1,0:T(8,128)(2,1)S(1)}, u32[]{:S(2)}) copy-start(bf16[2,64,640]{2,1,0:T(8,128)(2,1)S(1)} %collective-permute-done.2.refs_6_) | copy-start | bytes 491524
  20.7 3.3 %copy-start.3 = (bf16[2,64,640]{2,1,0:T(8,128)(2,1)}, bf16[2,64,640]{2,1,0:T(8,128)(2,1)S(1)}, u32[]{:S(2)}) copy-start(bf16[2,64,640]{2,1,0:T(8,128)(2,1)S(1)} %collective-permute-done.refs_2_) | copy-start | bytes 491524
  20.7 2.8 %collective-permute-start.3 = (bf16[2,64,640]{2,1,0:T(8,128)(2,1)}, bf16[2,64,640]{2,1,0:T(8,128)(2,1)S(1)}, u32[]{:S(2)}, u32[]{:S(2)}) collective-permute-start(bf16[2,64,640]{2,1,0:T(8,128)(2,1)} %get-tuple-element.17.refs_0_), channel_id=1, source_target_pairs={{0,1},{1,0},{2,3},{3,2},{4,5},{5,4},{6,7},{7,6},{8,9},{9,8},{10,11... | collective-permute-start | bytes 491528 | tf_op jit(solution)/shard_map/ppermute | solution.py:31
  20.8 2.7 %collective-permute-start.4 = (bf16[2,64,640]{2,1,0:T(8,128)(2,1)S(1)}, bf16[2,64,640]{2,1,0:T(8,128)(2,1)S(1)}, u32[]{:S(2)}, u32[]{:S(2)}) collective-permute-start(bf16[2,64,640]{2,1,0:T(8,128)(2,1)S(1)} %collective-permute-done.refs_2_), channel_id=1, source_target_pairs={{0,1},{1,0},{2,3},{3,2},{4,5},{5,4},{6,7},{7,6},{8,9},{9,8},{10,11... | collective-permute-start | bytes 491528 | tf_op jit(solution)/shard_map/ppermute | solution.py:31
  22.1 1.9 %copy-start.4 = (bf16[2,64,640]{2,1,0:T(8,128)(2,1)}, bf16[2,64,640]{2,1,0:T(8,128)(2,1)S(1)}, u32[]{:S(2)}) copy-start(bf16[2,64,640]{2,1,0:T(8,128)(2,1)S(1)} %collective-permute-done.9.refs_10_) | copy-start | bytes 491524
  22.1 1.4 %collective-permute-start.10 = (bf16[2,64,640]{2,1,0:T(8,128)(2,1)S(1)}, bf16[2,64,640]{2,1,0:T(8,128)(2,1)S(1)}, u32[]{:S(2)}, u32[]{:S(2)}) collective-permute-start(bf16[2,64,640]{2,1,0:T(8,128)(2,1)S(1)} %collective-permute-done.9.refs_10_), channel_id=1, source_target_pairs={{0,1},{1,0},{2,3},{3,2},{4,5},{5,4},{6,7},{7,6},{8,9},{9,8},{10,11... | collective-permute-start | bytes 491528 | tf_op jit(solution)/shard_map/ppermute | solution.py:31
  22.1 1.6 %collective-permute-start.5 = (bf16[2,64,640]{2,1,0:T(8,128)(2,1)S(1)}, bf16[2,64,640]{2,1,0:T(8,128)(2,1)S(1)}, u32[]{:S(2)}, u32[]{:S(2)}) collective-permute-start(bf16[2,64,640]{2,1,0:T(8,128)(2,1)S(1)} %collective-permute-done.1.refs_4_), channel_id=1, source_target_pairs={{0,1},{1,0},{2,3},{3,2},{4,5},{5,4},{6,7},{7,6},{8,9},{9,8},{10,11... | collective-permute-start | bytes 491528 | tf_op jit(solution)/shard_map/ppermute | solution.py:31
  22.6 1.4 %copy-start.5 = (bf16[2,64,640]{2,1,0:T(8,128)(2,1)}, bf16[2,64,640]{2,1,0:T(8,128)(2,1)S(1)}, u32[]{:S(2)}) copy-start(bf16[2,64,640]{2,1,0:T(8,128)(2,1)S(1)} %collective-permute-done.8.refs_9_) | copy-start | bytes 491524
  22.6 1.4 %collective-permute-start.6 = (bf16[2,64,640]{2,1,0:T(8,128)(2,1)S(1)}, bf16[2,64,640]{2,1,0:T(8,128)(2,1)S(1)}, u32[]{:S(2)}, u32[]{:S(2)}) collective-permute-start(bf16[2,64,640]{2,1,0:T(8,128)(2,1)S(1)} %collective-permute-done.2.refs_6_), channel_id=1, source_target_pairs={{0,1},{1,0},{2,3},{3,2},{4,5},{5,4},{6,7},{7,6},{8,9},{9,8},{10,11... | collective-permute-start | bytes 491528 | tf_op jit(solution)/shard_map/ppermute | solution.py:31
  23.5 0.7 %copy-start.8 = (bf16[2,64,640]{2,1,0:T(8,128)(2,1)}, bf16[2,64,640]{2,1,0:T(8,128)(2,1)S(1)}, u32[]{:S(2)}) copy-start(bf16[2,64,640]{2,1,0:T(8,128)(2,1)S(1)} %collective-permute-done.10.refs_11_) | copy-start | bytes 491524
  23.5 0.7 %copy-start.6 = (bf16[2,64,640]{2,1,0:T(8,128)(2,1)}, bf16[2,64,640]{2,1,0:T(8,128)(2,1)S(1)}, u32[]{:S(2)}) copy-start(bf16[2,64,640]{2,1,0:T(8,128)(2,1)S(1)} %collective-permute-done.3.refs_1_) | copy-start | bytes 491524
  23.5 0.8 %copy-start.7 = (bf16[2,64,640]{2,1,0:T(8,128)(2,1)}, bf16[2,64,640]{2,1,0:T(8,128)(2,1)S(1)}, u32[]{:S(2)}) copy-start(bf16[2,64,640]{2,1,0:T(8,128)(2,1)S(1)} %collective-permute-done.4.refs_3_) | copy-start | bytes 491524
  33.4 1.9 %collective-permute-start.11 = (bf16[64,640]{1,0:T(8,128)(2,1)}, bf16[64,640]{1,0:T(8,128)(2,1)S(1)}, u32[]{:S(2)}, u32[]{:S(2)}) collective-permute-start(bf16[64,640]{1,0:T(8,128)(2,1)} %get-tuple-element.22), channel_id=1, source_target_pairs={{0,1},{1,0},{2,3},{3,2},{4,5},{5,4},{6,7},{7,6},{8,9},{9,8},{10,11... | collective-permute-start | bytes 245768 | tf_op jit(solution)/shard_map/ppermute | solution.py:31
  33.8 5.5 %collective-permute-start.12 = (bf16[64,640]{1,0:T(8,128)(2,1)}, bf16[64,640]{1,0:T(8,128)(2,1)S(1)}, u32[]{:S(2)}, u32[]{:S(2)}) collective-permute-start(bf16[64,640]{1,0:T(8,128)(2,1)} %get-tuple-element.23), channel_id=1, source_target_pairs={{0,2},{1,3},{2,0},{3,1},{4,6},{5,7},{6,4},{7,5},{8,10},{9,11},{10,... | collective-permute-start | bytes 245768 | tf_op jit(solution)/shard_map/ppermute | solution.py:31
  34.7 5.0 %collective-permute-start.13 = (bf16[64,640]{1,0:T(8,128)(2,1)}, bf16[64,640]{1,0:T(8,128)(2,1)S(1)}, u32[]{:S(2)}, u32[]{:S(2)}) collective-permute-start(bf16[64,640]{1,0:T(8,128)(2,1)} %get-tuple-element.24), channel_id=1, source_target_pairs={{0,3},{1,2},{2,1},{3,0},{4,7},{5,6},{6,5},{7,4},{8,11},{9,10},{10,... | collective-permute-start | bytes 245768 | tf_op jit(solution)/shard_map/ppermute | solution.py:31
  35.3 4.3 %copy-start.11 = (bf16[64,640]{1,0:T(8,128)(2,1)}, bf16[64,640]{1,0:T(8,128)(2,1)S(1)}, u32[]{:S(2)}) copy-start(bf16[64,640]{1,0:T(8,128)(2,1)S(1)} %collective-permute-done.11.refs_1_) | copy-start | bytes 245764
  (4 other events, 2.6 us)

commit v5 on v4

--- a/solution.py
+++ b/solution.py
@@ -74,12 +74,12 @@
 
 def attend_kernel(cells, planes, *refs):
     sources, refs = refs[:12], refs[12:]
-    off_hbm, num_hbm, w_hbm, own_ref, sib_ref, far_own_ref, far_sib_ref = refs[:7]
+    ints_hbm, w_ref, own_ref, sib_ref, far_own_ref, far_sib_ref = refs[:6]
     (
-        off_ref, num_ref, w_ref, part_ref, norm_ref, q_ref, k_ref, v_ref, bias_ref, coef_ref, acc_ref, sem,
-    ) = refs[7:]
+        ints_ref, part_ref, norm_ref, q_ref, k_ref, v_ref, bias_ref, coef_ref, acc_ref, sem,
+    ) = refs[6:]
     core, chip, plane = place()
-    channels = w_ref.shape[0]
+    channels = own_ref.shape[1] // PACK
     head_dim = channels // HEADS
     half = cells // PACK
     part_rows = part_ref.shape[1]
@@ -93,7 +93,7 @@
     chunks, lanes = k_ref.shape[0], k_ref.shape[2]
     copies = fetch(
         [(src.at[i % 2], part_ref.at[i]) for i, src in enumerate(sources)]
-        + [(w_hbm, w_ref), (off_hbm, off_ref), (num_hbm, num_ref)],
+        + [(ints_hbm, ints_ref)],
         sem,
     )
 
@@ -104,11 +104,9 @@
             norm_ref[start : start + part_rows] = jnp.concatenate(x, 1).astype(jnp.bfloat16)
     for copy in copies[len(sources) :]:
         copy.wait()
-    pad = jnp.zeros((channels, chunks * lanes - channels), jnp.bfloat16)
-    below = jnp.zeros((chunks * lanes - channels, chunks * lanes), jnp.bfloat16)
+    pad = jnp.zeros((chunks * lanes, chunks * lanes - channels), jnp.bfloat16)
     for i, (out_ref, rows) in enumerate(((q_ref, query_rows), (k_ref, key_rows), (v_ref, key_rows))):
         w = jnp.concatenate([w_ref[:, i * channels : (i + 1) * channels], pad], 1)
-        w = jnp.concatenate([w, below], 0)
         for a in range(PACK):
             here = norm_ref[a * key_rows : a * key_rows + rows]
             res = jnp.dot(here, w, preferred_element_type=jnp.float32)
@@ -137,11 +135,11 @@
         owner = jnp.where(owner < 0, owner + blocks, owner)
         shift = jnp.zeros((1, wide), jnp.int32)
         for w in range(blocks):
-            shift = jnp.where(owner == w, off_ref[w], shift)
+            shift = jnp.where(owner == w, ints_ref[w], shift)
         at = BLOCK * back + rest - shift
         weight = jnp.zeros((1, wide), jnp.int32)
         for j in range(WINDOW):
-            weight = jnp.where(at == j, num_ref[j], weight)
+            weight = jnp.where(at == j, ints_ref[blocks + j], weight)
         weights.append(weight.astype(jnp.float32))
         rel = key - (BLOCK * owner + shift)
         rel = jnp.where(rel < 0, rel + frames, rel)
@@ -203,10 +201,10 @@
         out_ref[...] = pack_lanes(*pieces).astype(out_ref.dtype)
 
 
-def attend(parts, w_qkv, offsets, numerators, cells, planes):
-    channels = w_qkv.shape[0]
+def attend(parts, w_wide, ints, cells, planes):
+    channels = w_wide.shape[1] // 3
     vmem = pl.BlockSpec(memory_space=pltpu.VMEM)
-    _, rows, packed = parts[0].shape
+    _, rows, packed = parts[1].shape
     chunks = -(-channels // LANES)
     query_frames = 4 * rows * PACK // cells
     wide = GROUP * HEADS * query_frames
@@ -214,12 +212,10 @@
     return pl.pallas_call(
         functools.partial(attend_kernel, cells, planes),
         out_shape=[jax.ShapeDtypeStruct((rows, packed), jnp.bfloat16)] * 4,
-        in_specs=[pl.BlockSpec(memory_space=pl.ANY)] * 15,
+        in_specs=[pl.BlockSpec(memory_space=pl.ANY)] * 13 + [vmem],
         out_specs=[vmem] * 4,
         scratch_shapes=[
-            pltpu.SMEM(offsets.shape, jnp.int32),
-            pltpu.SMEM(numerators.shape, jnp.int32),
-            pltpu.VMEM(w_qkv.shape, jnp.bfloat16),
+            pltpu.SMEM(ints.shape, jnp.int32),
             pltpu.VMEM((12, rows, packed), jnp.bfloat16),
             pltpu.VMEM((keys, chunks * LANES), jnp.bfloat16),
             pltpu.VMEM((chunks, queries, LANES), jnp.float32),
@@ -228,11 +224,11 @@
             pltpu.VMEM((REACH + 1, 3 * query_frames, wide), jnp.float32),
             pltpu.VMEM((REACH + 1, 1, wide), jnp.float32),
             pltpu.VMEM((chunks, queries, LANES), jnp.float32),
-            pltpu.SemaphoreType.DMA((15,)),
+            pltpu.SemaphoreType.DMA((13,)),
         ],
-        compiler_params=pltpu.CompilerParams(vmem_limit_bytes=60 * 1024 * 1024),
+        compiler_params=pltpu.CompilerParams(vmem_limit_bytes=30 * 1024 * 1024),
         name="window_attention",
-    )(*parts, offsets, numerators, w_qkv)
+    )(*parts, ints, w_wide)
 
 
 def group_mean(sums, spread, count):
@@ -259,7 +255,7 @@
 
 def conv_rows(acts, w_ref, taps_ref):
     frames, cols, channels = acts[0].shape
-    deep = w_ref.shape[1]
+    deep = w_ref.shape[2]
     count = len(acts)
     col = lax.broadcasted_iota(jnp.int32, (frames * cols, 1), 0) % cols
     for r, act in enumerate(acts):
@@ -273,7 +269,7 @@
     for r in range(count):
         lo, hi = max(r - 1, 0), min(r + 1, count - 1)
         left = taps_ref[:, 3 * lo * deep : 3 * (hi + 1) * deep]
-        right = w_ref[3 * (lo - r + 1) : 3 * (hi - r + 2)]
+        right = w_ref[lo - r + 1 : hi - r + 2]
         right = right.reshape(-1, channels)
         out = jnp.dot(left, right, preferred_element_type=jnp.float32)
         outs.append(out.reshape(frames, cols, channels))
@@ -281,24 +277,17 @@
 
 
 def res_kernel(*refs):
-    sources, out_ref = refs[:10], refs[10]
-    (
-        part_ref, lat_ref, w_out_ref, gn_ref, step_ref, one_ref, two_ref, comb_ref, taps_ref, sem,
-    ) = refs[11:]
-    frames, count, cols, channels = lat_ref.shape
-    deep = one_ref.shape[1]
-    targets = [part_ref.at[i] for i in range(4)] + [w_out_ref, lat_ref, gn_ref, step_ref]
-    targets += [ref.at[:, :channels, :] for ref in (one_ref, two_ref)]
-    copies = fetch(list(zip(sources, targets)), sem)
-    for ref in (one_ref, two_ref):
-        ref[:, channels:, :] = jnp.zeros((ref.shape[0], deep - channels, channels), jnp.bfloat16)
+    part_refs, (lat_ref, w_out_ref, gn_ref, one_ref, two_ref, out_ref) = refs[:4], refs[4:10]
+    comb_ref, taps_ref = refs[10:]
+    count, frames, cols, channels = lat_ref.shape
+    deep = one_ref.shape[2]
     for i in range(3 * count):
         taps_ref[:, i * deep + channels : (i + 1) * deep] = jnp.zeros(
             (frames * cols, deep - channels), jnp.bfloat16
         )
     size = channels // NORM_GROUPS
-    group_r = lax.broadcasted_iota(jnp.int32, (channels, channels), 0) // size
-    group_c = lax.broadcasted_iota(jnp.int32, (channels, channels), 1) // size
+    group_r = lax.broadcasted_iota(jnp.int32, (channels, 1), 0) // size
+    group_c = lax.broadcasted_iota(jnp.int32, (1, channels), 1) // size
     spread = jnp.where(group_r == group_c, 1.0, 0.0).astype(jnp.bfloat16)
     members = count * cols * size
 
@@ -307,61 +296,43 @@
     for i, (side, tall) in enumerate(
         ((core, chip), (1 - core, chip), (core, 1 - chip), (1 - core, 1 - chip))
     ):
-        copies[i].wait()
-        for a, piece in enumerate(unpack_lanes(part_ref[i].astype(jnp.float32))):
+        for a, piece in enumerate(unpack_lanes(part_refs[i][...].astype(jnp.float32))):
             piece = jnp.concatenate(piece, 1)[:, :channels].astype(jnp.bfloat16)
             comb_ref[:, side * 2 + tall, a * half : (a + 1) * half, :] = piece.reshape(
                 frames, half, channels
             )
-    for copy in copies[4:8]:
-        copy.wait()
     combined = comb_ref[...].reshape(frames, count * cols, channels)
     hidden = []
     for r in range(count):
         comb = combined[:, r * cols : (r + 1) * cols, :].reshape(frames * cols, channels)
-        proj = jnp.dot(comb, w_out_ref[...], preferred_element_type=jnp.float32)
-        hid = lat_ref[:, r].astype(jnp.float32) + proj.reshape(frames, cols, channels)
+        proj = jnp.dot(comb, w_out_ref[:channels], preferred_element_type=jnp.float32)
+        hid = lat_ref[r].astype(jnp.float32) + proj.reshape(frames, cols, channels)
         hidden.append(hid.astype(jnp.bfloat16).astype(jnp.float32))
     acts = group_act(hidden, gn_ref[0:1], spread, members)
-    copies[8].wait()
-    middle = [row + step_ref[...].reshape(1, 1, channels) for row in conv_rows(acts, one_ref, taps_ref)]
+    middle = [row + gn_ref[2:3][None] for row in conv_rows(acts, one_ref, taps_ref)]
     acts = group_act(middle, gn_ref[1:2], spread, members)
-    copies[9].wait()
     for r, row in enumerate(conv_rows(acts, two_ref, taps_ref)):
         out_ref[:, r] = (hidden[r] + row).astype(out_ref.dtype)
 
 
-def res_block(parts, latents, w_out, gn_gain, conv_one, conv_two, step_embed):
-    frames, count, cols, channels = latents.shape
-    deep = -(-channels // 128) * 128
+def res_block(parts, extras):
+    count, frames, cols, channels = extras[0].shape
+    deep = -(-channels // LANES) * LANES
     vmem = pl.BlockSpec(memory_space=pltpu.VMEM)
     return pl.pallas_call(
         res_kernel,
-        out_shape=jax.ShapeDtypeStruct(latents.shape, jnp.bfloat16),
-        in_specs=[pl.BlockSpec(memory_space=pl.ANY)] * 10,
+        out_shape=jax.ShapeDtypeStruct((frames, count, cols, channels), jnp.bfloat16),
+        in_specs=[vmem] * 9,
         out_specs=vmem,
         scratch_shapes=[
-            pltpu.VMEM((4,) + parts[0].shape, jnp.bfloat16),
-            pltpu.VMEM(latents.shape, jnp.bfloat16),
-            pltpu.VMEM(w_out.shape, jnp.bfloat16),
-            pltpu.VMEM(gn_gain.shape, jnp.float32),
-            pltpu.VMEM(step_embed.shape, jnp.float32),
-            pltpu.VMEM((9, deep, channels), jnp.bfloat16),
-            pltpu.VMEM((9, deep, channels), jnp.bfloat16),
             pltpu.VMEM((frames, QUARTERS, count * cols // QUARTERS, channels), jnp.bfloat16),
             pltpu.VMEM((frames * cols, 3 * count * deep), jnp.bfloat16),
-            pltpu.SemaphoreType.DMA((10,)),
         ],
-        compiler_params=pltpu.CompilerParams(vmem_limit_bytes=60 * 1024 * 1024),
+        compiler_params=pltpu.CompilerParams(vmem_limit_bytes=30 * 1024 * 1024),
         name="res_block",
     )(
         *parts,
-        w_out,
-        latents,
-        gn_gain,
-        step_embed,
-        conv_one.reshape(9, channels, channels),
-        conv_two.reshape(9, channels, channels),
+        *extras,
     )
 
 
@@ -388,20 +359,31 @@
         moved(near, lambda i: i - QUARTERS),
         moved(far, lambda i: (i ^ 2) - QUARTERS),
     ]
-    landed[:4] = lax.optimization_barrier(landed[:4])
+    more = (0, -channels % LANES)
+    extras = [
+        jnp.pad(w_qkv, (more, (0, 0))),
+        jnp.concatenate([offsets, numerators]),
+        latents.transpose(1, 0, 2, 3),
+        jnp.pad(w_out, (more, (0, 0))),
+        jnp.concatenate([gn_gain, step_embed[None]]),
+        jnp.pad(conv_one, ((0, 0), (0, 0), more, (0, 0))),
+        jnp.pad(conv_two, ((0, 0), (0, 0), more, (0, 0))),
+    ]
+    landed[1:4] = lax.optimization_barrier(landed[1:4])
+    landed[0], extras = lax.optimization_barrier((near, extras))
     parts = []
     for piece in landed:
         parts += [piece, moved(piece, lambda i: i ^ 1)]
-    own, sib, far_own, far_sib = attend(
-        parts, w_qkv, offsets, numerators, cells, planes
-    )
+    parts[0] = parts[0][:1]
+    w_wide, ints, *extras = extras
+    own, sib, far_own, far_sib = attend(parts, w_wide, ints, cells, planes)
     pieces = [
         own,
         moved(sib, lambda i: i ^ 1),
         moved(far_own, lambda i: i ^ 2),
         moved(far_sib, lambda i: i ^ 3),
     ]
-    return res_block(pieces, latents, w_out, gn_gain, conv_one, conv_two, step_embed)
+    return res_block(pieces, extras)
 
 
 def solution(mesh):

time: 47.7 us -> 46 us (0.964)
  waiting for transfers between devices: 13.8 us -> 8.44 us
  local copies, waits for them, and re-layouts: 1.66 us -> 6.39 us
  Pallas kernels: 17.5 us -> 15.9 us
  other arithmetic: 0 us -> 1.44 us
  starting transfers between devices: 14.4 us -> 13.4 us
    ppermute x14, waiting for transfers between devices: 13.8 us -> 8.44 us  [moved(): lax.ppermute(array, 'frame', [(i, target(i) % count) for i in range(count)])]
    pad x0 -> x4, local copies, waits for them, and re-layouts: none -> 2.73 us  [the longest x1 1.18 us: body(): jnp.pad(w_qkv, (more, (0, 0)))]
    concatenate x0 -> x2, other arithmetic: none -> 1.44 us  [the longest x1 0.75 us: body(): jnp.concatenate([offsets, numerators])]
    pallas_call x1, Pallas kernels: 7.11 us -> 5.72 us  [res_block(): pl.pallas_call(res_kernel, out_shape=jax.ShapeDtypeStruct((frames, count,...]
    unnamed x28 -> x7, local copies, waits for them, and re-layouts: 1.66 us -> 2.97 us
    ppermute x14, starting transfers between devices: 14.4 us -> 13.4 us  [moved(): lax.ppermute(array, 'frame', [(i, target(i) % count) for i in range(count)])]
    broadcast_in_dim x0 -> x1, local copies, waits for them, and re-layouts: none -> 0.69 us  [body(): step_embed[None]]
  transfers between devices with their start and end apart: 14 -> 14, of which waited for: 8 -> 6; matrix products, arithmetic and copies ran while one was open for 0% -> 13% of each run, Pallas kernels for 0% -> 0%
where the time goes in v5:
time: 46 us; the launch traced here: 45.6 us
  Pallas kernels  15.9 us (35%)
  starting transfers between devices  13.4 us (29%)
  waiting for transfers between devices  8.44 us (18%)
  local copies, waits for them, and re-layouts  6.39 us (14%)
  other arithmetic  1.44 us (3%)
    ppermute x14, starting transfers between devices, moved(): lax.ppermute(array, 'frame', [(i, target(i) % count) for i in range(count)])  13.4 us
    ppermute x14, waiting for transfers between devices, moved(): lax.ppermute(array, 'frame', [(i, target(i) % count) for i in range(count)])  8.44 us
    pallas_call x1, Pallas kernels, attend(): pl.pallas_call(functools.partial(attend_kernel, cells, planes), out_shape...  8 us
    pallas_call x1, Pallas kernels, res_block(): pl.pallas_call(res_kernel, out_shape=jax.ShapeDtypeStruct((frames, count,...  5.72 us
    unnamed x7, local copies, waits for them, and re-layouts  2.97 us
    pallas_call x1, Pallas kernels, body(): pl.pallas_call(pack_kernel, out_shape=[jax.ShapeDtypeStruct((2, rows, pac...  2.2 us
    pad x1, local copies, waits for them, and re-layouts, body(): jnp.pad(w_qkv, (more, (0, 0)))  1.18 us
    pad x1, local copies, waits for them, and re-layouts, body(): jnp.pad(w_out, (more, (0, 0)))  0.97 us
  transfers between devices with their start and end apart: 14, of which 6 were waited for; matrix products, arithmetic and copies ran while one was open for 13% of the time, Pallas kernels for 0%

profile of v5, /device:TPU:0, one launch (start us, length us, event | category | flops | bytes accessed | tf_op | source)
XLA Modules:
  0.0 45.6 jit_solution(7188904631103748694)
XLA Ops:
  0.0 2.2 %norm_pack.1 = (bf16[2,64,640]{2,1,0:T(8,128)(2,1)}, bf16[2,64,640]{2,1,0:T(8,128)(2,1)}) custom-call(bf16[4,4,32,320]{3,2,1,0:T(8,128)(2,1)} %bitcast.5, f32[320]{0:T(512)} %gain_ref.1), custom_call_target="tpu_custom_call" | custom-call | tf_op jit(solution)/shard_map/norm_pack/pallas_call | solution.py:347
  2.2 5.0 %collective-permute-start.7 = (bf16[2,64,640]{2,1,0:T(8,128)(2,1)}, bf16[2,64,640]{2,1,0:T(8,128)(2,1)S(1)}, u32[]{:S(2)}, u32[]{:S(2)}) collective-permute-start(bf16[2,64,640]{2,1,0:T(8,128)(2,1)} %get-tuple-element.23), channel_id=1, source_target_pairs={{0,12},{1,13},{2,14},{3,15},{4,0},{5,1},{6,2},{7,3},{8,4},{9,5},{1... | collective-permute-start | bytes 491528 | tf_op jit(solution)/shard_map/ppermute | solution.py:31
  7.3 4.8 %collective-permute-start.9 = (bf16[2,64,640]{2,1,0:T(8,128)(2,1)}, bf16[2,64,640]{2,1,0:T(8,128)(2,1)S(1)}, u32[]{:S(2)}, u32[]{:S(2)}) collective-permute-start(bf16[2,64,640]{2,1,0:T(8,128)(2,1)} %get-tuple-element.24), channel_id=1, source_target_pairs={{0,14},{1,15},{2,12},{3,13},{4,2},{5,3},{6,0},{7,1},{8,6},{9,7},{1... | collective-permute-start | bytes 491528 | tf_op jit(solution)/shard_map/ppermute | solution.py:31
  12.0 0.5 %collective-permute-start.1 = (bf16[2,64,640]{2,1,0:T(8,128)(2,1)}, bf16[2,64,640]{2,1,0:T(8,128)(2,1)S(1)}, u32[]{:S(2)}, u32[]{:S(2)}) collective-permute-start(bf16[2,64,640]{2,1,0:T(8,128)(2,1)} %get-tuple-element.24), channel_id=1, source_target_pairs={{0,2},{1,3},{2,0},{3,1},{4,6},{5,7},{6,4},{7,5},{8,10},{9,11},{10,... | collective-permute-start | bytes 491528 | tf_op jit(solution)/shard_map/ppermute | solution.py:31
  12.5 0.7 %pad_add_fusion.refs_12_ = s32[32]{0:T(128)S(1)} fusion(s32[16]{0:T(128)} %param.19, s32[16]{0:T(128)} %param.18), kind=kLoop, calls=%fused_computation.2 | loop fusion | flops 32 | bytes 256 | tf_op jit(solution)/shard_map/concatenate | solution.py:365
  13.3 1.0 %copy.13 = bf16[4,2,64,320]{3,2,0,1:T(8,128)(2,1)S(1)} copy(bf16[4,2,64,320]{3,2,1,0:T(8,128)(2,1)} %param.10) | data formatting | bytes 655360 | tf_op args[0]
  14.3 0.7 %broadcast_in_dim.3 = f32[1,320]{1,0:T(1,128)S(1)} reshape(f32[320]{0:T(512)} %param.17) | data formatting | bytes 2560 | tf_op jit(solution)/shard_map/broadcast_in_dim | solution.py:368
  15.0 0.7 %pad_maximum_fusion.refs_6_ = f32[3,320]{1,0:T(4,128)S(1)} fusion(f32[1,320]{1,0:T(1,128)S(1)} %broadcast_in_dim.3, f32[2,320]{1,0:T(2,128)} %param.14), kind=kLoop, calls=%fused_computation.1 | loop fusion | flops 960 | bytes 7680 | tf_op jit(solution)/shard_map/concatenate | solution.py:368
  15.7 1.0 %pad.16.refs_5_ = bf16[384,320]{1,0:T(8,128)(2,1)S(1)} pad(bf16[320,320]{1,0:T(8,128)(2,1)} %param.13, bf16[]{:T(256)} %constant.2.clone.1), padding=0_64x0_0 | pad | bytes 450562 | tf_op jit(solution)/shard_map/jit(_pad)/pad | solution.py:367
  16.7 1.2 %pad.15.refs_13_ = bf16[384,960]{1,0:T(8,128)(2,1)S(1)} pad(bf16[320,960]{1,0:T(8,128)(2,1)} %param.12, bf16[]{:T(256)} %constant.2.clone.1), padding=0_64x0_0 | pad | bytes 1351682 | tf_op jit(solution)/shard_map/jit(_pad)/pad | solution.py:364
  17.9 0.3 pad.17.refs_7_
  18.2 1.3 %copy-done.1 = bf16[3,3,320,320]{3,2,1,0:T(8,128)(2,1)S(1)} copy-done((bf16[3,3,320,320]{3,2,1,0:T(8,128)(2,1)S(1)}, bf16[3,3,320,320]{3,2,1,0:T(8,128)(2,1)}, u32[]{:S(2)}) %copy-start.1) | copy-done | bytes 1843224
  19.8 0.6 %copy-done.2 = bf16[2,64,640]{2,1,0:T(8,128)(2,1)S(1)} copy-done((bf16[2,64,640]{2,1,0:T(8,128)(2,1)S(1)}, bf16[2,64,640]{2,1,0:T(8,128)(2,1)}, u32[]{:S(2)}) %copy-start.2) | copy-done | bytes 163864
  20.4 3.0 %collective-permute-done.3.refs_6_ = bf16[2,64,640]{2,1,0:T(8,128)(2,1)S(1)} collective-permute-done((bf16[2,64,640]{2,1,0:T(8,128)(2,1)}, bf16[2,64,640]{2,1,0:T(8,128)(2,1)S(1)}, u32[]{:S(2)}, u32[]{:S(2)}) %collective-permute-start.3) | collective-permute-done | bytes 163872 | tf_op jit(solution)/shard_map/ppermute | solution.py:31
  23.4 0.5 %collective-permute-start.5 = (bf16[2,64,640]{2,1,0:T(8,128)(2,1)S(1)}, bf16[2,64,640]{2,1,0:T(8,128)(2,1)S(1)}, u32[]{:S(2)}, u32[]{:S(2)}) collective-permute-start(bf16[2,64,640]{2,1,0:T(8,128)(2,1)S(1)} %collective-permute-done.2.refs_4_), channel_id=1, source_target_pairs={{0,1},{1,0},{2,3},{3,2},{4,5},{5,4},{6,7},{7,6},{8,9},{9,8},{10,11... | collective-permute-start | bytes 491528 | tf_op jit(solution)/shard_map/ppermute | solution.py:31
  24.0 0.5 %collective-permute-start.10 = (bf16[2,64,640]{2,1,0:T(8,128)(2,1)S(1)}, bf16[2,64,640]{2,1,0:T(8,128)(2,1)S(1)}, u32[]{:S(2)}, u32[]{:S(2)}) collective-permute-start(bf16[2,64,640]{2,1,0:T(8,128)(2,1)S(1)} %collective-permute-done.9.refs_10_), channel_id=1, source_target_pairs={{0,1},{1,0},{2,3},{3,2},{4,5},{5,4},{6,7},{7,6},{8,9},{9,8},{10,11... | collective-permute-start | bytes 491528 | tf_op jit(solution)/shard_map/ppermute | solution.py:31
  24.6 0.8 %collective-permute-done.8.refs_9_ = bf16[2,64,640]{2,1,0:T(8,128)(2,1)S(1)} collective-permute-done((bf16[2,64,640]{2,1,0:T(8,128)(2,1)S(1)}, bf16[2,64,640]{2,1,0:T(8,128)(2,1)S(1)}, u32[]{:S(2)}, u32[]{:S(2)}) %collective-permute-start.8) | collective-permute-done | bytes 163872 | tf_op jit(solution)/shard_map/ppermute | solution.py:31
  25.9 8.0 %window_attention.1 = (bf16[64,640]{1,0:T(8,128)(2,1)S(1)}, bf16[64,640]{1,0:T(8,128)(2,1)S(1)}, bf16[64,640]{1,0:T(8,128)(2,1)S(1)}, bf16[64,640]{1,0:T(8,128)(2,1)S(1)}) custom-call(bf16[1,64,640]{2,1,0:T(8,128)(2,1)S(1)} %slice.3.refs_0_, bf16[2,64,640]{2,1,0:T(8,128)(2,1)S(1)} %collective-permute-done.refs_1_, ...), custom_call_target="tpu_custom_call" | custom-call | tf_op jit(solution)/shard_map/window_attention/pallas_call | solution.py:212
  33.9 0.3 collective-permute-start.11
  34.2 0.5 %collective-permute-start.12 = (bf16[64,640]{1,0:T(8,128)(2,1)S(1)}, bf16[64,640]{1,0:T(8,128)(2,1)S(1)}, u32[]{:S(2)}, u32[]{:S(2)}) collective-permute-start(bf16[64,640]{1,0:T(8,128)(2,1)S(1)} %get-tuple-element.32), channel_id=1, source_target_pairs={{0,2},{1,3},{2,0},{3,1},{4,6},{5,7},{6,4},{7,5},{8,10},{9,11},{10,... | collective-permute-start | bytes 245768 | tf_op jit(solution)/shard_map/ppermute | solution.py:31
  34.7 1.1 %collective-permute-start.13 = (bf16[64,640]{1,0:T(8,128)(2,1)S(1)}, bf16[64,640]{1,0:T(8,128)(2,1)S(1)}, u32[]{:S(2)}, u32[]{:S(2)}) collective-permute-start(bf16[64,640]{1,0:T(8,128)(2,1)S(1)} %get-tuple-element.33), channel_id=1, source_target_pairs={{0,3},{1,2},{2,1},{3,0},{4,7},{5,6},{6,5},{7,4},{8,11},{9,10},{10,... | collective-permute-start | bytes 245768 | tf_op jit(solution)/shard_map/ppermute | solution.py:31
  35.8 3.6 %collective-permute-done.12.refs_2_ = bf16[64,640]{1,0:T(8,128)(2,1)S(1)} collective-permute-done((bf16[64,640]{1,0:T(8,128)(2,1)S(1)}, bf16[64,640]{1,0:T(8,128)(2,1)S(1)}, u32[]{:S(2)}, u32[]{:S(2)}) %collective-permute-start.12) | collective-permute-done | bytes 81952 | tf_op jit(solution)/shard_map/ppermute | solution.py:31
  39.4 0.5 %collective-permute-done.13.refs_3_ = bf16[64,640]{1,0:T(8,128)(2,1)S(1)} collective-permute-done((bf16[64,640]{1,0:T(8,128)(2,1)S(1)}, bf16[64,640]{1,0:T(8,128)(2,1)S(1)}, u32[]{:S(2)}, u32[]{:S(2)}) %collective-permute-start.13) | collective-permute-done | bytes 81952 | tf_op jit(solution)/shard_map/ppermute | solution.py:31
  39.9 5.7 %res_block.1 = bf16[4,2,64,320]{3,2,1,0:T(8,128)(2,1)} custom-call(bf16[64,640]{1,0:T(8,128)(2,1)S(1)} %get-tuple-element.30.refs_0_, bf16[64,640]{1,0:T(8,128)(2,1)S(1)} %collective-permute-done.11.refs_1_, bf16[64,640]{1,0:T(8,128)(2,1)S(1)} %collective-permute-done.12.refs_2_, bf16[64,640]{1,0:T(8,128)(2,1)S(1)} %collective-permute-done.13.refs_3_, ...), custom_call_target="tpu_custom_call" | custom-call | tf_op jit(solution)/shard_map/res_block/pallas_call | solution.py:322
  (22 shorter events, 0.9 us)
Async XLA Ops:
  0.0 17.9 %copy-start = (bf16[3,3,320,320]{3,2,1,0:T(8,128)(2,1)S(1)}, bf16[3,3,320,320]{3,2,1,0:T(8,128)(2,1)}, u32[]{:S(2)}) copy-start(bf16[3,3,320,320]{3,2,1,0:T(8,128)(2,1)} %param.15) | copy-start | bytes 5529604
  2.2 21.8 %collective-permute-start.7 = (bf16[2,64,640]{2,1,0:T(8,128)(2,1)}, bf16[2,64,640]{2,1,0:T(8,128)(2,1)S(1)}, u32[]{:S(2)}, u32[]{:S(2)}) collective-permute-start(bf16[2,64,640]{2,1,0:T(8,128)(2,1)} %get-tuple-element.23), channel_id=1, source_target_pairs={{0,12},{1,13},{2,14},{3,15},{4,0},{5,1},{6,2},{7,3},{8,4},{9,5},{1... | collective-permute-start | bytes 491528 | tf_op jit(solution)/shard_map/ppermute | solution.py:31
  7.2 12.6 %collective-permute-start.2 = (bf16[2,64,640]{2,1,0:T(8,128)(2,1)}, bf16[2,64,640]{2,1,0:T(8,128)(2,1)S(1)}, u32[]{:S(2)}, u32[]{:S(2)}) collective-permute-start(bf16[2,64,640]{2,1,0:T(8,128)(2,1)} %get-tuple-element.23), channel_id=1, source_target_pairs={{0,4},{1,5},{2,6},{3,7},{4,8},{5,9},{6,10},{7,11},{8,12},{9,13},{1... | collective-permute-start | bytes 491528 | tf_op jit(solution)/shard_map/ppermute | solution.py:31
  7.3 16.7 %collective-permute-start.9 = (bf16[2,64,640]{2,1,0:T(8,128)(2,1)}, bf16[2,64,640]{2,1,0:T(8,128)(2,1)S(1)}, u32[]{:S(2)}, u32[]{:S(2)}) collective-permute-start(bf16[2,64,640]{2,1,0:T(8,128)(2,1)} %get-tuple-element.24), channel_id=1, source_target_pairs={{0,14},{1,15},{2,12},{3,13},{4,2},{5,3},{6,0},{7,1},{8,6},{9,7},{1... | collective-permute-start | bytes 491528 | tf_op jit(solution)/shard_map/ppermute | solution.py:31
  12.0 11.4 %collective-permute-start.3 = (bf16[2,64,640]{2,1,0:T(8,128)(2,1)}, bf16[2,64,640]{2,1,0:T(8,128)(2,1)S(1)}, u32[]{:S(2)}, u32[]{:S(2)}) collective-permute-start(bf16[2,64,640]{2,1,0:T(8,128)(2,1)} %get-tuple-element.24), channel_id=1, source_target_pairs={{0,6},{1,7},{2,4},{3,5},{4,10},{5,11},{6,8},{7,9},{8,14},{9,15},{1... | collective-permute-start | bytes 491528 | tf_op jit(solution)/shard_map/ppermute | solution.py:31
  12.0 11.4 %collective-permute-start.1 = (bf16[2,64,640]{2,1,0:T(8,128)(2,1)}, bf16[2,64,640]{2,1,0:T(8,128)(2,1)S(1)}, u32[]{:S(2)}, u32[]{:S(2)}) collective-permute-start(bf16[2,64,640]{2,1,0:T(8,128)(2,1)} %get-tuple-element.24), channel_id=1, source_target_pairs={{0,2},{1,3},{2,0},{3,1},{4,6},{5,7},{6,4},{7,5},{8,10},{9,11},{10,... | collective-permute-start | bytes 491528 | tf_op jit(solution)/shard_map/ppermute | solution.py:31
  17.9 1.6 %copy-start.1 = (bf16[3,3,320,320]{3,2,1,0:T(8,128)(2,1)S(1)}, bf16[3,3,320,320]{3,2,1,0:T(8,128)(2,1)}, u32[]{:S(2)}) copy-start(bf16[3,3,320,320]{3,2,1,0:T(8,128)(2,1)} %param.16) | copy-start | bytes 5529604
  19.5 0.9 %copy-start.2 = (bf16[2,64,640]{2,1,0:T(8,128)(2,1)S(1)}, bf16[2,64,640]{2,1,0:T(8,128)(2,1)}, u32[]{:S(2)}) copy-start(bf16[2,64,640]{2,1,0:T(8,128)(2,1)} %get-tuple-element.23) | copy-start | bytes 491524
  20.4 4.1 %collective-permute-start = (bf16[2,64,640]{2,1,0:T(8,128)(2,1)S(1)}, bf16[2,64,640]{2,1,0:T(8,128)(2,1)S(1)}, u32[]{:S(2)}, u32[]{:S(2)}) collective-permute-start(bf16[2,64,640]{2,1,0:T(8,128)(2,1)S(1)} %copy-done.2), channel_id=1, source_target_pairs={{0,1},{1,0},{2,3},{3,2},{4,5},{5,4},{6,7},{7,6},{8,9},{9,8},{10,11... | collective-permute-start | bytes 491528 | tf_op jit(solution)/shard_map/ppermute | solution.py:31
  23.4 2.1 %collective-permute-start.4 = (bf16[2,64,640]{2,1,0:T(8,128)(2,1)S(1)}, bf16[2,64,640]{2,1,0:T(8,128)(2,1)S(1)}, u32[]{:S(2)}, u32[]{:S(2)}) collective-permute-start(bf16[2,64,640]{2,1,0:T(8,128)(2,1)S(1)} %collective-permute-done.1.refs_2_), channel_id=1, source_target_pairs={{0,1},{1,0},{2,3},{3,2},{4,5},{5,4},{6,7},{7,6},{8,9},{9,8},{10,11... | collective-permute-start | bytes 491528 | tf_op jit(solution)/shard_map/ppermute | solution.py:31
  23.4 2.1 %collective-permute-start.5 = (bf16[2,64,640]{2,1,0:T(8,128)(2,1)S(1)}, bf16[2,64,640]{2,1,0:T(8,128)(2,1)S(1)}, u32[]{:S(2)}, u32[]{:S(2)}) collective-permute-start(bf16[2,64,640]{2,1,0:T(8,128)(2,1)S(1)} %collective-permute-done.2.refs_4_), channel_id=1, source_target_pairs={{0,1},{1,0},{2,3},{3,2},{4,5},{5,4},{6,7},{7,6},{8,9},{9,8},{10,11... | collective-permute-start | bytes 491528 | tf_op jit(solution)/shard_map/ppermute | solution.py:31
  24.0 1.4 %collective-permute-start.8 = (bf16[2,64,640]{2,1,0:T(8,128)(2,1)S(1)}, bf16[2,64,640]{2,1,0:T(8,128)(2,1)S(1)}, u32[]{:S(2)}, u32[]{:S(2)}) collective-permute-start(bf16[2,64,640]{2,1,0:T(8,128)(2,1)S(1)} %collective-permute-done.7.refs_8_), channel_id=1, source_target_pairs={{0,1},{1,0},{2,3},{3,2},{4,5},{5,4},{6,7},{7,6},{8,9},{9,8},{10,11... | collective-permute-start | bytes 491528 | tf_op jit(solution)/shard_map/ppermute | solution.py:31
  24.0 1.6 %collective-permute-start.10 = (bf16[2,64,640]{2,1,0:T(8,128)(2,1)S(1)}, bf16[2,64,640]{2,1,0:T(8,128)(2,1)S(1)}, u32[]{:S(2)}, u32[]{:S(2)}) collective-permute-start(bf16[2,64,640]{2,1,0:T(8,128)(2,1)S(1)} %collective-permute-done.9.refs_10_), channel_id=1, source_target_pairs={{0,1},{1,0},{2,3},{3,2},{4,5},{5,4},{6,7},{7,6},{8,9},{9,8},{10,11... | collective-permute-start | bytes 491528 | tf_op jit(solution)/shard_map/ppermute | solution.py:31
  24.5 1.4 %collective-permute-start.6 = (bf16[2,64,640]{2,1,0:T(8,128)(2,1)S(1)}, bf16[2,64,640]{2,1,0:T(8,128)(2,1)S(1)}, u32[]{:S(2)}, u32[]{:S(2)}) collective-permute-start(bf16[2,64,640]{2,1,0:T(8,128)(2,1)S(1)} %collective-permute-done.3.refs_6_), channel_id=1, source_target_pairs={{0,1},{1,0},{2,3},{3,2},{4,5},{5,4},{6,7},{7,6},{8,9},{9,8},{10,11... | collective-permute-start | bytes 491528 | tf_op jit(solution)/shard_map/ppermute | solution.py:31
  33.9 1.9 %collective-permute-start.11 = (bf16[64,640]{1,0:T(8,128)(2,1)S(1)}, bf16[64,640]{1,0:T(8,128)(2,1)S(1)}, u32[]{:S(2)}, u32[]{:S(2)}) collective-permute-start(bf16[64,640]{1,0:T(8,128)(2,1)S(1)} %get-tuple-element.31), channel_id=1, source_target_pairs={{0,1},{1,0},{2,3},{3,2},{4,5},{5,4},{6,7},{7,6},{8,9},{9,8},{10,11... | collective-permute-start | bytes 245768 | tf_op jit(solution)/shard_map/ppermute | solution.py:31
  34.2 5.3 %collective-permute-start.12 = (bf16[64,640]{1,0:T(8,128)(2,1)S(1)}, bf16[64,640]{1,0:T(8,128)(2,1)S(1)}, u32[]{:S(2)}, u32[]{:S(2)}) collective-permute-start(bf16[64,640]{1,0:T(8,128)(2,1)S(1)} %get-tuple-element.32), channel_id=1, source_target_pairs={{0,2},{1,3},{2,0},{3,1},{4,6},{5,7},{6,4},{7,5},{8,10},{9,11},{10,... | collective-permute-start | bytes 245768 | tf_op jit(solution)/shard_map/ppermute | solution.py:31
  34.7 5.2 %collective-permute-start.13 = (bf16[64,640]{1,0:T(8,128)(2,1)S(1)}, bf16[64,640]{1,0:T(8,128)(2,1)S(1)}, u32[]{:S(2)}, u32[]{:S(2)}) collective-permute-start(bf16[64,640]{1,0:T(8,128)(2,1)S(1)} %get-tuple-element.33), channel_id=1, source_target_pairs={{0,3},{1,2},{2,1},{3,0},{4,7},{5,6},{6,5},{7,4},{8,11},{9,10},{10,... | collective-permute-start | bytes 245768 | tf_op jit(solution)/shard_map/ppermute | solution.py:31

commit v6 on v5

--- a/solution.py
+++ b/solution.py
@@ -44,13 +44,6 @@
     first = chunks[:full] + [jnp.where(low, chunks[-1], 0.0)]
     second = chunks[full:-1] + [jnp.where(low, pltpu.roll(chunks[-1], LANES // 2, 1), 0.0)]
     return first, second
-
-
-def fetch(pairs, sem):
-    copies = [pltpu.make_async_copy(src, dst, sem.at[i]) for i, (src, dst) in enumerate(pairs)]
-    for copy in copies:
-        copy.start()
-    return copies
 
 
 def pack_kernel(lat_ref, gain_ref, near_ref, far_ref):
@@ -76,13 +69,13 @@
     sources, refs = refs[:12], refs[12:]
     ints_hbm, w_ref, own_ref, sib_ref, far_own_ref, far_sib_ref = refs[:6]
     (
-        ints_ref, part_ref, norm_ref, q_ref, k_ref, v_ref, bias_ref, coef_ref, acc_ref, sem,
+        ints_ref, norm_ref, q_ref, k_ref, v_ref, bias_ref, coef_ref, acc_ref, sem,
     ) = refs[6:]
     core, chip, plane = place()
     channels = own_ref.shape[1] // PACK
     head_dim = channels // HEADS
     half = cells // PACK
-    part_rows = part_ref.shape[1]
+    part_rows = sources[1].shape[1]
     part_frames = part_rows // half
     key_frames, query_frames = part_frames * 12, part_frames * 4
     key_rows, query_rows = key_frames * half, query_frames * half
@@ -91,19 +84,13 @@
     group = GROUP
     wide = group * HEADS * query_frames
     chunks, lanes = k_ref.shape[0], k_ref.shape[2]
-    copies = fetch(
-        [(src.at[i % 2], part_ref.at[i]) for i, src in enumerate(sources)]
-        + [(ints_hbm, ints_ref)],
-        sem,
-    )
+    copy = pltpu.make_async_copy(ints_hbm, ints_ref, sem)
+    copy.start()
 
     for i in range(len(sources)):
-        copies[i].wait()
-        for a, x in enumerate(unpack_lanes(part_ref[i].astype(jnp.float32))):
+        for a, x in enumerate(unpack_lanes(sources[i][i % 2].astype(jnp.float32))):
             start = a * key_rows + i * part_rows
             norm_ref[start : start + part_rows] = jnp.concatenate(x, 1).astype(jnp.bfloat16)
-    for copy in copies[len(sources) :]:
-        copy.wait()
     pad = jnp.zeros((chunks * lanes, chunks * lanes - channels), jnp.bfloat16)
     for i, (out_ref, rows) in enumerate(((q_ref, query_rows), (k_ref, key_rows), (v_ref, key_rows))):
         w = jnp.concatenate([w_ref[:, i * channels : (i + 1) * channels], pad], 1)
@@ -113,6 +100,7 @@
             for j in range(chunks):
                 out_ref[j, a * rows : (a + 1) * rows] = res[:, j * lanes : (j + 1) * lanes]
 
+    copy.wait()
     ids = []
     for step in (0, planes - 1, 1):
         for tall in (chip, 1 - chip):
@@ -212,11 +200,10 @@
     return pl.pallas_call(
         functools.partial(attend_kernel, cells, planes),
         out_shape=[jax.ShapeDtypeStruct((rows, packed), jnp.bfloat16)] * 4,
-        in_specs=[pl.BlockSpec(memory_space=pl.ANY)] * 13 + [vmem],
+        in_specs=[vmem] * 12 + [pl.BlockSpec(memory_space=pl.ANY), vmem],
         out_specs=[vmem] * 4,
         scratch_shapes=[
             pltpu.SMEM(ints.shape, jnp.int32),
-            pltpu.VMEM((12, rows, packed), jnp.bfloat16),
             pltpu.VMEM((keys, chunks * LANES), jnp.bfloat16),
             pltpu.VMEM((chunks, queries, LANES), jnp.float32),
             pltpu.VMEM((chunks, keys, LANES), jnp.float32),
@@ -224,7 +211,7 @@
             pltpu.VMEM((REACH + 1, 3 * query_frames, wide), jnp.float32),
             pltpu.VMEM((REACH + 1, 1, wide), jnp.float32),
             pltpu.VMEM((chunks, queries, LANES), jnp.float32),
-            pltpu.SemaphoreType.DMA((13,)),
+            pltpu.SemaphoreType.DMA,
         ],
         compiler_params=pltpu.CompilerParams(vmem_limit_bytes=30 * 1024 * 1024),
         name="window_attention",
@@ -232,12 +219,12 @@
 
 
 def group_mean(sums, spread, count):
-    high = sums.astype(jnp.bfloat16)
-    left = sums - high.astype(jnp.float32)
-    mid = left.astype(jnp.bfloat16)
-    low = (left - mid.astype(jnp.float32)).astype(jnp.bfloat16)
-    dot = functools.partial(jnp.dot, preferred_element_type=jnp.float32)
-    return (dot(high, spread) + dot(mid, spread) + dot(low, spread)) * (1.0 / count)
+    rows = sums.shape[0]
+    high = sums.astype(jnp.bfloat16).astype(jnp.float32)
+    mid = (sums - high).astype(jnp.bfloat16).astype(jnp.float32)
+    parts = jnp.concatenate([high, mid, sums - high - mid], 0).astype(jnp.bfloat16)
+    full = jnp.dot(parts, spread, preferred_element_type=jnp.float32)
+    return (full[:rows] + full[rows : 2 * rows] + full[2 * rows :]) * (1.0 / count)
 
 
 def group_act(rows, gain, spread, count):

time: 46 us -> 43.3 us (0.941)
  Pallas kernels: 15.9 us -> 13.2 us
    pallas_call x1, Pallas kernels: 8 us -> 5.75 us  [attend(): pl.pallas_call(functools.partial(attend_kernel, cells, planes), out_shape...]
    pallas_call x1, Pallas kernels: 5.72 us -> 5.23 us  [res_block(): pl.pallas_call(res_kernel, out_shape=jax.ShapeDtypeStruct((frames, count,...]
  transfers between devices with their start and end apart: 14 -> 14, of which waited for: 6 -> 6; matrix products, arithmetic and copies ran while one was open for 13% -> 14% of each run, Pallas kernels for 0% -> 0%
where the time goes in v6:
time: 43.3 us; the launch traced here: 42.9 us
  starting transfers between devices  13.4 us (31%)
  Pallas kernels  13.2 us (30%)
  waiting for transfers between devices  8.44 us (19%)
  local copies, waits for them, and re-layouts  6.39 us (15%)
  other arithmetic  1.44 us (3%)
    ppermute x14, starting transfers between devices, moved(): lax.ppermute(array, 'frame', [(i, target(i) % count) for i in range(count)])  13.4 us
    ppermute x14, waiting for transfers between devices, moved(): lax.ppermute(array, 'frame', [(i, target(i) % count) for i in range(count)])  8.44 us
    pallas_call x1, Pallas kernels, attend(): pl.pallas_call(functools.partial(attend_kernel, cells, planes), out_shape...  5.75 us
    pallas_call x1, Pallas kernels, res_block(): pl.pallas_call(res_kernel, out_shape=jax.ShapeDtypeStruct((frames, count,...  5.23 us
    unnamed x7, local copies, waits for them, and re-layouts  2.97 us
    pallas_call x1, Pallas kernels, body(): pl.pallas_call(pack_kernel, out_shape=[jax.ShapeDtypeStruct((2, rows, pac...  2.2 us
    pad x1, local copies, waits for them, and re-layouts, body(): jnp.pad(w_qkv, (more, (0, 0)))  1.18 us
    pad x1, local copies, waits for them, and re-layouts, body(): jnp.pad(w_out, (more, (0, 0)))  0.97 us
  transfers between devices with their start and end apart: 14, of which 6 were waited for; matrix products, arithmetic and copies ran while one was open for 14% of the time, Pallas kernels for 0%

profile of v6, /device:TPU:0, one launch (start us, length us, event | category | flops | bytes accessed | tf_op | source)
XLA Modules:
  0.0 42.9 jit_solution(12122221058259318341)
XLA Ops:
  0.0 2.2 %norm_pack.1 = (bf16[2,64,640]{2,1,0:T(8,128)(2,1)}, bf16[2,64,640]{2,1,0:T(8,128)(2,1)}) custom-call(bf16[4,4,32,320]{3,2,1,0:T(8,128)(2,1)} %bitcast.5, f32[320]{0:T(512)} %gain_ref.1), custom_call_target="tpu_custom_call" | custom-call | tf_op jit(solution)/shard_map/norm_pack/pallas_call | solution.py:334
  2.2 5.0 %collective-permute-start.7 = (bf16[2,64,640]{2,1,0:T(8,128)(2,1)}, bf16[2,64,640]{2,1,0:T(8,128)(2,1)S(1)}, u32[]{:S(2)}, u32[]{:S(2)}) collective-permute-start(bf16[2,64,640]{2,1,0:T(8,128)(2,1)} %get-tuple-element.23), channel_id=1, source_target_pairs={{0,12},{1,13},{2,14},{3,15},{4,0},{5,1},{6,2},{7,3},{8,4},{9,5},{1... | collective-permute-start | bytes 491528 | tf_op jit(solution)/shard_map/ppermute | solution.py:31
  7.3 4.8 %collective-permute-start.9 = (bf16[2,64,640]{2,1,0:T(8,128)(2,1)}, bf16[2,64,640]{2,1,0:T(8,128)(2,1)S(1)}, u32[]{:S(2)}, u32[]{:S(2)}) collective-permute-start(bf16[2,64,640]{2,1,0:T(8,128)(2,1)} %get-tuple-element.24), channel_id=1, source_target_pairs={{0,14},{1,15},{2,12},{3,13},{4,2},{5,3},{6,0},{7,1},{8,6},{9,7},{1... | collective-permute-start | bytes 491528 | tf_op jit(solution)/shard_map/ppermute | solution.py:31
  12.0 0.5 %collective-permute-start.1 = (bf16[2,64,640]{2,1,0:T(8,128)(2,1)}, bf16[2,64,640]{2,1,0:T(8,128)(2,1)S(1)}, u32[]{:S(2)}, u32[]{:S(2)}) collective-permute-start(bf16[2,64,640]{2,1,0:T(8,128)(2,1)} %get-tuple-element.24), channel_id=1, source_target_pairs={{0,2},{1,3},{2,0},{3,1},{4,6},{5,7},{6,4},{7,5},{8,10},{9,11},{10,... | collective-permute-start | bytes 491528 | tf_op jit(solution)/shard_map/ppermute | solution.py:31
  12.5 0.7 %pad_add_fusion.refs_12_ = s32[32]{0:T(128)S(1)} fusion(s32[16]{0:T(128)} %param.19, s32[16]{0:T(128)} %param.18), kind=kLoop, calls=%fused_computation.2 | loop fusion | flops 32 | bytes 256 | tf_op jit(solution)/shard_map/concatenate | solution.py:352
  13.3 1.0 %copy.13 = bf16[4,2,64,320]{3,2,0,1:T(8,128)(2,1)S(1)} copy(bf16[4,2,64,320]{3,2,1,0:T(8,128)(2,1)} %param.10) | data formatting | bytes 655360 | tf_op args[0]
  14.3 0.7 %broadcast_in_dim.3 = f32[1,320]{1,0:T(1,128)S(1)} reshape(f32[320]{0:T(512)} %param.17) | data formatting | bytes 2560 | tf_op jit(solution)/shard_map/broadcast_in_dim | solution.py:355
  15.0 0.7 %pad_maximum_fusion.refs_6_ = f32[3,320]{1,0:T(4,128)S(1)} fusion(f32[1,320]{1,0:T(1,128)S(1)} %broadcast_in_dim.3, f32[2,320]{1,0:T(2,128)} %param.14), kind=kLoop, calls=%fused_computation.1 | loop fusion | flops 960 | bytes 7680 | tf_op jit(solution)/shard_map/concatenate | solution.py:355
  15.7 1.0 %pad.16.refs_5_ = bf16[384,320]{1,0:T(8,128)(2,1)S(1)} pad(bf16[320,320]{1,0:T(8,128)(2,1)} %param.13, bf16[]{:T(256)} %constant.2.clone.1), padding=0_64x0_0 | pad | bytes 450562 | tf_op jit(solution)/shard_map/jit(_pad)/pad | solution.py:354
  16.7 1.2 %pad.15.refs_13_ = bf16[384,960]{1,0:T(8,128)(2,1)S(1)} pad(bf16[320,960]{1,0:T(8,128)(2,1)} %param.12, bf16[]{:T(256)} %constant.2.clone.1), padding=0_64x0_0 | pad | bytes 1351682 | tf_op jit(solution)/shard_map/jit(_pad)/pad | solution.py:351
  17.9 0.3 pad.17.refs_7_
  18.2 1.3 %copy-done.1 = bf16[3,3,320,320]{3,2,1,0:T(8,128)(2,1)S(1)} copy-done((bf16[3,3,320,320]{3,2,1,0:T(8,128)(2,1)S(1)}, bf16[3,3,320,320]{3,2,1,0:T(8,128)(2,1)}, u32[]{:S(2)}) %copy-start.1) | copy-done | bytes 1843224
  19.8 0.6 %copy-done.2 = bf16[2,64,640]{2,1,0:T(8,128)(2,1)S(1)} copy-done((bf16[2,64,640]{2,1,0:T(8,128)(2,1)S(1)}, bf16[2,64,640]{2,1,0:T(8,128)(2,1)}, u32[]{:S(2)}) %copy-start.2) | copy-done | bytes 163864
  20.4 3.0 %collective-permute-done.3.refs_6_ = bf16[2,64,640]{2,1,0:T(8,128)(2,1)S(1)} collective-permute-done((bf16[2,64,640]{2,1,0:T(8,128)(2,1)}, bf16[2,64,640]{2,1,0:T(8,128)(2,1)S(1)}, u32[]{:S(2)}, u32[]{:S(2)}) %collective-permute-start.3) | collective-permute-done | bytes 163872 | tf_op jit(solution)/shard_map/ppermute | solution.py:31
  23.4 0.5 %collective-permute-start.5 = (bf16[2,64,640]{2,1,0:T(8,128)(2,1)S(1)}, bf16[2,64,640]{2,1,0:T(8,128)(2,1)S(1)}, u32[]{:S(2)}, u32[]{:S(2)}) collective-permute-start(bf16[2,64,640]{2,1,0:T(8,128)(2,1)S(1)} %collective-permute-done.2.refs_4_), channel_id=1, source_target_pairs={{0,1},{1,0},{2,3},{3,2},{4,5},{5,4},{6,7},{7,6},{8,9},{9,8},{10,11... | collective-permute-start | bytes 491528 | tf_op jit(solution)/shard_map/ppermute | solution.py:31
  24.0 0.5 %collective-permute-start.10 = (bf16[2,64,640]{2,1,0:T(8,128)(2,1)S(1)}, bf16[2,64,640]{2,1,0:T(8,128)(2,1)S(1)}, u32[]{:S(2)}, u32[]{:S(2)}) collective-permute-start(bf16[2,64,640]{2,1,0:T(8,128)(2,1)S(1)} %collective-permute-done.9.refs_10_), channel_id=1, source_target_pairs={{0,1},{1,0},{2,3},{3,2},{4,5},{5,4},{6,7},{7,6},{8,9},{9,8},{10,11... | collective-permute-start | bytes 491528 | tf_op jit(solution)/shard_map/ppermute | solution.py:31
  24.6 0.8 %collective-permute-done.8.refs_9_ = bf16[2,64,640]{2,1,0:T(8,128)(2,1)S(1)} collective-permute-done((bf16[2,64,640]{2,1,0:T(8,128)(2,1)S(1)}, bf16[2,64,640]{2,1,0:T(8,128)(2,1)S(1)}, u32[]{:S(2)}, u32[]{:S(2)}) %collective-permute-start.8) | collective-permute-done | bytes 163872 | tf_op jit(solution)/shard_map/ppermute | solution.py:31
  25.9 5.8 %window_attention.1 = (bf16[64,640]{1,0:T(8,128)(2,1)S(1)}, bf16[64,640]{1,0:T(8,128)(2,1)S(1)}, bf16[64,640]{1,0:T(8,128)(2,1)S(1)}, bf16[64,640]{1,0:T(8,128)(2,1)S(1)}) custom-call(bf16[1,64,640]{2,1,0:T(8,128)(2,1)S(1)} %slice.3.refs_0_, bf16[2,64,640]{2,1,0:T(8,128)(2,1)S(1)} %collective-permute-done.refs_1_, ...), custom_call_target="tpu_custom_call" | custom-call | tf_op jit(solution)/shard_map/window_attention/pallas_call | solution.py:200
  31.6 0.3 collective-permute-start.11
  31.9 0.5 %collective-permute-start.12 = (bf16[64,640]{1,0:T(8,128)(2,1)S(1)}, bf16[64,640]{1,0:T(8,128)(2,1)S(1)}, u32[]{:S(2)}, u32[]{:S(2)}) collective-permute-start(bf16[64,640]{1,0:T(8,128)(2,1)S(1)} %get-tuple-element.32), channel_id=1, source_target_pairs={{0,2},{1,3},{2,0},{3,1},{4,6},{5,7},{6,4},{7,5},{8,10},{9,11},{10,... | collective-permute-start | bytes 245768 | tf_op jit(solution)/shard_map/ppermute | solution.py:31
  32.4 1.1 %collective-permute-start.13 = (bf16[64,640]{1,0:T(8,128)(2,1)S(1)}, bf16[64,640]{1,0:T(8,128)(2,1)S(1)}, u32[]{:S(2)}, u32[]{:S(2)}) collective-permute-start(bf16[64,640]{1,0:T(8,128)(2,1)S(1)} %get-tuple-element.33), channel_id=1, source_target_pairs={{0,3},{1,2},{2,1},{3,0},{4,7},{5,6},{6,5},{7,4},{8,11},{9,10},{10,... | collective-permute-start | bytes 245768 | tf_op jit(solution)/shard_map/ppermute | solution.py:31
  33.6 3.6 %collective-permute-done.12.refs_2_ = bf16[64,640]{1,0:T(8,128)(2,1)S(1)} collective-permute-done((bf16[64,640]{1,0:T(8,128)(2,1)S(1)}, bf16[64,640]{1,0:T(8,128)(2,1)S(1)}, u32[]{:S(2)}, u32[]{:S(2)}) %collective-permute-start.12) | collective-permute-done | bytes 81952 | tf_op jit(solution)/shard_map/ppermute | solution.py:31
  37.2 0.5 %collective-permute-done.13.refs_3_ = bf16[64,640]{1,0:T(8,128)(2,1)S(1)} collective-permute-done((bf16[64,640]{1,0:T(8,128)(2,1)S(1)}, bf16[64,640]{1,0:T(8,128)(2,1)S(1)}, u32[]{:S(2)}, u32[]{:S(2)}) %collective-permute-start.13) | collective-permute-done | bytes 81952 | tf_op jit(solution)/shard_map/ppermute | solution.py:31
  37.7 5.2 %res_block.1 = bf16[4,2,64,320]{3,2,1,0:T(8,128)(2,1)} custom-call(bf16[64,640]{1,0:T(8,128)(2,1)S(1)} %get-tuple-element.30.refs_0_, bf16[64,640]{1,0:T(8,128)(2,1)S(1)} %collective-permute-done.11.refs_1_, bf16[64,640]{1,0:T(8,128)(2,1)S(1)} %collective-permute-done.12.refs_2_, bf16[64,640]{1,0:T(8,128)(2,1)S(1)} %collective-permute-done.13.refs_3_, ...), custom_call_target="tpu_custom_call" | custom-call | tf_op jit(solution)/shard_map/res_block/pallas_call | solution.py:309
  (22 shorter events, 0.9 us)
Async XLA Ops:
  0.0 17.9 %copy-start = (bf16[3,3,320,320]{3,2,1,0:T(8,128)(2,1)S(1)}, bf16[3,3,320,320]{3,2,1,0:T(8,128)(2,1)}, u32[]{:S(2)}) copy-start(bf16[3,3,320,320]{3,2,1,0:T(8,128)(2,1)} %param.15) | copy-start | bytes 5529604
  2.2 21.8 %collective-permute-start.7 = (bf16[2,64,640]{2,1,0:T(8,128)(2,1)}, bf16[2,64,640]{2,1,0:T(8,128)(2,1)S(1)}, u32[]{:S(2)}, u32[]{:S(2)}) collective-permute-start(bf16[2,64,640]{2,1,0:T(8,128)(2,1)} %get-tuple-element.23), channel_id=1, source_target_pairs={{0,12},{1,13},{2,14},{3,15},{4,0},{5,1},{6,2},{7,3},{8,4},{9,5},{1... | collective-permute-start | bytes 491528 | tf_op jit(solution)/shard_map/ppermute | solution.py:31
  7.2 12.6 %collective-permute-start.2 = (bf16[2,64,640]{2,1,0:T(8,128)(2,1)}, bf16[2,64,640]{2,1,0:T(8,128)(2,1)S(1)}, u32[]{:S(2)}, u32[]{:S(2)}) collective-permute-start(bf16[2,64,640]{2,1,0:T(8,128)(2,1)} %get-tuple-element.23), channel_id=1, source_target_pairs={{0,4},{1,5},{2,6},{3,7},{4,8},{5,9},{6,10},{7,11},{8,12},{9,13},{1... | collective-permute-start | bytes 491528 | tf_op jit(solution)/shard_map/ppermute | solution.py:31
  7.3 16.7 %collective-permute-start.9 = (bf16[2,64,640]{2,1,0:T(8,128)(2,1)}, bf16[2,64,640]{2,1,0:T(8,128)(2,1)S(1)}, u32[]{:S(2)}, u32[]{:S(2)}) collective-permute-start(bf16[2,64,640]{2,1,0:T(8,128)(2,1)} %get-tuple-element.24), channel_id=1, source_target_pairs={{0,14},{1,15},{2,12},{3,13},{4,2},{5,3},{6,0},{7,1},{8,6},{9,7},{1... | collective-permute-start | bytes 491528 | tf_op jit(solution)/shard_map/ppermute | solution.py:31
  12.0 11.4 %collective-permute-start.3 = (bf16[2,64,640]{2,1,0:T(8,128)(2,1)}, bf16[2,64,640]{2,1,0:T(8,128)(2,1)S(1)}, u32[]{:S(2)}, u32[]{:S(2)}) collective-permute-start(bf16[2,64,640]{2,1,0:T(8,128)(2,1)} %get-tuple-element.24), channel_id=1, source_target_pairs={{0,6},{1,7},{2,4},{3,5},{4,10},{5,11},{6,8},{7,9},{8,14},{9,15},{1... | collective-permute-start | bytes 491528 | tf_op jit(solution)/shard_map/ppermute | solution.py:31
  12.0 11.4 %collective-permute-start.1 = (bf16[2,64,640]{2,1,0:T(8,128)(2,1)}, bf16[2,64,640]{2,1,0:T(8,128)(2,1)S(1)}, u32[]{:S(2)}, u32[]{:S(2)}) collective-permute-start(bf16[2,64,640]{2,1,0:T(8,128)(2,1)} %get-tuple-element.24), channel_id=1, source_target_pairs={{0,2},{1,3},{2,0},{3,1},{4,6},{5,7},{6,4},{7,5},{8,10},{9,11},{10,... | collective-permute-start | bytes 491528 | tf_op jit(solution)/shard_map/ppermute | solution.py:31
  17.9 1.6 %copy-start.1 = (bf16[3,3,320,320]{3,2,1,0:T(8,128)(2,1)S(1)}, bf16[3,3,320,320]{3,2,1,0:T(8,128)(2,1)}, u32[]{:S(2)}) copy-start(bf16[3,3,320,320]{3,2,1,0:T(8,128)(2,1)} %param.16) | copy-start | bytes 5529604
  19.5 0.9 %copy-start.2 = (bf16[2,64,640]{2,1,0:T(8,128)(2,1)S(1)}, bf16[2,64,640]{2,1,0:T(8,128)(2,1)}, u32[]{:S(2)}) copy-start(bf16[2,64,640]{2,1,0:T(8,128)(2,1)} %get-tuple-element.23) | copy-start | bytes 491524
  20.4 4.1 %collective-permute-start = (bf16[2,64,640]{2,1,0:T(8,128)(2,1)S(1)}, bf16[2,64,640]{2,1,0:T(8,128)(2,1)S(1)}, u32[]{:S(2)}, u32[]{:S(2)}) collective-permute-start(bf16[2,64,640]{2,1,0:T(8,128)(2,1)S(1)} %copy-done.2), channel_id=1, source_target_pairs={{0,1},{1,0},{2,3},{3,2},{4,5},{5,4},{6,7},{7,6},{8,9},{9,8},{10,11... | collective-permute-start | bytes 491528 | tf_op jit(solution)/shard_map/ppermute | solution.py:31
  23.4 2.1 %collective-permute-start.4 = (bf16[2,64,640]{2,1,0:T(8,128)(2,1)S(1)}, bf16[2,64,640]{2,1,0:T(8,128)(2,1)S(1)}, u32[]{:S(2)}, u32[]{:S(2)}) collective-permute-start(bf16[2,64,640]{2,1,0:T(8,128)(2,1)S(1)} %collective-permute-done.1.refs_2_), channel_id=1, source_target_pairs={{0,1},{1,0},{2,3},{3,2},{4,5},{5,4},{6,7},{7,6},{8,9},{9,8},{10,11... | collective-permute-start | bytes 491528 | tf_op jit(solution)/shard_map/ppermute | solution.py:31
  23.4 2.1 %collective-permute-start.5 = (bf16[2,64,640]{2,1,0:T(8,128)(2,1)S(1)}, bf16[2,64,640]{2,1,0:T(8,128)(2,1)S(1)}, u32[]{:S(2)}, u32[]{:S(2)}) collective-permute-start(bf16[2,64,640]{2,1,0:T(8,128)(2,1)S(1)} %collective-permute-done.2.refs_4_), channel_id=1, source_target_pairs={{0,1},{1,0},{2,3},{3,2},{4,5},{5,4},{6,7},{7,6},{8,9},{9,8},{10,11... | collective-permute-start | bytes 491528 | tf_op jit(solution)/shard_map/ppermute | solution.py:31
  24.0 1.4 %collective-permute-start.8 = (bf16[2,64,640]{2,1,0:T(8,128)(2,1)S(1)}, bf16[2,64,640]{2,1,0:T(8,128)(2,1)S(1)}, u32[]{:S(2)}, u32[]{:S(2)}) collective-permute-start(bf16[2,64,640]{2,1,0:T(8,128)(2,1)S(1)} %collective-permute-done.7.refs_8_), channel_id=1, source_target_pairs={{0,1},{1,0},{2,3},{3,2},{4,5},{5,4},{6,7},{7,6},{8,9},{9,8},{10,11... | collective-permute-start | bytes 491528 | tf_op jit(solution)/shard_map/ppermute | solution.py:31
  24.0 1.6 %collective-permute-start.10 = (bf16[2,64,640]{2,1,0:T(8,128)(2,1)S(1)}, bf16[2,64,640]{2,1,0:T(8,128)(2,1)S(1)}, u32[]{:S(2)}, u32[]{:S(2)}) collective-permute-start(bf16[2,64,640]{2,1,0:T(8,128)(2,1)S(1)} %collective-permute-done.9.refs_10_), channel_id=1, source_target_pairs={{0,1},{1,0},{2,3},{3,2},{4,5},{5,4},{6,7},{7,6},{8,9},{9,8},{10,11... | collective-permute-start | bytes 491528 | tf_op jit(solution)/shard_map/ppermute | solution.py:31
  24.5 1.4 %collective-permute-start.6 = (bf16[2,64,640]{2,1,0:T(8,128)(2,1)S(1)}, bf16[2,64,640]{2,1,0:T(8,128)(2,1)S(1)}, u32[]{:S(2)}, u32[]{:S(2)}) collective-permute-start(bf16[2,64,640]{2,1,0:T(8,128)(2,1)S(1)} %collective-permute-done.3.refs_6_), channel_id=1, source_target_pairs={{0,1},{1,0},{2,3},{3,2},{4,5},{5,4},{6,7},{7,6},{8,9},{9,8},{10,11... | collective-permute-start | bytes 491528 | tf_op jit(solution)/shard_map/ppermute | solution.py:31
  31.6 1.9 %collective-permute-start.11 = (bf16[64,640]{1,0:T(8,128)(2,1)S(1)}, bf16[64,640]{1,0:T(8,128)(2,1)S(1)}, u32[]{:S(2)}, u32[]{:S(2)}) collective-permute-start(bf16[64,640]{1,0:T(8,128)(2,1)S(1)} %get-tuple-element.31), channel_id=1, source_target_pairs={{0,1},{1,0},{2,3},{3,2},{4,5},{5,4},{6,7},{7,6},{8,9},{9,8},{10,11... | collective-permute-start | bytes 245768 | tf_op jit(solution)/shard_map/ppermute | solution.py:31
  31.9 5.3 %collective-permute-start.12 = (bf16[64,640]{1,0:T(8,128)(2,1)S(1)}, bf16[64,640]{1,0:T(8,128)(2,1)S(1)}, u32[]{:S(2)}, u32[]{:S(2)}) collective-permute-start(bf16[64,640]{1,0:T(8,128)(2,1)S(1)} %get-tuple-element.32), channel_id=1, source_target_pairs={{0,2},{1,3},{2,0},{3,1},{4,6},{5,7},{6,4},{7,5},{8,10},{9,11},{10,... | collective-permute-start | bytes 245768 | tf_op jit(solution)/shard_map/ppermute | solution.py:31
  32.4 5.2 %collective-permute-start.13 = (bf16[64,640]{1,0:T(8,128)(2,1)S(1)}, bf16[64,640]{1,0:T(8,128)(2,1)S(1)}, u32[]{:S(2)}, u32[]{:S(2)}) collective-permute-start(bf16[64,640]{1,0:T(8,128)(2,1)S(1)} %get-tuple-element.33), channel_id=1, source_target_pairs={{0,3},{1,2},{2,1},{3,0},{4,7},{5,6},{6,5},{7,4},{8,11},{9,10},{10,... | collective-permute-start | bytes 245768 | tf_op jit(solution)/shard_map/ppermute | solution.py:31

commit v7 on v6

--- a/solution.py
+++ b/solution.py
@@ -356,8 +356,7 @@
         jnp.pad(conv_one, ((0, 0), (0, 0), more, (0, 0))),
         jnp.pad(conv_two, ((0, 0), (0, 0), more, (0, 0))),
     ]
-    landed[1:4] = lax.optimization_barrier(landed[1:4])
-    landed[0], extras = lax.optimization_barrier((near, extras))
+    landed[2], extras = lax.optimization_barrier((landed[2], extras))
     parts = []
     for piece in landed:
         parts += [piece, moved(piece, lambda i: i ^ 1)]

time: 43.3 us -> 41.2 us (0.952)
  waiting for transfers between devices: 8.44 us -> 5.6 us
  starting transfers between devices: 13.4 us -> 15 us
  other arithmetic: 1.44 us -> 0.76 us
    ppermute x14, waiting for transfers between devices: 8.44 us -> 5.6 us  [moved(): lax.ppermute(array, 'frame', [(i, target(i) % count) for i in range(count)])]
    ppermute x14, starting transfers between devices: 13.4 us -> 15 us  [moved(): lax.ppermute(array, 'frame', [(i, target(i) % count) for i in range(count)])]
    concatenate x1, other arithmetic: 0.69 us -> 0.01 us  [body(): jnp.concatenate([gn_gain, step_embed[None]])]
    unnamed x7 -> x9, local copies, waits for them, and re-layouts: 2.97 us -> 2.75 us
  transfers between devices with their start and end apart: 14 -> 14, of which waited for: 6 -> 6; matrix products, arithmetic and copies ran while one was open for 14% -> 13% of each run, Pallas kernels for 0% -> 0%
where the time goes in v7:
time: 41.2 us; the launch traced here: 40.8 us
  starting transfers between devices  15 us (36%)
  Pallas kernels  13.2 us (32%)
  local copies, waits for them, and re-layouts  6.18 us (15%)
  waiting for transfers between devices  5.6 us (14%)
  other arithmetic  0.76 us (2%)
    ppermute x14, starting transfers between devices, moved(): lax.ppermute(array, 'frame', [(i, target(i) % count) for i in range(count)])  15 us
    pallas_call x1, Pallas kernels, attend(): pl.pallas_call(functools.partial(attend_kernel, cells, planes), out_shape...  5.76 us
    ppermute x14, waiting for transfers between devices, moved(): lax.ppermute(array, 'frame', [(i, target(i) % count) for i in range(count)])  5.6 us
    pallas_call x1, Pallas kernels, res_block(): pl.pallas_call(res_kernel, out_shape=jax.ShapeDtypeStruct((frames, count,...  5.23 us
    unnamed x9, local copies, waits for them, and re-layouts  2.75 us
    pallas_call x1, Pallas kernels, body(): pl.pallas_call(pack_kernel, out_shape=[jax.ShapeDtypeStruct((2, rows, pac...  2.18 us
    pad x1, local copies, waits for them, and re-layouts, body(): jnp.pad(w_qkv, (more, (0, 0)))  1.18 us
    pad x1, local copies, waits for them, and re-layouts, body(): jnp.pad(w_out, (more, (0, 0)))  0.97 us
  transfers between devices with their start and end apart: 14, of which 6 were waited for; matrix products, arithmetic and copies ran while one was open for 13% of the time, Pallas kernels for 0%

profile of v7, /device:TPU:0, one launch (start us, length us, event | category | flops | bytes accessed | tf_op | source)
XLA Modules:
  0.0 40.8 jit_solution(10013125059349439696)
XLA Ops:
  0.0 2.2 %norm_pack.1 = (bf16[2,64,640]{2,1,0:T(8,128)(2,1)}, bf16[2,64,640]{2,1,0:T(8,128)(2,1)}) custom-call(bf16[4,4,32,320]{3,2,1,0:T(8,128)(2,1)} %bitcast.5, f32[320]{0:T(512)} %gain_ref.1), custom_call_target="tpu_custom_call" | custom-call | tf_op jit(solution)/shard_map/norm_pack/pallas_call | solution.py:334
  2.2 3.0 %collective-permute-start.3 = (bf16[2,64,640]{2,1,0:T(8,128)(2,1)}, bf16[2,64,640]{2,1,0:T(8,128)(2,1)S(1)}, u32[]{:S(2)}, u32[]{:S(2)}) collective-permute-start(bf16[2,64,640]{2,1,0:T(8,128)(2,1)} %get-tuple-element.19), channel_id=1, source_target_pairs={{0,4},{1,5},{2,6},{3,7},{4,8},{5,9},{6,10},{7,11},{8,12},{9,13},{1... | collective-permute-start | bytes 491528 | tf_op jit(solution)/shard_map/ppermute | solution.py:31
  5.2 3.2 %collective-permute-start.9 = (bf16[2,64,640]{2,1,0:T(8,128)(2,1)}, bf16[2,64,640]{2,1,0:T(8,128)(2,1)S(1)}, u32[]{:S(2)}, u32[]{:S(2)}) collective-permute-start(bf16[2,64,640]{2,1,0:T(8,128)(2,1)} %get-tuple-element.20), channel_id=1, source_target_pairs={{0,14},{1,15},{2,12},{3,13},{4,2},{5,3},{6,0},{7,1},{8,6},{9,7},{1... | collective-permute-start | bytes 491528 | tf_op jit(solution)/shard_map/ppermute | solution.py:31
  8.4 1.2 %collective-permute-start.1 = (bf16[2,64,640]{2,1,0:T(8,128)(2,1)}, bf16[2,64,640]{2,1,0:T(8,128)(2,1)S(1)}, u32[]{:S(2)}, u32[]{:S(2)}) collective-permute-start(bf16[2,64,640]{2,1,0:T(8,128)(2,1)} %get-tuple-element.20), channel_id=1, source_target_pairs={{0,2},{1,3},{2,0},{3,1},{4,6},{5,7},{6,4},{7,5},{8,10},{9,11},{10,... | collective-permute-start | bytes 491528 | tf_op jit(solution)/shard_map/ppermute | solution.py:31
  9.7 4.0 %collective-permute-start.7 = (bf16[2,64,640]{2,1,0:T(8,128)(2,1)}, bf16[2,64,640]{2,1,0:T(8,128)(2,1)S(1)}, u32[]{:S(2)}, u32[]{:S(2)}) collective-permute-start(bf16[2,64,640]{2,1,0:T(8,128)(2,1)} %get-tuple-element.19), channel_id=1, source_target_pairs={{0,12},{1,13},{2,14},{3,15},{4,0},{5,1},{6,2},{7,3},{8,4},{9,5},{1... | collective-permute-start | bytes 491528 | tf_op jit(solution)/shard_map/ppermute | solution.py:31
  13.7 0.7 %pad_add_fusion.refs_12_ = s32[32]{0:T(128)S(1)} fusion(s32[16]{0:T(128)} %param.19, s32[16]{0:T(128)} %param.18), kind=kLoop, calls=%fused_computation.2 | loop fusion | flops 32 | bytes 256 | tf_op jit(solution)/shard_map/concatenate | solution.py:352
  14.5 1.0 %copy.13 = bf16[4,2,64,320]{3,2,0,1:T(8,128)(2,1)S(1)} copy(bf16[4,2,64,320]{3,2,1,0:T(8,128)(2,1)} %param.10) | data formatting | bytes 655360 | tf_op args[0]
  15.5 0.7 %broadcast_in_dim.3 = f32[1,320]{1,0:T(1,128)S(1)} reshape(f32[320]{0:T(512)} %param.17) | data formatting | bytes 2560 | tf_op jit(solution)/shard_map/broadcast_in_dim | solution.py:355
  16.2 1.0 %pad.16.refs_5_ = bf16[384,320]{1,0:T(8,128)(2,1)S(1)} pad(bf16[320,320]{1,0:T(8,128)(2,1)} %param.13, bf16[]{:T(256)} %constant.2.clone.1), padding=0_64x0_0 | pad | bytes 450562 | tf_op jit(solution)/shard_map/jit(_pad)/pad | solution.py:354
  17.2 1.2 %pad.15.refs_13_ = bf16[384,960]{1,0:T(8,128)(2,1)S(1)} pad(bf16[320,960]{1,0:T(8,128)(2,1)} %param.12, bf16[]{:T(256)} %constant.2.clone.1), padding=0_64x0_0 | pad | bytes 1351682 | tf_op jit(solution)/shard_map/jit(_pad)/pad | solution.py:351
  18.7 1.3 %copy-done.1 = bf16[3,3,320,320]{3,2,1,0:T(8,128)(2,1)S(1)} copy-done((bf16[3,3,320,320]{3,2,1,0:T(8,128)(2,1)S(1)}, bf16[3,3,320,320]{3,2,1,0:T(8,128)(2,1)}, u32[]{:S(2)}) %copy-start.1) | copy-done | bytes 1843224
  20.3 0.4 copy-done.3
  20.7 0.6 %collective-permute-start.10 = (bf16[2,64,640]{2,1,0:T(8,128)(2,1)S(1)}, bf16[2,64,640]{2,1,0:T(8,128)(2,1)S(1)}, u32[]{:S(2)}, u32[]{:S(2)}) collective-permute-start(bf16[2,64,640]{2,1,0:T(8,128)(2,1)S(1)} %collective-permute-done.9.refs_10_), channel_id=1, source_target_pairs={{0,1},{1,0},{2,3},{3,2},{4,5},{5,4},{6,7},{7,6},{8,9},{9,8},{10,11... | collective-permute-start | bytes 491528 | tf_op jit(solution)/shard_map/ppermute | solution.py:31
  21.4 0.4 %collective-permute-start.2 = (bf16[2,64,640]{2,1,0:T(8,128)(2,1)S(1)}, bf16[2,64,640]{2,1,0:T(8,128)(2,1)S(1)}, u32[]{:S(2)}, u32[]{:S(2)}) collective-permute-start(bf16[2,64,640]{2,1,0:T(8,128)(2,1)S(1)} %collective-permute-done.1.refs_2_), channel_id=1, source_target_pairs={{0,1},{1,0},{2,3},{3,2},{4,5},{5,4},{6,7},{7,6},{8,9},{9,8},{10,11... | collective-permute-start | bytes 491528 | tf_op jit(solution)/shard_map/ppermute | solution.py:31
  21.8 0.4 %collective-permute-done.7.refs_8_ = bf16[2,64,640]{2,1,0:T(8,128)(2,1)S(1)} collective-permute-done((bf16[2,64,640]{2,1,0:T(8,128)(2,1)}, bf16[2,64,640]{2,1,0:T(8,128)(2,1)S(1)}, u32[]{:S(2)}, u32[]{:S(2)}) %collective-permute-start.7) | collective-permute-done | bytes 163872 | tf_op jit(solution)/shard_map/ppermute | solution.py:31
  22.2 0.5 %collective-permute-start.4 = (bf16[2,64,640]{2,1,0:T(8,128)(2,1)S(1)}, bf16[2,64,640]{2,1,0:T(8,128)(2,1)S(1)}, u32[]{:S(2)}, u32[]{:S(2)}) collective-permute-start(bf16[2,64,640]{2,1,0:T(8,128)(2,1)S(1)} %collective-permute-done.3.refs_4_), channel_id=1, source_target_pairs={{0,1},{1,0},{2,3},{3,2},{4,5},{5,4},{6,7},{7,6},{8,9},{9,8},{10,11... | collective-permute-start | bytes 491528 | tf_op jit(solution)/shard_map/ppermute | solution.py:31
  22.9 0.7 %collective-permute-done.8.refs_9_ = bf16[2,64,640]{2,1,0:T(8,128)(2,1)S(1)} collective-permute-done((bf16[2,64,640]{2,1,0:T(8,128)(2,1)S(1)}, bf16[2,64,640]{2,1,0:T(8,128)(2,1)S(1)}, u32[]{:S(2)}, u32[]{:S(2)}) %collective-permute-start.8) | collective-permute-done | bytes 163872 | tf_op jit(solution)/shard_map/ppermute | solution.py:31
  23.8 5.8 %window_attention.1 = (bf16[64,640]{1,0:T(8,128)(2,1)S(1)}, bf16[64,640]{1,0:T(8,128)(2,1)S(1)}, bf16[64,640]{1,0:T(8,128)(2,1)S(1)}, bf16[64,640]{1,0:T(8,128)(2,1)S(1)}) custom-call(bf16[1,64,640]{2,1,0:T(8,128)(2,1)S(1)} %slice.3.refs_0_, bf16[2,64,640]{2,1,0:T(8,128)(2,1)S(1)} %collective-permute-done.refs_1_, ...), custom_call_target="tpu_custom_call" | custom-call | tf_op jit(solution)/shard_map/window_attention/pallas_call | solution.py:200
  29.6 0.3 collective-permute-start.11
  30.0 0.9 %collective-permute-start.12 = (bf16[64,640]{1,0:T(8,128)(2,1)S(1)}, bf16[64,640]{1,0:T(8,128)(2,1)S(1)}, u32[]{:S(2)}, u32[]{:S(2)}) collective-permute-start(bf16[64,640]{1,0:T(8,128)(2,1)S(1)} %get-tuple-element.26), channel_id=1, source_target_pairs={{0,2},{1,3},{2,0},{3,1},{4,6},{5,7},{6,4},{7,5},{8,10},{9,11},{10,... | collective-permute-start | bytes 245768 | tf_op jit(solution)/shard_map/ppermute | solution.py:31
  30.9 0.7 %collective-permute-start.13 = (bf16[64,640]{1,0:T(8,128)(2,1)S(1)}, bf16[64,640]{1,0:T(8,128)(2,1)S(1)}, u32[]{:S(2)}, u32[]{:S(2)}) collective-permute-start(bf16[64,640]{1,0:T(8,128)(2,1)S(1)} %get-tuple-element.27), channel_id=1, source_target_pairs={{0,3},{1,2},{2,1},{3,0},{4,7},{5,6},{6,5},{7,4},{8,11},{9,10},{10,... | collective-permute-start | bytes 245768 | tf_op jit(solution)/shard_map/ppermute | solution.py:31
  31.5 3.7 %collective-permute-done.12.refs_2_ = bf16[64,640]{1,0:T(8,128)(2,1)S(1)} collective-permute-done((bf16[64,640]{1,0:T(8,128)(2,1)S(1)}, bf16[64,640]{1,0:T(8,128)(2,1)S(1)}, u32[]{:S(2)}, u32[]{:S(2)}) %collective-permute-start.12) | collective-permute-done | bytes 81952 | tf_op jit(solution)/shard_map/ppermute | solution.py:31
  35.2 0.4 collective-permute-done.13.refs_3_
  35.6 5.2 %res_block.1 = bf16[4,2,64,320]{3,2,1,0:T(8,128)(2,1)} custom-call(bf16[64,640]{1,0:T(8,128)(2,1)S(1)} %get-tuple-element.24.refs_0_, bf16[64,640]{1,0:T(8,128)(2,1)S(1)} %collective-permute-done.11.refs_1_, bf16[64,640]{1,0:T(8,128)(2,1)S(1)} %collective-permute-done.12.refs_2_, bf16[64,640]{1,0:T(8,128)(2,1)S(1)} %collective-permute-done.13.refs_3_, ...), custom_call_target="tpu_custom_call" | custom-call | tf_op jit(solution)/shard_map/res_block/pallas_call | solution.py:309
  (24 shorter events, 1.1 us)
Async XLA Ops:
  0.0 18.3 %copy-start = (bf16[3,3,320,320]{3,2,1,0:T(8,128)(2,1)S(1)}, bf16[3,3,320,320]{3,2,1,0:T(8,128)(2,1)}, u32[]{:S(2)}) copy-start(bf16[3,3,320,320]{3,2,1,0:T(8,128)(2,1)} %param.15) | copy-start | bytes 5529604
  2.2 11.5 %collective-permute-start.3 = (bf16[2,64,640]{2,1,0:T(8,128)(2,1)}, bf16[2,64,640]{2,1,0:T(8,128)(2,1)S(1)}, u32[]{:S(2)}, u32[]{:S(2)}) collective-permute-start(bf16[2,64,640]{2,1,0:T(8,128)(2,1)} %get-tuple-element.19), channel_id=1, source_target_pairs={{0,4},{1,5},{2,6},{3,7},{4,8},{5,9},{6,10},{7,11},{8,12},{9,13},{1... | collective-permute-start | bytes 491528 | tf_op jit(solution)/shard_map/ppermute | solution.py:31
  5.2 15.5 %collective-permute-start.9 = (bf16[2,64,640]{2,1,0:T(8,128)(2,1)}, bf16[2,64,640]{2,1,0:T(8,128)(2,1)S(1)}, u32[]{:S(2)}, u32[]{:S(2)}) collective-permute-start(bf16[2,64,640]{2,1,0:T(8,128)(2,1)} %get-tuple-element.20), channel_id=1, source_target_pairs={{0,14},{1,15},{2,12},{3,13},{4,2},{5,3},{6,0},{7,1},{8,6},{9,7},{1... | collective-permute-start | bytes 491528 | tf_op jit(solution)/shard_map/ppermute | solution.py:31
  8.4 12.9 %collective-permute-start.5 = (bf16[2,64,640]{2,1,0:T(8,128)(2,1)}, bf16[2,64,640]{2,1,0:T(8,128)(2,1)S(1)}, u32[]{:S(2)}, u32[]{:S(2)}) collective-permute-start(bf16[2,64,640]{2,1,0:T(8,128)(2,1)} %get-tuple-element.20), channel_id=1, source_target_pairs={{0,6},{1,7},{2,4},{3,5},{4,10},{5,11},{6,8},{7,9},{8,14},{9,15},{1... | collective-permute-start | bytes 491528 | tf_op jit(solution)/shard_map/ppermute | solution.py:31
  8.4 12.9 %collective-permute-start.1 = (bf16[2,64,640]{2,1,0:T(8,128)(2,1)}, bf16[2,64,640]{2,1,0:T(8,128)(2,1)S(1)}, u32[]{:S(2)}, u32[]{:S(2)}) collective-permute-start(bf16[2,64,640]{2,1,0:T(8,128)(2,1)} %get-tuple-element.20), channel_id=1, source_target_pairs={{0,2},{1,3},{2,0},{3,1},{4,6},{5,7},{6,4},{7,5},{8,10},{9,11},{10,... | collective-permute-start | bytes 491528 | tf_op jit(solution)/shard_map/ppermute | solution.py:31
  9.7 12.6 %collective-permute-start.7 = (bf16[2,64,640]{2,1,0:T(8,128)(2,1)}, bf16[2,64,640]{2,1,0:T(8,128)(2,1)S(1)}, u32[]{:S(2)}, u32[]{:S(2)}) collective-permute-start(bf16[2,64,640]{2,1,0:T(8,128)(2,1)} %get-tuple-element.19), channel_id=1, source_target_pairs={{0,12},{1,13},{2,14},{3,15},{4,0},{5,1},{6,2},{7,3},{8,4},{9,5},{1... | collective-permute-start | bytes 491528 | tf_op jit(solution)/shard_map/ppermute | solution.py:31
  13.7 8.5 %collective-permute-start = (bf16[2,64,640]{2,1,0:T(8,128)(2,1)}, bf16[2,64,640]{2,1,0:T(8,128)(2,1)S(1)}, u32[]{:S(2)}, u32[]{:S(2)}) collective-permute-start(bf16[2,64,640]{2,1,0:T(8,128)(2,1)} %get-tuple-element.19), channel_id=1, source_target_pairs={{0,1},{1,0},{2,3},{3,2},{4,5},{5,4},{6,7},{7,6},{8,9},{9,8},{10,11... | collective-permute-start | bytes 491528 | tf_op jit(solution)/shard_map/ppermute | solution.py:31
  18.4 1.6 %copy-start.1 = (bf16[3,3,320,320]{3,2,1,0:T(8,128)(2,1)S(1)}, bf16[3,3,320,320]{3,2,1,0:T(8,128)(2,1)}, u32[]{:S(2)}) copy-start(bf16[3,3,320,320]{3,2,1,0:T(8,128)(2,1)} %param.16) | copy-start | bytes 5529604
  20.0 0.7 %copy-start.3 = (f32[2,320]{1,0:T(2,128)S(1)}, f32[2,320]{1,0:T(2,128)}, u32[]{:S(2)}) copy-start(f32[2,320]{1,0:T(2,128)} %param.14) | copy-start | bytes 7684
  20.0 2.8 %copy-start.2 = (bf16[2,64,640]{2,1,0:T(8,128)(2,1)S(1)}, bf16[2,64,640]{2,1,0:T(8,128)(2,1)}, u32[]{:S(2)}) copy-start(bf16[2,64,640]{2,1,0:T(8,128)(2,1)} %get-tuple-element.19) | copy-start | bytes 491524
  20.7 2.1 %collective-permute-start.10 = (bf16[2,64,640]{2,1,0:T(8,128)(2,1)S(1)}, bf16[2,64,640]{2,1,0:T(8,128)(2,1)S(1)}, u32[]{:S(2)}, u32[]{:S(2)}) collective-permute-start(bf16[2,64,640]{2,1,0:T(8,128)(2,1)S(1)} %collective-permute-done.9.refs_10_), channel_id=1, source_target_pairs={{0,1},{1,0},{2,3},{3,2},{4,5},{5,4},{6,7},{7,6},{8,9},{9,8},{10,11... | collective-permute-start | bytes 491528 | tf_op jit(solution)/shard_map/ppermute | solution.py:31
  21.3 1.5 %collective-permute-start.6 = (bf16[2,64,640]{2,1,0:T(8,128)(2,1)S(1)}, bf16[2,64,640]{2,1,0:T(8,128)(2,1)S(1)}, u32[]{:S(2)}, u32[]{:S(2)}) collective-permute-start(bf16[2,64,640]{2,1,0:T(8,128)(2,1)S(1)} %collective-permute-done.5.refs_6_), channel_id=1, source_target_pairs={{0,1},{1,0},{2,3},{3,2},{4,5},{5,4},{6,7},{7,6},{8,9},{9,8},{10,11... | collective-permute-start | bytes 491528 | tf_op jit(solution)/shard_map/ppermute | solution.py:31
  21.4 1.5 %collective-permute-start.2 = (bf16[2,64,640]{2,1,0:T(8,128)(2,1)S(1)}, bf16[2,64,640]{2,1,0:T(8,128)(2,1)S(1)}, u32[]{:S(2)}, u32[]{:S(2)}) collective-permute-start(bf16[2,64,640]{2,1,0:T(8,128)(2,1)S(1)} %collective-permute-done.1.refs_2_), channel_id=1, source_target_pairs={{0,1},{1,0},{2,3},{3,2},{4,5},{5,4},{6,7},{7,6},{8,9},{9,8},{10,11... | collective-permute-start | bytes 491528 | tf_op jit(solution)/shard_map/ppermute | solution.py:31
  22.2 1.4 %collective-permute-start.8 = (bf16[2,64,640]{2,1,0:T(8,128)(2,1)S(1)}, bf16[2,64,640]{2,1,0:T(8,128)(2,1)S(1)}, u32[]{:S(2)}, u32[]{:S(2)}) collective-permute-start(bf16[2,64,640]{2,1,0:T(8,128)(2,1)S(1)} %collective-permute-done.7.refs_8_), channel_id=1, source_target_pairs={{0,1},{1,0},{2,3},{3,2},{4,5},{5,4},{6,7},{7,6},{8,9},{9,8},{10,11... | collective-permute-start | bytes 491528 | tf_op jit(solution)/shard_map/ppermute | solution.py:31
  22.2 1.6 %collective-permute-start.4 = (bf16[2,64,640]{2,1,0:T(8,128)(2,1)S(1)}, bf16[2,64,640]{2,1,0:T(8,128)(2,1)S(1)}, u32[]{:S(2)}, u32[]{:S(2)}) collective-permute-start(bf16[2,64,640]{2,1,0:T(8,128)(2,1)S(1)} %collective-permute-done.3.refs_4_), channel_id=1, source_target_pairs={{0,1},{1,0},{2,3},{3,2},{4,5},{5,4},{6,7},{7,6},{8,9},{9,8},{10,11... | collective-permute-start | bytes 491528 | tf_op jit(solution)/shard_map/ppermute | solution.py:31
  29.6 1.9 %collective-permute-start.11 = (bf16[64,640]{1,0:T(8,128)(2,1)S(1)}, bf16[64,640]{1,0:T(8,128)(2,1)S(1)}, u32[]{:S(2)}, u32[]{:S(2)}) collective-permute-start(bf16[64,640]{1,0:T(8,128)(2,1)S(1)} %get-tuple-element.25), channel_id=1, source_target_pairs={{0,1},{1,0},{2,3},{3,2},{4,5},{5,4},{6,7},{7,6},{8,9},{9,8},{10,11... | collective-permute-start | bytes 245768 | tf_op jit(solution)/shard_map/ppermute | solution.py:31
  30.0 5.3 %collective-permute-start.12 = (bf16[64,640]{1,0:T(8,128)(2,1)S(1)}, bf16[64,640]{1,0:T(8,128)(2,1)S(1)}, u32[]{:S(2)}, u32[]{:S(2)}) collective-permute-start(bf16[64,640]{1,0:T(8,128)(2,1)S(1)} %get-tuple-element.26), channel_id=1, source_target_pairs={{0,2},{1,3},{2,0},{3,1},{4,6},{5,7},{6,4},{7,5},{8,10},{9,11},{10,... | collective-permute-start | bytes 245768 | tf_op jit(solution)/shard_map/ppermute | solution.py:31
  30.9 4.7 %collective-permute-start.13 = (bf16[64,640]{1,0:T(8,128)(2,1)S(1)}, bf16[64,640]{1,0:T(8,128)(2,1)S(1)}, u32[]{:S(2)}, u32[]{:S(2)}) collective-permute-start(bf16[64,640]{1,0:T(8,128)(2,1)S(1)} %get-tuple-element.27), channel_id=1, source_target_pairs={{0,3},{1,2},{2,1},{3,0},{4,7},{5,6},{6,5},{7,4},{8,11},{9,10},{10,... | collective-permute-start | bytes 245768 | tf_op jit(solution)/shard_map/ppermute | solution.py:31

commit v8 on v7

--- a/solution.py
+++ b/solution.py
@@ -161,10 +161,19 @@
         scores = scores * LOG2E
         mixed = jnp.zeros((key_frames, wide), jnp.float32)
         for back in range(REACH + 1):
-            s = scores + bias_ref[back]
+            third = key_frames // 3
+            spans = {0: ((0, third), (2 * third, key_frames)), REACH: ((0, 2 * third),)}
+            spans = spans.get(back, ((0, key_frames),))
+            s = jnp.concatenate([scores[lo:hi] + bias_ref[back, lo:hi] for lo, hi in spans], 0)
             e = jnp.exp2(s - jnp.max(s, axis=0, keepdims=True))
             z = jnp.sum(e, axis=0, keepdims=True)
-            mixed = mixed + e * (coef_ref[back] / z)
+            e = e * (coef_ref[back] / z)
+            if back == 0:
+                none = jnp.zeros((third, wide), jnp.float32)
+                e = jnp.concatenate([e[:third], none, e[third:]], 0)
+            elif back == REACH:
+                e = jnp.concatenate([e, jnp.zeros((third, wide), jnp.float32)], 0)
+            mixed = mixed + e
         mixed = mixed.T.astype(jnp.bfloat16)
         for g in range(group):
             full = jnp.dot(

time: 41.2 us -> 41 us (level)
  no operation moved by 1% of the time
where the time goes in v8:
time: 41 us; the launch traced here: 40.6 us
  starting transfers between devices  15 us (37%)
  Pallas kernels  13 us (32%)
  local copies, waits for them, and re-layouts  6.18 us (15%)
  waiting for transfers between devices  5.59 us (14%)
  other arithmetic  0.76 us (2%)
    ppermute x14, starting transfers between devices, moved(): lax.ppermute(array, 'frame', [(i, target(i) % count) for i in range(count)])  15 us
    ppermute x14, waiting for transfers between devices, moved(): lax.ppermute(array, 'frame', [(i, target(i) % count) for i in range(count)])  5.59 us
    pallas_call x1, Pallas kernels, attend(): pl.pallas_call(functools.partial(attend_kernel, cells, planes), out_shape...  5.55 us
    pallas_call x1, Pallas kernels, res_block(): pl.pallas_call(res_kernel, out_shape=jax.ShapeDtypeStruct((frames, count,...  5.23 us
    unnamed x9, local copies, waits for them, and re-layouts  2.75 us
    pallas_call x1, Pallas kernels, body(): pl.pallas_call(pack_kernel, out_shape=[jax.ShapeDtypeStruct((2, rows, pac...  2.18 us
    pad x1, local copies, waits for them, and re-layouts, body(): jnp.pad(w_qkv, (more, (0, 0)))  1.18 us
    pad x1, local copies, waits for them, and re-layouts, body(): jnp.pad(w_out, (more, (0, 0)))  0.97 us
  transfers between devices with their start and end apart: 14, of which 6 were waited for; matrix products, arithmetic and copies ran while one was open for 13% of the time, Pallas kernels for 0%

profile of v8, /device:TPU:0, one launch (start us, length us, event | category | flops | bytes accessed | tf_op | source)
XLA Modules:
  0.0 40.6 jit_solution(9953827079600805980)
XLA Ops:
  0.0 2.2 %norm_pack.1 = (bf16[2,64,640]{2,1,0:T(8,128)(2,1)}, bf16[2,64,640]{2,1,0:T(8,128)(2,1)}) custom-call(bf16[4,4,32,320]{3,2,1,0:T(8,128)(2,1)} %bitcast.5, f32[320]{0:T(512)} %gain_ref.1), custom_call_target="tpu_custom_call" | custom-call | tf_op jit(solution)/shard_map/norm_pack/pallas_call | solution.py:343
  2.2 3.0 %collective-permute-start.3 = (bf16[2,64,640]{2,1,0:T(8,128)(2,1)}, bf16[2,64,640]{2,1,0:T(8,128)(2,1)S(1)}, u32[]{:S(2)}, u32[]{:S(2)}) collective-permute-start(bf16[2,64,640]{2,1,0:T(8,128)(2,1)} %get-tuple-element.19), channel_id=1, source_target_pairs={{0,4},{1,5},{2,6},{3,7},{4,8},{5,9},{6,10},{7,11},{8,12},{9,13},{1... | collective-permute-start | bytes 491528 | tf_op jit(solution)/shard_map/ppermute | solution.py:31
  5.2 3.2 %collective-permute-start.9 = (bf16[2,64,640]{2,1,0:T(8,128)(2,1)}, bf16[2,64,640]{2,1,0:T(8,128)(2,1)S(1)}, u32[]{:S(2)}, u32[]{:S(2)}) collective-permute-start(bf16[2,64,640]{2,1,0:T(8,128)(2,1)} %get-tuple-element.20), channel_id=1, source_target_pairs={{0,14},{1,15},{2,12},{3,13},{4,2},{5,3},{6,0},{7,1},{8,6},{9,7},{1... | collective-permute-start | bytes 491528 | tf_op jit(solution)/shard_map/ppermute | solution.py:31
  8.4 1.2 %collective-permute-start.1 = (bf16[2,64,640]{2,1,0:T(8,128)(2,1)}, bf16[2,64,640]{2,1,0:T(8,128)(2,1)S(1)}, u32[]{:S(2)}, u32[]{:S(2)}) collective-permute-start(bf16[2,64,640]{2,1,0:T(8,128)(2,1)} %get-tuple-element.20), channel_id=1, source_target_pairs={{0,2},{1,3},{2,0},{3,1},{4,6},{5,7},{6,4},{7,5},{8,10},{9,11},{10,... | collective-permute-start | bytes 491528 | tf_op jit(solution)/shard_map/ppermute | solution.py:31
  9.7 4.0 %collective-permute-start.7 = (bf16[2,64,640]{2,1,0:T(8,128)(2,1)}, bf16[2,64,640]{2,1,0:T(8,128)(2,1)S(1)}, u32[]{:S(2)}, u32[]{:S(2)}) collective-permute-start(bf16[2,64,640]{2,1,0:T(8,128)(2,1)} %get-tuple-element.19), channel_id=1, source_target_pairs={{0,12},{1,13},{2,14},{3,15},{4,0},{5,1},{6,2},{7,3},{8,4},{9,5},{1... | collective-permute-start | bytes 491528 | tf_op jit(solution)/shard_map/ppermute | solution.py:31
  13.7 0.7 %pad_add_fusion.refs_12_ = s32[32]{0:T(128)S(1)} fusion(s32[16]{0:T(128)} %param.19, s32[16]{0:T(128)} %param.18), kind=kLoop, calls=%fused_computation.2 | loop fusion | flops 32 | bytes 256 | tf_op jit(solution)/shard_map/concatenate | solution.py:361
  14.5 1.0 %copy.13 = bf16[4,2,64,320]{3,2,0,1:T(8,128)(2,1)S(1)} copy(bf16[4,2,64,320]{3,2,1,0:T(8,128)(2,1)} %param.10) | data formatting | bytes 655360 | tf_op args[0]
  15.5 0.7 %broadcast_in_dim.3 = f32[1,320]{1,0:T(1,128)S(1)} reshape(f32[320]{0:T(512)} %param.17) | data formatting | bytes 2560 | tf_op jit(solution)/shard_map/broadcast_in_dim | solution.py:364
  16.2 1.0 %pad.16.refs_5_ = bf16[384,320]{1,0:T(8,128)(2,1)S(1)} pad(bf16[320,320]{1,0:T(8,128)(2,1)} %param.13, bf16[]{:T(256)} %constant.2.clone.1), padding=0_64x0_0 | pad | bytes 450562 | tf_op jit(solution)/shard_map/jit(_pad)/pad | solution.py:363
  17.2 1.2 %pad.15.refs_13_ = bf16[384,960]{1,0:T(8,128)(2,1)S(1)} pad(bf16[320,960]{1,0:T(8,128)(2,1)} %param.12, bf16[]{:T(256)} %constant.2.clone.1), padding=0_64x0_0 | pad | bytes 1351682 | tf_op jit(solution)/shard_map/jit(_pad)/pad | solution.py:360
  18.7 1.3 %copy-done.1 = bf16[3,3,320,320]{3,2,1,0:T(8,128)(2,1)S(1)} copy-done((bf16[3,3,320,320]{3,2,1,0:T(8,128)(2,1)S(1)}, bf16[3,3,320,320]{3,2,1,0:T(8,128)(2,1)}, u32[]{:S(2)}) %copy-start.1) | copy-done | bytes 1843224
  20.3 0.4 copy-done.3
  20.7 0.6 %collective-permute-start.10 = (bf16[2,64,640]{2,1,0:T(8,128)(2,1)S(1)}, bf16[2,64,640]{2,1,0:T(8,128)(2,1)S(1)}, u32[]{:S(2)}, u32[]{:S(2)}) collective-permute-start(bf16[2,64,640]{2,1,0:T(8,128)(2,1)S(1)} %collective-permute-done.9.refs_10_), channel_id=1, source_target_pairs={{0,1},{1,0},{2,3},{3,2},{4,5},{5,4},{6,7},{7,6},{8,9},{9,8},{10,11... | collective-permute-start | bytes 491528 | tf_op jit(solution)/shard_map/ppermute | solution.py:31
  21.4 0.4 %collective-permute-start.2 = (bf16[2,64,640]{2,1,0:T(8,128)(2,1)S(1)}, bf16[2,64,640]{2,1,0:T(8,128)(2,1)S(1)}, u32[]{:S(2)}, u32[]{:S(2)}) collective-permute-start(bf16[2,64,640]{2,1,0:T(8,128)(2,1)S(1)} %collective-permute-done.1.refs_2_), channel_id=1, source_target_pairs={{0,1},{1,0},{2,3},{3,2},{4,5},{5,4},{6,7},{7,6},{8,9},{9,8},{10,11... | collective-permute-start | bytes 491528 | tf_op jit(solution)/shard_map/ppermute | solution.py:31
  21.8 0.4 %collective-permute-done.7.refs_8_ = bf16[2,64,640]{2,1,0:T(8,128)(2,1)S(1)} collective-permute-done((bf16[2,64,640]{2,1,0:T(8,128)(2,1)}, bf16[2,64,640]{2,1,0:T(8,128)(2,1)S(1)}, u32[]{:S(2)}, u32[]{:S(2)}) %collective-permute-start.7) | collective-permute-done | bytes 163872 | tf_op jit(solution)/shard_map/ppermute | solution.py:31
  22.2 0.5 %collective-permute-start.4 = (bf16[2,64,640]{2,1,0:T(8,128)(2,1)S(1)}, bf16[2,64,640]{2,1,0:T(8,128)(2,1)S(1)}, u32[]{:S(2)}, u32[]{:S(2)}) collective-permute-start(bf16[2,64,640]{2,1,0:T(8,128)(2,1)S(1)} %collective-permute-done.3.refs_4_), channel_id=1, source_target_pairs={{0,1},{1,0},{2,3},{3,2},{4,5},{5,4},{6,7},{7,6},{8,9},{9,8},{10,11... | collective-permute-start | bytes 491528 | tf_op jit(solution)/shard_map/ppermute | solution.py:31
  22.9 0.7 %collective-permute-done.8.refs_9_ = bf16[2,64,640]{2,1,0:T(8,128)(2,1)S(1)} collective-permute-done((bf16[2,64,640]{2,1,0:T(8,128)(2,1)S(1)}, bf16[2,64,640]{2,1,0:T(8,128)(2,1)S(1)}, u32[]{:S(2)}, u32[]{:S(2)}) %collective-permute-start.8) | collective-permute-done | bytes 163872 | tf_op jit(solution)/shard_map/ppermute | solution.py:31
  23.8 5.6 %window_attention.1 = (bf16[64,640]{1,0:T(8,128)(2,1)S(1)}, bf16[64,640]{1,0:T(8,128)(2,1)S(1)}, bf16[64,640]{1,0:T(8,128)(2,1)S(1)}, bf16[64,640]{1,0:T(8,128)(2,1)S(1)}) custom-call(bf16[1,64,640]{2,1,0:T(8,128)(2,1)S(1)} %slice.3.refs_0_, bf16[2,64,640]{2,1,0:T(8,128)(2,1)S(1)} %collective-permute-done.refs_1_, ...), custom_call_target="tpu_custom_call" | custom-call | tf_op jit(solution)/shard_map/window_attention/pallas_call | solution.py:209
  29.4 0.3 collective-permute-start.11
  29.7 0.9 %collective-permute-start.12 = (bf16[64,640]{1,0:T(8,128)(2,1)S(1)}, bf16[64,640]{1,0:T(8,128)(2,1)S(1)}, u32[]{:S(2)}, u32[]{:S(2)}) collective-permute-start(bf16[64,640]{1,0:T(8,128)(2,1)S(1)} %get-tuple-element.26), channel_id=1, source_target_pairs={{0,2},{1,3},{2,0},{3,1},{4,6},{5,7},{6,4},{7,5},{8,10},{9,11},{10,... | collective-permute-start | bytes 245768 | tf_op jit(solution)/shard_map/ppermute | solution.py:31
  30.7 0.7 %collective-permute-start.13 = (bf16[64,640]{1,0:T(8,128)(2,1)S(1)}, bf16[64,640]{1,0:T(8,128)(2,1)S(1)}, u32[]{:S(2)}, u32[]{:S(2)}) collective-permute-start(bf16[64,640]{1,0:T(8,128)(2,1)S(1)} %get-tuple-element.27), channel_id=1, source_target_pairs={{0,3},{1,2},{2,1},{3,0},{4,7},{5,6},{6,5},{7,4},{8,11},{9,10},{10,... | collective-permute-start | bytes 245768 | tf_op jit(solution)/shard_map/ppermute | solution.py:31
  31.3 3.7 %collective-permute-done.12.refs_2_ = bf16[64,640]{1,0:T(8,128)(2,1)S(1)} collective-permute-done((bf16[64,640]{1,0:T(8,128)(2,1)S(1)}, bf16[64,640]{1,0:T(8,128)(2,1)S(1)}, u32[]{:S(2)}, u32[]{:S(2)}) %collective-permute-start.12) | collective-permute-done | bytes 81952 | tf_op jit(solution)/shard_map/ppermute | solution.py:31
  35.0 0.4 collective-permute-done.13.refs_3_
  35.4 5.2 %res_block.1 = bf16[4,2,64,320]{3,2,1,0:T(8,128)(2,1)} custom-call(bf16[64,640]{1,0:T(8,128)(2,1)S(1)} %get-tuple-element.24.refs_0_, bf16[64,640]{1,0:T(8,128)(2,1)S(1)} %collective-permute-done.11.refs_1_, bf16[64,640]{1,0:T(8,128)(2,1)S(1)} %collective-permute-done.12.refs_2_, bf16[64,640]{1,0:T(8,128)(2,1)S(1)} %collective-permute-done.13.refs_3_, ...), custom_call_target="tpu_custom_call" | custom-call | tf_op jit(solution)/shard_map/res_block/pallas_call | solution.py:318
  (24 shorter events, 1.1 us)
Async XLA Ops:
  0.0 18.3 %copy-start = (bf16[3,3,320,320]{3,2,1,0:T(8,128)(2,1)S(1)}, bf16[3,3,320,320]{3,2,1,0:T(8,128)(2,1)}, u32[]{:S(2)}) copy-start(bf16[3,3,320,320]{3,2,1,0:T(8,128)(2,1)} %param.15) | copy-start | bytes 5529604
  2.2 11.5 %collective-permute-start.3 = (bf16[2,64,640]{2,1,0:T(8,128)(2,1)}, bf16[2,64,640]{2,1,0:T(8,128)(2,1)S(1)}, u32[]{:S(2)}, u32[]{:S(2)}) collective-permute-start(bf16[2,64,640]{2,1,0:T(8,128)(2,1)} %get-tuple-element.19), channel_id=1, source_target_pairs={{0,4},{1,5},{2,6},{3,7},{4,8},{5,9},{6,10},{7,11},{8,12},{9,13},{1... | collective-permute-start | bytes 491528 | tf_op jit(solution)/shard_map/ppermute | solution.py:31
  5.2 15.5 %collective-permute-start.9 = (bf16[2,64,640]{2,1,0:T(8,128)(2,1)}, bf16[2,64,640]{2,1,0:T(8,128)(2,1)S(1)}, u32[]{:S(2)}, u32[]{:S(2)}) collective-permute-start(bf16[2,64,640]{2,1,0:T(8,128)(2,1)} %get-tuple-element.20), channel_id=1, source_target_pairs={{0,14},{1,15},{2,12},{3,13},{4,2},{5,3},{6,0},{7,1},{8,6},{9,7},{1... | collective-permute-start | bytes 491528 | tf_op jit(solution)/shard_map/ppermute | solution.py:31
  8.4 12.9 %collective-permute-start.5 = (bf16[2,64,640]{2,1,0:T(8,128)(2,1)}, bf16[2,64,640]{2,1,0:T(8,128)(2,1)S(1)}, u32[]{:S(2)}, u32[]{:S(2)}) collective-permute-start(bf16[2,64,640]{2,1,0:T(8,128)(2,1)} %get-tuple-element.20), channel_id=1, source_target_pairs={{0,6},{1,7},{2,4},{3,5},{4,10},{5,11},{6,8},{7,9},{8,14},{9,15},{1... | collective-permute-start | bytes 491528 | tf_op jit(solution)/shard_map/ppermute | solution.py:31
  8.4 12.9 %collective-permute-start.1 = (bf16[2,64,640]{2,1,0:T(8,128)(2,1)}, bf16[2,64,640]{2,1,0:T(8,128)(2,1)S(1)}, u32[]{:S(2)}, u32[]{:S(2)}) collective-permute-start(bf16[2,64,640]{2,1,0:T(8,128)(2,1)} %get-tuple-element.20), channel_id=1, source_target_pairs={{0,2},{1,3},{2,0},{3,1},{4,6},{5,7},{6,4},{7,5},{8,10},{9,11},{10,... | collective-permute-start | bytes 491528 | tf_op jit(solution)/shard_map/ppermute | solution.py:31
  9.7 12.6 %collective-permute-start.7 = (bf16[2,64,640]{2,1,0:T(8,128)(2,1)}, bf16[2,64,640]{2,1,0:T(8,128)(2,1)S(1)}, u32[]{:S(2)}, u32[]{:S(2)}) collective-permute-start(bf16[2,64,640]{2,1,0:T(8,128)(2,1)} %get-tuple-element.19), channel_id=1, source_target_pairs={{0,12},{1,13},{2,14},{3,15},{4,0},{5,1},{6,2},{7,3},{8,4},{9,5},{1... | collective-permute-start | bytes 491528 | tf_op jit(solution)/shard_map/ppermute | solution.py:31
  13.7 8.5 %collective-permute-start = (bf16[2,64,640]{2,1,0:T(8,128)(2,1)}, bf16[2,64,640]{2,1,0:T(8,128)(2,1)S(1)}, u32[]{:S(2)}, u32[]{:S(2)}) collective-permute-start(bf16[2,64,640]{2,1,0:T(8,128)(2,1)} %get-tuple-element.19), channel_id=1, source_target_pairs={{0,1},{1,0},{2,3},{3,2},{4,5},{5,4},{6,7},{7,6},{8,9},{9,8},{10,11... | collective-permute-start | bytes 491528 | tf_op jit(solution)/shard_map/ppermute | solution.py:31
  18.4 1.6 %copy-start.1 = (bf16[3,3,320,320]{3,2,1,0:T(8,128)(2,1)S(1)}, bf16[3,3,320,320]{3,2,1,0:T(8,128)(2,1)}, u32[]{:S(2)}) copy-start(bf16[3,3,320,320]{3,2,1,0:T(8,128)(2,1)} %param.16) | copy-start | bytes 5529604
  20.0 0.7 %copy-start.3 = (f32[2,320]{1,0:T(2,128)S(1)}, f32[2,320]{1,0:T(2,128)}, u32[]{:S(2)}) copy-start(f32[2,320]{1,0:T(2,128)} %param.14) | copy-start | bytes 7684
  20.0 2.8 %copy-start.2 = (bf16[2,64,640]{2,1,0:T(8,128)(2,1)S(1)}, bf16[2,64,640]{2,1,0:T(8,128)(2,1)}, u32[]{:S(2)}) copy-start(bf16[2,64,640]{2,1,0:T(8,128)(2,1)} %get-tuple-element.19) | copy-start | bytes 491524
  20.7 2.1 %collective-permute-start.10 = (bf16[2,64,640]{2,1,0:T(8,128)(2,1)S(1)}, bf16[2,64,640]{2,1,0:T(8,128)(2,1)S(1)}, u32[]{:S(2)}, u32[]{:S(2)}) collective-permute-start(bf16[2,64,640]{2,1,0:T(8,128)(2,1)S(1)} %collective-permute-done.9.refs_10_), channel_id=1, source_target_pairs={{0,1},{1,0},{2,3},{3,2},{4,5},{5,4},{6,7},{7,6},{8,9},{9,8},{10,11... | collective-permute-start | bytes 491528 | tf_op jit(solution)/shard_map/ppermute | solution.py:31
  21.3 1.5 %collective-permute-start.6 = (bf16[2,64,640]{2,1,0:T(8,128)(2,1)S(1)}, bf16[2,64,640]{2,1,0:T(8,128)(2,1)S(1)}, u32[]{:S(2)}, u32[]{:S(2)}) collective-permute-start(bf16[2,64,640]{2,1,0:T(8,128)(2,1)S(1)} %collective-permute-done.5.refs_6_), channel_id=1, source_target_pairs={{0,1},{1,0},{2,3},{3,2},{4,5},{5,4},{6,7},{7,6},{8,9},{9,8},{10,11... | collective-permute-start | bytes 491528 | tf_op jit(solution)/shard_map/ppermute | solution.py:31
  21.4 1.5 %collective-permute-start.2 = (bf16[2,64,640]{2,1,0:T(8,128)(2,1)S(1)}, bf16[2,64,640]{2,1,0:T(8,128)(2,1)S(1)}, u32[]{:S(2)}, u32[]{:S(2)}) collective-permute-start(bf16[2,64,640]{2,1,0:T(8,128)(2,1)S(1)} %collective-permute-done.1.refs_2_), channel_id=1, source_target_pairs={{0,1},{1,0},{2,3},{3,2},{4,5},{5,4},{6,7},{7,6},{8,9},{9,8},{10,11... | collective-permute-start | bytes 491528 | tf_op jit(solution)/shard_map/ppermute | solution.py:31
  22.2 1.4 %collective-permute-start.8 = (bf16[2,64,640]{2,1,0:T(8,128)(2,1)S(1)}, bf16[2,64,640]{2,1,0:T(8,128)(2,1)S(1)}, u32[]{:S(2)}, u32[]{:S(2)}) collective-permute-start(bf16[2,64,640]{2,1,0:T(8,128)(2,1)S(1)} %collective-permute-done.7.refs_8_), channel_id=1, source_target_pairs={{0,1},{1,0},{2,3},{3,2},{4,5},{5,4},{6,7},{7,6},{8,9},{9,8},{10,11... | collective-permute-start | bytes 491528 | tf_op jit(solution)/shard_map/ppermute | solution.py:31
  22.2 1.6 %collective-permute-start.4 = (bf16[2,64,640]{2,1,0:T(8,128)(2,1)S(1)}, bf16[2,64,640]{2,1,0:T(8,128)(2,1)S(1)}, u32[]{:S(2)}, u32[]{:S(2)}) collective-permute-start(bf16[2,64,640]{2,1,0:T(8,128)(2,1)S(1)} %collective-permute-done.3.refs_4_), channel_id=1, source_target_pairs={{0,1},{1,0},{2,3},{3,2},{4,5},{5,4},{6,7},{7,6},{8,9},{9,8},{10,11... | collective-permute-start | bytes 491528 | tf_op jit(solution)/shard_map/ppermute | solution.py:31
  29.4 1.9 %collective-permute-start.11 = (bf16[64,640]{1,0:T(8,128)(2,1)S(1)}, bf16[64,640]{1,0:T(8,128)(2,1)S(1)}, u32[]{:S(2)}, u32[]{:S(2)}) collective-permute-start(bf16[64,640]{1,0:T(8,128)(2,1)S(1)} %get-tuple-element.25), channel_id=1, source_target_pairs={{0,1},{1,0},{2,3},{3,2},{4,5},{5,4},{6,7},{7,6},{8,9},{9,8},{10,11... | collective-permute-start | bytes 245768 | tf_op jit(solution)/shard_map/ppermute | solution.py:31
  29.7 5.3 %collective-permute-start.12 = (bf16[64,640]{1,0:T(8,128)(2,1)S(1)}, bf16[64,640]{1,0:T(8,128)(2,1)S(1)}, u32[]{:S(2)}, u32[]{:S(2)}) collective-permute-start(bf16[64,640]{1,0:T(8,128)(2,1)S(1)} %get-tuple-element.26), channel_id=1, source_target_pairs={{0,2},{1,3},{2,0},{3,1},{4,6},{5,7},{6,4},{7,5},{8,10},{9,11},{10,... | collective-permute-start | bytes 245768 | tf_op jit(solution)/shard_map/ppermute | solution.py:31
  30.7 4.7 %collective-permute-start.13 = (bf16[64,640]{1,0:T(8,128)(2,1)S(1)}, bf16[64,640]{1,0:T(8,128)(2,1)S(1)}, u32[]{:S(2)}, u32[]{:S(2)}) collective-permute-start(bf16[64,640]{1,0:T(8,128)(2,1)S(1)} %get-tuple-element.27), channel_id=1, source_target_pairs={{0,3},{1,2},{2,1},{3,0},{4,7},{5,6},{6,5},{7,4},{8,11},{9,10},{10,... | collective-permute-start | bytes 245768 | tf_op jit(solution)/shard_map/ppermute | solution.py:31

commit v9 on v8

--- a/solution.py
+++ b/solution.py
@@ -275,7 +275,7 @@
 def res_kernel(*refs):
     part_refs, (lat_ref, w_out_ref, gn_ref, one_ref, two_ref, out_ref) = refs[:4], refs[4:10]
     comb_ref, taps_ref = refs[10:]
-    count, frames, cols, channels = lat_ref.shape
+    frames, count, cols, channels = lat_ref.shape
     deep = one_ref.shape[2]
     for i in range(3 * count):
         taps_ref[:, i * deep + channels : (i + 1) * deep] = jnp.zeros(
@@ -302,7 +302,7 @@
     for r in range(count):
         comb = combined[:, r * cols : (r + 1) * cols, :].reshape(frames * cols, channels)
         proj = jnp.dot(comb, w_out_ref[:channels], preferred_element_type=jnp.float32)
-        hid = lat_ref[r].astype(jnp.float32) + proj.reshape(frames, cols, channels)
+        hid = lat_ref[:, r].astype(jnp.float32) + proj.reshape(frames, cols, channels)
         hidden.append(hid.astype(jnp.bfloat16).astype(jnp.float32))
     acts = group_act(hidden, gn_ref[0:1], spread, members)
     middle = [row + gn_ref[2:3][None] for row in conv_rows(acts, one_ref, taps_ref)]
@@ -312,7 +312,7 @@
 
 
 def res_block(parts, extras):
-    count, frames, cols, channels = extras[0].shape
+    frames, count, cols, channels = extras[0].shape
     deep = -(-channels // LANES) * LANES
     vmem = pl.BlockSpec(memory_space=pltpu.VMEM)
     return pl.pallas_call(
@@ -359,7 +359,7 @@
     extras = [
         jnp.pad(w_qkv, (more, (0, 0))),
         jnp.concatenate([offsets, numerators]),
-        latents.transpose(1, 0, 2, 3),
+        latents,
         jnp.pad(w_out, (more, (0, 0))),
         jnp.concatenate([gn_gain, step_embed[None]]),
         jnp.pad(conv_one, ((0, 0), (0, 0), more, (0, 0))),

time: 41 us -> 41 us (level)
  local copies, waits for them, and re-layouts: 6.18 us -> 5.14 us
  waiting for transfers between devices: 5.59 us -> 6.63 us
    ppermute x14, waiting for transfers between devices: 5.59 us -> 6.63 us  [moved(): lax.ppermute(array, 'frame', [(i, target(i) % count) for i in range(count)])]
    unnamed x9 -> x10, local copies, waits for them, and re-layouts: 2.75 us -> 1.72 us
  transfers between devices with their start and end apart: 14 -> 14, of which waited for: 6 -> 6; matrix products, arithmetic and copies ran while one was open for 13% -> 10% of each run, Pallas kernels for 0% -> 0%
where the time goes in v9:
time: 41 us; the launch traced here: 40.6 us
  starting transfers between devices  15 us (37%)
  Pallas kernels  13 us (32%)
  waiting for transfers between devices  6.63 us (16%)
  local copies, waits for them, and re-layouts  5.14 us (13%)
  other arithmetic  0.76 us (2%)
    ppermute x14, starting transfers between devices, moved(): lax.ppermute(array, 'frame', [(i, target(i) % count) for i in range(count)])  15 us
    ppermute x14, waiting for transfers between devices, moved(): lax.ppermute(array, 'frame', [(i, target(i) % count) for i in range(count)])  6.63 us
    pallas_call x1, Pallas kernels, attend(): pl.pallas_call(functools.partial(attend_kernel, cells, planes), out_shape...  5.55 us
    pallas_call x1, Pallas kernels, res_block(): pl.pallas_call(res_kernel, out_shape=jax.ShapeDtypeStruct((frames, count,...  5.24 us
    pallas_call x1, Pallas kernels, body(): pl.pallas_call(pack_kernel, out_shape=[jax.ShapeDtypeStruct((2, rows, pac...  2.19 us
    unnamed x10, local copies, waits for them, and re-layouts  1.72 us
    pad x1, local copies, waits for them, and re-layouts, body(): jnp.pad(w_qkv, (more, (0, 0)))  1.18 us
    pad x1, local copies, waits for them, and re-layouts, body(): jnp.pad(w_out, (more, (0, 0)))  0.97 us
  transfers between devices with their start and end apart: 14, of which 6 were waited for; matrix products, arithmetic and copies ran while one was open for 10% of the time, Pallas kernels for 0%

profile of v9, /device:TPU:0, one launch (start us, length us, event | category | flops | bytes accessed | tf_op | source)
XLA Modules:
  0.0 40.6 jit_solution(8165135697166456389)
XLA Ops:
  0.0 2.2 %norm_pack.1 = (bf16[2,64,640]{2,1,0:T(8,128)(2,1)}, bf16[2,64,640]{2,1,0:T(8,128)(2,1)}) custom-call(bf16[4,4,32,320]{3,2,1,0:T(8,128)(2,1)} %bitcast.1, f32[320]{0:T(512)} %gain_ref.1), custom_call_target="tpu_custom_call" | custom-call | tf_op jit(solution)/shard_map/norm_pack/pallas_call | solution.py:343
  2.2 3.0 %collective-permute-start.3 = (bf16[2,64,640]{2,1,0:T(8,128)(2,1)}, bf16[2,64,640]{2,1,0:T(8,128)(2,1)S(1)}, u32[]{:S(2)}, u32[]{:S(2)}) collective-permute-start(bf16[2,64,640]{2,1,0:T(8,128)(2,1)} %get-tuple-element.19), channel_id=1, source_target_pairs={{0,4},{1,5},{2,6},{3,7},{4,8},{5,9},{6,10},{7,11},{8,12},{9,13},{1... | collective-permute-start | bytes 491528 | tf_op jit(solution)/shard_map/ppermute | solution.py:31
  5.2 3.2 %collective-permute-start.9 = (bf16[2,64,640]{2,1,0:T(8,128)(2,1)}, bf16[2,64,640]{2,1,0:T(8,128)(2,1)S(1)}, u32[]{:S(2)}, u32[]{:S(2)}) collective-permute-start(bf16[2,64,640]{2,1,0:T(8,128)(2,1)} %get-tuple-element.20), channel_id=1, source_target_pairs={{0,14},{1,15},{2,12},{3,13},{4,2},{5,3},{6,0},{7,1},{8,6},{9,7},{1... | collective-permute-start | bytes 491528 | tf_op jit(solution)/shard_map/ppermute | solution.py:31
  8.4 1.2 %collective-permute-start.1 = (bf16[2,64,640]{2,1,0:T(8,128)(2,1)}, bf16[2,64,640]{2,1,0:T(8,128)(2,1)S(1)}, u32[]{:S(2)}, u32[]{:S(2)}) collective-permute-start(bf16[2,64,640]{2,1,0:T(8,128)(2,1)} %get-tuple-element.20), channel_id=1, source_target_pairs={{0,2},{1,3},{2,0},{3,1},{4,6},{5,7},{6,4},{7,5},{8,10},{9,11},{10,... | collective-permute-start | bytes 491528 | tf_op jit(solution)/shard_map/ppermute | solution.py:31
  9.7 4.0 %collective-permute-start.7 = (bf16[2,64,640]{2,1,0:T(8,128)(2,1)}, bf16[2,64,640]{2,1,0:T(8,128)(2,1)S(1)}, u32[]{:S(2)}, u32[]{:S(2)}) collective-permute-start(bf16[2,64,640]{2,1,0:T(8,128)(2,1)} %get-tuple-element.19), channel_id=1, source_target_pairs={{0,12},{1,13},{2,14},{3,15},{4,0},{5,1},{6,2},{7,3},{8,4},{9,5},{1... | collective-permute-start | bytes 491528 | tf_op jit(solution)/shard_map/ppermute | solution.py:31
  13.7 0.7 %pad_add_fusion.refs_12_ = s32[32]{0:T(128)S(1)} fusion(s32[16]{0:T(128)} %param.19, s32[16]{0:T(128)} %param.18), kind=kLoop, calls=%fused_computation.1 | loop fusion | flops 32 | bytes 256 | tf_op jit(solution)/shard_map/concatenate | solution.py:361
  14.5 0.7 %broadcast_in_dim.3 = f32[1,320]{1,0:T(1,128)S(1)} reshape(f32[320]{0:T(512)} %param.17) | data formatting | bytes 2560 | tf_op jit(solution)/shard_map/broadcast_in_dim | solution.py:364
  15.1 1.0 %pad.16.refs_5_ = bf16[384,320]{1,0:T(8,128)(2,1)S(1)} pad(bf16[320,320]{1,0:T(8,128)(2,1)} %param.13, bf16[]{:T(256)} %constant.2.clone.1), padding=0_64x0_0 | pad | bytes 450562 | tf_op jit(solution)/shard_map/jit(_pad)/pad | solution.py:363
  16.1 1.2 %pad.15.refs_13_ = bf16[384,960]{1,0:T(8,128)(2,1)S(1)} pad(bf16[320,960]{1,0:T(8,128)(2,1)} %param.12, bf16[]{:T(256)} %constant.2.clone.1), padding=0_64x0_0 | pad | bytes 1351682 | tf_op jit(solution)/shard_map/jit(_pad)/pad | solution.py:360
  17.6 1.3 %copy-done.2 = bf16[3,3,320,320]{3,2,1,0:T(8,128)(2,1)S(1)} copy-done((bf16[3,3,320,320]{3,2,1,0:T(8,128)(2,1)S(1)}, bf16[3,3,320,320]{3,2,1,0:T(8,128)(2,1)}, u32[]{:S(2)}) %copy-start.2) | copy-done | bytes 1843224
  19.2 0.4 copy-done.4
  19.7 0.6 %collective-permute-start.10 = (bf16[2,64,640]{2,1,0:T(8,128)(2,1)S(1)}, bf16[2,64,640]{2,1,0:T(8,128)(2,1)S(1)}, u32[]{:S(2)}, u32[]{:S(2)}) collective-permute-start(bf16[2,64,640]{2,1,0:T(8,128)(2,1)S(1)} %collective-permute-done.9.refs_10_), channel_id=1, source_target_pairs={{0,1},{1,0},{2,3},{3,2},{4,5},{5,4},{6,7},{7,6},{8,9},{9,8},{10,11... | collective-permute-start | bytes 491528 | tf_op jit(solution)/shard_map/ppermute | solution.py:31
  20.2 0.6 %collective-permute-done.5.refs_6_ = bf16[2,64,640]{2,1,0:T(8,128)(2,1)S(1)} collective-permute-done((bf16[2,64,640]{2,1,0:T(8,128)(2,1)}, bf16[2,64,640]{2,1,0:T(8,128)(2,1)S(1)}, u32[]{:S(2)}, u32[]{:S(2)}) %collective-permute-start.5) | collective-permute-done | bytes 163872 | tf_op jit(solution)/shard_map/ppermute | solution.py:31
  20.8 0.5 %collective-permute-start.2 = (bf16[2,64,640]{2,1,0:T(8,128)(2,1)S(1)}, bf16[2,64,640]{2,1,0:T(8,128)(2,1)S(1)}, u32[]{:S(2)}, u32[]{:S(2)}) collective-permute-start(bf16[2,64,640]{2,1,0:T(8,128)(2,1)S(1)} %collective-permute-done.1.refs_2_), channel_id=1, source_target_pairs={{0,1},{1,0},{2,3},{3,2},{4,5},{5,4},{6,7},{7,6},{8,9},{9,8},{10,11... | collective-permute-start | bytes 491528 | tf_op jit(solution)/shard_map/ppermute | solution.py:31
  21.3 0.9 %collective-permute-done.7.refs_8_ = bf16[2,64,640]{2,1,0:T(8,128)(2,1)S(1)} collective-permute-done((bf16[2,64,640]{2,1,0:T(8,128)(2,1)}, bf16[2,64,640]{2,1,0:T(8,128)(2,1)S(1)}, u32[]{:S(2)}, u32[]{:S(2)}) %collective-permute-start.7) | collective-permute-done | bytes 163872 | tf_op jit(solution)/shard_map/ppermute | solution.py:31
  22.2 0.5 %collective-permute-start.4 = (bf16[2,64,640]{2,1,0:T(8,128)(2,1)S(1)}, bf16[2,64,640]{2,1,0:T(8,128)(2,1)S(1)}, u32[]{:S(2)}, u32[]{:S(2)}) collective-permute-start(bf16[2,64,640]{2,1,0:T(8,128)(2,1)S(1)} %collective-permute-done.3.refs_4_), channel_id=1, source_target_pairs={{0,1},{1,0},{2,3},{3,2},{4,5},{5,4},{6,7},{7,6},{8,9},{9,8},{10,11... | collective-permute-start | bytes 491528 | tf_op jit(solution)/shard_map/ppermute | solution.py:31
  22.8 0.8 %collective-permute-done.8.refs_9_ = bf16[2,64,640]{2,1,0:T(8,128)(2,1)S(1)} collective-permute-done((bf16[2,64,640]{2,1,0:T(8,128)(2,1)S(1)}, bf16[2,64,640]{2,1,0:T(8,128)(2,1)S(1)}, u32[]{:S(2)}, u32[]{:S(2)}) %collective-permute-start.8) | collective-permute-done | bytes 163872 | tf_op jit(solution)/shard_map/ppermute | solution.py:31
  23.9 5.6 %window_attention.1 = (bf16[64,640]{1,0:T(8,128)(2,1)S(1)}, bf16[64,640]{1,0:T(8,128)(2,1)S(1)}, bf16[64,640]{1,0:T(8,128)(2,1)S(1)}, bf16[64,640]{1,0:T(8,128)(2,1)S(1)}) custom-call(bf16[1,64,640]{2,1,0:T(8,128)(2,1)S(1)} %slice.3.refs_0_, bf16[2,64,640]{2,1,0:T(8,128)(2,1)S(1)} %collective-permute-done.refs_1_, ...), custom_call_target="tpu_custom_call" | custom-call | tf_op jit(solution)/shard_map/window_attention/pallas_call | solution.py:209
  29.4 0.3 collective-permute-start.11
  29.8 0.9 %collective-permute-start.12 = (bf16[64,640]{1,0:T(8,128)(2,1)S(1)}, bf16[64,640]{1,0:T(8,128)(2,1)S(1)}, u32[]{:S(2)}, u32[]{:S(2)}) collective-permute-start(bf16[64,640]{1,0:T(8,128)(2,1)S(1)} %get-tuple-element.26), channel_id=1, source_target_pairs={{0,2},{1,3},{2,0},{3,1},{4,6},{5,7},{6,4},{7,5},{8,10},{9,11},{10,... | collective-permute-start | bytes 245768 | tf_op jit(solution)/shard_map/ppermute | solution.py:31
  30.7 0.7 %collective-permute-start.13 = (bf16[64,640]{1,0:T(8,128)(2,1)S(1)}, bf16[64,640]{1,0:T(8,128)(2,1)S(1)}, u32[]{:S(2)}, u32[]{:S(2)}) collective-permute-start(bf16[64,640]{1,0:T(8,128)(2,1)S(1)} %get-tuple-element.27), channel_id=1, source_target_pairs={{0,3},{1,2},{2,1},{3,0},{4,7},{5,6},{6,5},{7,4},{8,11},{9,10},{10,... | collective-permute-start | bytes 245768 | tf_op jit(solution)/shard_map/ppermute | solution.py:31
  31.3 3.7 %collective-permute-done.12.refs_2_ = bf16[64,640]{1,0:T(8,128)(2,1)S(1)} collective-permute-done((bf16[64,640]{1,0:T(8,128)(2,1)S(1)}, bf16[64,640]{1,0:T(8,128)(2,1)S(1)}, u32[]{:S(2)}, u32[]{:S(2)}) %collective-permute-start.12) | collective-permute-done | bytes 81952 | tf_op jit(solution)/shard_map/ppermute | solution.py:31
  35.0 0.4 collective-permute-done.13.refs_3_
  35.4 5.2 %res_block.1 = bf16[4,2,64,320]{3,2,1,0:T(8,128)(2,1)} custom-call(bf16[64,640]{1,0:T(8,128)(2,1)S(1)} %get-tuple-element.24.refs_0_, bf16[64,640]{1,0:T(8,128)(2,1)S(1)} %collective-permute-done.11.refs_1_, bf16[64,640]{1,0:T(8,128)(2,1)S(1)} %collective-permute-done.12.refs_2_, bf16[64,640]{1,0:T(8,128)(2,1)S(1)} %collective-permute-done.13.refs_3_, ...), custom_call_target="tpu_custom_call" | custom-call | tf_op jit(solution)/shard_map/res_block/pallas_call | solution.py:318
  (25 shorter events, 0.9 us)
Async XLA Ops:
  0.0 17.3 %copy-start.1 = (bf16[3,3,320,320]{3,2,1,0:T(8,128)(2,1)S(1)}, bf16[3,3,320,320]{3,2,1,0:T(8,128)(2,1)}, u32[]{:S(2)}) copy-start(bf16[3,3,320,320]{3,2,1,0:T(8,128)(2,1)} %param.15) | copy-start | bytes 5529604
  2.2 11.5 %collective-permute-start.3 = (bf16[2,64,640]{2,1,0:T(8,128)(2,1)}, bf16[2,64,640]{2,1,0:T(8,128)(2,1)S(1)}, u32[]{:S(2)}, u32[]{:S(2)}) collective-permute-start(bf16[2,64,640]{2,1,0:T(8,128)(2,1)} %get-tuple-element.19), channel_id=1, source_target_pairs={{0,4},{1,5},{2,6},{3,7},{4,8},{5,9},{6,10},{7,11},{8,12},{9,13},{1... | collective-permute-start | bytes 491528 | tf_op jit(solution)/shard_map/ppermute | solution.py:31
  5.2 14.4 %collective-permute-start.9 = (bf16[2,64,640]{2,1,0:T(8,128)(2,1)}, bf16[2,64,640]{2,1,0:T(8,128)(2,1)S(1)}, u32[]{:S(2)}, u32[]{:S(2)}) collective-permute-start(bf16[2,64,640]{2,1,0:T(8,128)(2,1)} %get-tuple-element.20), channel_id=1, source_target_pairs={{0,14},{1,15},{2,12},{3,13},{4,2},{5,3},{6,0},{7,1},{8,6},{9,7},{1... | collective-permute-start | bytes 491528 | tf_op jit(solution)/shard_map/ppermute | solution.py:31
  8.4 12.4 %collective-permute-start.5 = (bf16[2,64,640]{2,1,0:T(8,128)(2,1)}, bf16[2,64,640]{2,1,0:T(8,128)(2,1)S(1)}, u32[]{:S(2)}, u32[]{:S(2)}) collective-permute-start(bf16[2,64,640]{2,1,0:T(8,128)(2,1)} %get-tuple-element.20), channel_id=1, source_target_pairs={{0,6},{1,7},{2,4},{3,5},{4,10},{5,11},{6,8},{7,9},{8,14},{9,15},{1... | collective-permute-start | bytes 491528 | tf_op jit(solution)/shard_map/ppermute | solution.py:31
  8.4 12.4 %collective-permute-start.1 = (bf16[2,64,640]{2,1,0:T(8,128)(2,1)}, bf16[2,64,640]{2,1,0:T(8,128)(2,1)S(1)}, u32[]{:S(2)}, u32[]{:S(2)}) collective-permute-start(bf16[2,64,640]{2,1,0:T(8,128)(2,1)} %get-tuple-element.20), channel_id=1, source_target_pairs={{0,2},{1,3},{2,0},{3,1},{4,6},{5,7},{6,4},{7,5},{8,10},{9,11},{10,... | collective-permute-start | bytes 491528 | tf_op jit(solution)/shard_map/ppermute | solution.py:31
  9.7 12.6 %collective-permute-start.7 = (bf16[2,64,640]{2,1,0:T(8,128)(2,1)}, bf16[2,64,640]{2,1,0:T(8,128)(2,1)S(1)}, u32[]{:S(2)}, u32[]{:S(2)}) collective-permute-start(bf16[2,64,640]{2,1,0:T(8,128)(2,1)} %get-tuple-element.19), channel_id=1, source_target_pairs={{0,12},{1,13},{2,14},{3,15},{4,0},{5,1},{6,2},{7,3},{8,4},{9,5},{1... | collective-permute-start | bytes 491528 | tf_op jit(solution)/shard_map/ppermute | solution.py:31
  13.7 8.5 %collective-permute-start = (bf16[2,64,640]{2,1,0:T(8,128)(2,1)}, bf16[2,64,640]{2,1,0:T(8,128)(2,1)S(1)}, u32[]{:S(2)}, u32[]{:S(2)}) collective-permute-start(bf16[2,64,640]{2,1,0:T(8,128)(2,1)} %get-tuple-element.19), channel_id=1, source_target_pairs={{0,1},{1,0},{2,3},{3,2},{4,5},{5,4},{6,7},{7,6},{8,9},{9,8},{10,11... | collective-permute-start | bytes 491528 | tf_op jit(solution)/shard_map/ppermute | solution.py:31
  17.3 1.6 %copy-start.2 = (bf16[3,3,320,320]{3,2,1,0:T(8,128)(2,1)S(1)}, bf16[3,3,320,320]{3,2,1,0:T(8,128)(2,1)}, u32[]{:S(2)}) copy-start(bf16[3,3,320,320]{3,2,1,0:T(8,128)(2,1)} %param.16) | copy-start | bytes 5529604
  18.9 0.7 %copy-start.4 = (f32[2,320]{1,0:T(2,128)S(1)}, f32[2,320]{1,0:T(2,128)}, u32[]{:S(2)}) copy-start(f32[2,320]{1,0:T(2,128)} %param.14) | copy-start | bytes 7684
  18.9 3.8 %copy-start.3 = (bf16[2,64,640]{2,1,0:T(8,128)(2,1)S(1)}, bf16[2,64,640]{2,1,0:T(8,128)(2,1)}, u32[]{:S(2)}) copy-start(bf16[2,64,640]{2,1,0:T(8,128)(2,1)} %get-tuple-element.19) | copy-start | bytes 491524
  19.0 16.5 %copy-start = (bf16[4,2,64,320]{3,2,1,0:T(8,128)(2,1)S(1)}, bf16[4,2,64,320]{3,2,1,0:T(8,128)(2,1)}, u32[]{:S(2)}) copy-start(bf16[4,2,64,320]{3,2,1,0:T(8,128)(2,1)} %refs_4_) | copy-start | bytes 983044
  19.7 3.1 %collective-permute-start.10 = (bf16[2,64,640]{2,1,0:T(8,128)(2,1)S(1)}, bf16[2,64,640]{2,1,0:T(8,128)(2,1)S(1)}, u32[]{:S(2)}, u32[]{:S(2)}) collective-permute-start(bf16[2,64,640]{2,1,0:T(8,128)(2,1)S(1)} %collective-permute-done.9.refs_10_), channel_id=1, source_target_pairs={{0,1},{1,0},{2,3},{3,2},{4,5},{5,4},{6,7},{7,6},{8,9},{9,8},{10,11... | collective-permute-start | bytes 491528 | tf_op jit(solution)/shard_map/ppermute | solution.py:31
  20.8 1.9 %collective-permute-start.6 = (bf16[2,64,640]{2,1,0:T(8,128)(2,1)S(1)}, bf16[2,64,640]{2,1,0:T(8,128)(2,1)S(1)}, u32[]{:S(2)}, u32[]{:S(2)}) collective-permute-start(bf16[2,64,640]{2,1,0:T(8,128)(2,1)S(1)} %collective-permute-done.5.refs_6_), channel_id=1, source_target_pairs={{0,1},{1,0},{2,3},{3,2},{4,5},{5,4},{6,7},{7,6},{8,9},{9,8},{10,11... | collective-permute-start | bytes 491528 | tf_op jit(solution)/shard_map/ppermute | solution.py:31
  20.8 2.0 %collective-permute-start.2 = (bf16[2,64,640]{2,1,0:T(8,128)(2,1)S(1)}, bf16[2,64,640]{2,1,0:T(8,128)(2,1)S(1)}, u32[]{:S(2)}, u32[]{:S(2)}) collective-permute-start(bf16[2,64,640]{2,1,0:T(8,128)(2,1)S(1)} %collective-permute-done.1.refs_2_), channel_id=1, source_target_pairs={{0,1},{1,0},{2,3},{3,2},{4,5},{5,4},{6,7},{7,6},{8,9},{9,8},{10,11... | collective-permute-start | bytes 491528 | tf_op jit(solution)/shard_map/ppermute | solution.py:31
  22.2 1.4 %collective-permute-start.8 = (bf16[2,64,640]{2,1,0:T(8,128)(2,1)S(1)}, bf16[2,64,640]{2,1,0:T(8,128)(2,1)S(1)}, u32[]{:S(2)}, u32[]{:S(2)}) collective-permute-start(bf16[2,64,640]{2,1,0:T(8,128)(2,1)S(1)} %collective-permute-done.7.refs_8_), channel_id=1, source_target_pairs={{0,1},{1,0},{2,3},{3,2},{4,5},{5,4},{6,7},{7,6},{8,9},{9,8},{10,11... | collective-permute-start | bytes 491528 | tf_op jit(solution)/shard_map/ppermute | solution.py:31
  22.2 1.6 %collective-permute-start.4 = (bf16[2,64,640]{2,1,0:T(8,128)(2,1)S(1)}, bf16[2,64,640]{2,1,0:T(8,128)(2,1)S(1)}, u32[]{:S(2)}, u32[]{:S(2)}) collective-permute-start(bf16[2,64,640]{2,1,0:T(8,128)(2,1)S(1)} %collective-permute-done.3.refs_4_), channel_id=1, source_target_pairs={{0,1},{1,0},{2,3},{3,2},{4,5},{5,4},{6,7},{7,6},{8,9},{9,8},{10,11... | collective-permute-start | bytes 491528 | tf_op jit(solution)/shard_map/ppermute | solution.py:31
  29.4 1.9 %collective-permute-start.11 = (bf16[64,640]{1,0:T(8,128)(2,1)S(1)}, bf16[64,640]{1,0:T(8,128)(2,1)S(1)}, u32[]{:S(2)}, u32[]{:S(2)}) collective-permute-start(bf16[64,640]{1,0:T(8,128)(2,1)S(1)} %get-tuple-element.25), channel_id=1, source_target_pairs={{0,1},{1,0},{2,3},{3,2},{4,5},{5,4},{6,7},{7,6},{8,9},{9,8},{10,11... | collective-permute-start | bytes 245768 | tf_op jit(solution)/shard_map/ppermute | solution.py:31
  29.8 5.3 %collective-permute-start.12 = (bf16[64,640]{1,0:T(8,128)(2,1)S(1)}, bf16[64,640]{1,0:T(8,128)(2,1)S(1)}, u32[]{:S(2)}, u32[]{:S(2)}) collective-permute-start(bf16[64,640]{1,0:T(8,128)(2,1)S(1)} %get-tuple-element.26), channel_id=1, source_target_pairs={{0,2},{1,3},{2,0},{3,1},{4,6},{5,7},{6,4},{7,5},{8,10},{9,11},{10,... | collective-permute-start | bytes 245768 | tf_op jit(solution)/shard_map/ppermute | solution.py:31
  30.7 4.7 %collective-permute-start.13 = (bf16[64,640]{1,0:T(8,128)(2,1)S(1)}, bf16[64,640]{1,0:T(8,128)(2,1)S(1)}, u32[]{:S(2)}, u32[]{:S(2)}) collective-permute-start(bf16[64,640]{1,0:T(8,128)(2,1)S(1)} %get-tuple-element.27), channel_id=1, source_target_pairs={{0,3},{1,2},{2,1},{3,0},{4,7},{5,6},{6,5},{7,4},{8,11},{9,10},{10,... | collective-permute-start | bytes 245768 | tf_op jit(solution)/shard_map/ppermute | solution.py:31
